TPU v7x, 32 devices: a whole 2x2x4 slice. The times are simulated.
32 devices in a mesh: pulse: 8 (over z, y), rng: 4 (over x, core).
Axes of the slice: x: 2, y: 2, z: 4, core: 2. Of those that a mesh axis runs over, the one named last changes fastest.
Arguments:
- echoes: bfloat16 [2, 1024, 8192], P(None, 'pulse', 'rng'), may hold values from -6 to 6
- range_ref: bfloat16 [2, 1024], replicated, may hold values from -0.125 to 0.125
- band_weights: bfloat16 [64, 8192], P(None, 'rng'), may hold values from -0.75 to 0.75
- band_offsets: int32 [8192], P('rng'), may hold values from 0 to 32, as said below
- azimuth_ref: bfloat16 [2, 512], replicated, may hold values from -0.1875 to 0.1875
Outputs:
- image: float32 [2, 4, 2048, 1024], P(None, 'rng', 'pulse')
Inputs may be any that keep to these rules, and one draw needn't show every extreme that they name: `band_offsets`: every value from 0 to one half of 64 may occur; both ends occur in every draw.
All inputs are finite; a program needn't handle non-finite values.
Results may differ from a plain program's by a relative error of at most 0.0041.
Values may be sent and summed in bfloat16 or wider, within the bound.
No kernel may reach another device: no remote copies, remote signals or barrier semaphores. Data moves between devices by JAX's collectives and lax.ppermute only.
A program may use at most 64 MiB of HBM per device.

v0:
```python
import jax
import jax.numpy as jnp
from jax import lax
from jax.sharding import PartitionSpec as P

RT = 1024
AT = 512
BAND = 64
BLK = 128


def from_behind(value, axis, steps):
    count = lax.axis_size(axis)
    first, last = (max(0, -steps), min(count, count - steps))
    return lax.ppermute(value, axis, [(source, source + steps) for source in range(first, last)])


def with_halo(block, sides, width):
    for axis, dim in sides:
        count = lax.axis_size(axis)
        forward = [(i, i + 1) for i in range(count - 1)]
        backward = [(target, source) for source, target in forward]
        low = lax.ppermute(
            lax.slice_in_dim(block, block.shape[dim] - width, None, axis=dim), axis, forward
        )
        high = lax.ppermute(lax.slice_in_dim(block, 0, width, axis=dim), axis, backward)
        block = jnp.concatenate([low, block, high], axis=dim)
    return block


def skew_rows(matrix_rows):
    leading = matrix_rows.shape[:-2]
    row_count = matrix_rows.shape[-2]
    row_length = matrix_rows.shape[-1]
    widths = [(0, 0)] * len(leading) + [(0, 0), (0, row_count)]
    padded = jnp.pad(matrix_rows, widths)
    flattened = padded.reshape(leading + (row_count * (row_length + row_count),))
    kept = flattened[..., : row_count * (row_length + row_count - 1)]
    return kept.reshape(leading + (row_count, row_length + row_count - 1))


def toeplitz_real(filter_taps, block_count):
    tap_total = filter_taps.shape[1]
    span_total = block_count * BLK
    row_length = span_total - BLK + 1
    padded_taps = jnp.pad(filter_taps, ((0, 0), (0, row_length - tap_total)))
    repeated = jnp.broadcast_to(padded_taps[:, None, :], (2, BLK, row_length))
    skewed = skew_rows(repeated)
    skewed_parts = skewed.reshape(2, BLK, block_count, BLK).transpose(0, 2, 3, 1)
    real_part = skewed_parts[0]
    imag_part = skewed_parts[1]
    upper = jnp.stack([real_part, -imag_part], axis=2)
    lower = jnp.stack([imag_part, real_part], axis=2)
    return jnp.stack([upper, lower], axis=1)


def correlate(blocks, kernel, out_blocks):
    running = None
    for tap_block in range(kernel.shape[0]):
        window = blocks[:, :, tap_block : tap_block + out_blocks]
        partial_sum = jnp.einsum(
            "zrbi,ziwc->wrbc", window, kernel[tap_block], preferred_element_type=jnp.float32
        )
        running = partial_sum if running is None else running + partial_sum
    return running


def band_matrices(weights_t, offsets, block_total):
    table = weights_t.reshape(BAND, block_total, BLK).transpose(1, 0, 2)
    reach_rows = BAND + BAND // 2
    placed = jnp.pad(table, ((0, 0), (0, BAND // 2), (0, 0)))
    shifts = offsets.reshape(block_total, 1, BLK)
    for bit_number in range((BAND // 2).bit_length()):
        step_size = 1 << bit_number
        shifted = jnp.pad(placed[:, : reach_rows - step_size], ((0, 0), (step_size, 0), (0, 0)))
        placed = jnp.where(shifts // step_size % 2 == 1, shifted, placed)
    columns = jnp.pad(
        placed.transpose(0, 2, 1), ((0, 0), (0, 0), (BAND // 2, BLK + 1 - BAND // 2 - reach_rows))
    )
    skewed = skew_rows(columns)
    return skewed.transpose(0, 2, 1)


def migrate_padded(padded, weights_t, offsets):
    block_total = offsets.shape[0] // BLK
    matrices = band_matrices(weights_t, offsets, block_total)
    pulse_total = padded.shape[1]
    tiles = padded.reshape(2, pulse_total, block_total + 1, BLK)
    lower = jnp.einsum(
        "zrbi,bic->zbcr", tiles[:, :, :-1], matrices[:, :BLK], preferred_element_type=jnp.float32
    )
    upper = jnp.einsum(
        "zrbi,bic->zbcr", tiles[:, :, 1:], matrices[:, BLK:], preferred_element_type=jnp.float32
    )
    return (lower + upper).reshape(2, block_total * BLK, pulse_total).astype(jnp.bfloat16)


def azimuth_focus(migrated, kernel):
    bin_total = migrated.shape[1]
    pulse_total = migrated.shape[2]
    padded = jnp.pad(migrated, ((0, 0), (0, 0), (AT // 2, AT // 2)))
    blocks = padded.reshape(2, bin_total, (pulse_total + AT) // BLK, BLK)
    return correlate(blocks, kernel, pulse_total // BLK).reshape(2, bin_total, pulse_total)


def per_device(echoes, range_ref, band_weights, band_offsets, azimuth_ref):
    pulse_rows = echoes.shape[1]
    quarter_len = echoes.shape[2]
    block_total = quarter_len // BLK
    range_kernel = toeplitz_real(range_ref, RT // BLK + 1)
    following = from_behind(echoes[:, :, :RT], "rng", -1)
    joined = jnp.concatenate([echoes, following], axis=2)
    blocks = joined.reshape(2, pulse_rows, block_total + RT // BLK, BLK)
    compressed = (
        correlate(blocks, range_kernel, block_total)
        .reshape(2, pulse_rows, quarter_len)
        .astype(jnp.bfloat16)
    )
    padded = with_halo(compressed, (("rng", 2),), BAND)
    migrated = migrate_padded(padded, band_weights, band_offsets)
    pulse_peers = lax.axis_size("pulse")
    grouped = migrated.reshape(2, pulse_peers, quarter_len // pulse_peers, pulse_rows)
    azimuth_kernel = toeplitz_real(azimuth_ref, AT // BLK + 1)
    return azimuth_focus(
        lax.all_to_all(grouped, "pulse", split_axis=1, concat_axis=3, tiled=True)[:, 0],
        azimuth_kernel,
    )[:, None]


def solution(mesh):
    return jax.shard_map(
        per_device,
        mesh=mesh,
        in_specs=(P(None, "pulse", "rng"), P(), P(None, "rng"), P("rng"), P()),
        out_specs=P(None, "rng", "pulse", None),
        check_vma=False,
    )
```

profile of v0, /device:TPU:1, one launch (start us, length us, event | category | flops | bytes accessed | tf_op | source)
XLA Modules:
  0.0 139.3 jit_solution(7214780590196264062)
XLA Ops:
  0.0 1.6 %copy.42 = bf16[2,128,2048]{1,2,0:T(8,128)(2,1)S(1)} copy(bf16[2,128,2048]{2,1,0:T(8,128)(2,1)} %param.5) | data formatting | bytes 2097152 | tf_op args[0]
  1.6 0.8 slice.209
  2.5 2.0 %collective-permute-start = (bf16[2,128,1024]{1,2,0:T(8,128)(2,1)}, bf16[2,128,1024]{1,2,0:T(8,128)(2,1)}, u32[]{:S(2)}, u32[]{:S(2)}) collective-permute-start(bf16[2,128,1024]{1,2,0:T(8,128)(2,1)} %slice.209), channel_id=1, source_target_pairs={{1,0},{2,1},{3,2},{5,4},{6,5},{7,6},{9,8},{10,9},{11,10},{13,12},{... | collective-permute-start | bytes 1572872 | tf_op jit(solution)/shard_map/ppermute | solution.py:15
  4.6 1.7 %reshape.457 = bf16[2,147584]{1,0:T(2,128)(2,1)S(1)} reshape(bf16[2,128,1153]{2,1,0:T(8,128)(2,1)S(1)} %pad.68) | data formatting | bytes 1180672 | tf_op jit(solution)/shard_map/reshape | solution.py:37
  7.5 0.7 copy-done.5
  8.6 0.6 pad_select_fusion.4
  10.8 1.3 pad_select_fusion
  12.1 2.1 %collective-permute-done = bf16[2,128,1024]{1,2,0:T(8,128)(2,1)} collective-permute-done((bf16[2,128,1024]{1,2,0:T(8,128)(2,1)}, bf16[2,128,1024]{1,2,0:T(8,128)(2,1)}, u32[]{:S(2)}, u32[]{:S(2)}) %collective-permute-start) | collective-permute-done | bytes 524320 | tf_op jit(solution)/shard_map/ppermute | solution.py:15
  14.1 1.1 pad_maximum_fusion
  15.3 3.1 %fusion.111 = (bf16[2,128,16,128]{1,3,2,0:T(8,128)(2,1)}, bf16[2,128,16,128]{1,3,2,0:T(8,128)(2,1)S(1)}, bf16[2,128,16,128]{1,3,2,0:T(8,128)(2,1)S(1)}, bf16[2,1...) fusion(bf16[2,128,24,128]{1,3,2,0:T(8,128)(2,1)S(1)} %bitcast.301), kind=kLoop, calls=%fused_computation.191 | loop fusion | bytes 18874368 | tf_op jit(solution)/shard_map/slice | solution.py:60
  18.4 1.3 copy.101
  19.7 1.3 copy.100
  21.0 1.8 %fusion.15 = f32[2,128,128,16,1]{2,1,4,3,0:T(8,128)S(1)} fusion(bf16[2,128,16,128]{3,1,0,2:T(8,128)(2,1)} %copy.101, bf16[9,1,128,2,128]{2,4,1,3,0:T(8,128)(2,1)S(1)} %get-tuple-element.28, bf16[9,1,128,2,128]{2,4,1,3,0:T(8,128)(2,1)S(1)} %get-tuple-element.27), kind=kOutput, calls=%fused_computation.46 | convolution fusion | flops 268697600 | bytes 4325376 | tf_op jit(solution)/shard_map/zrbi,ziwc->wrbc/dot_general | solution.py:61
  22.8 1.8 %fusion.17 = f32[2,128,128,16,1]{2,1,4,3,0:T(8,128)} fusion(bf16[2,128,16,128]{3,1,0,2:T(8,128)(2,1)S(1)} %copy-done.3, bf16[9,1,128,2,128]{2,4,1,3,0:T(8,128)(2,1)S(1)} %get-tuple-element.28, bf16[9,1,128,2,128]{2,4,1,3,0:T(8,128)(2,1)S(1)} %get-tuple-element.27), kind=kOutput, calls=%fused_computation.48 | convolution fusion | flops 268697600 | bytes 4325376 | tf_op jit(solution)/shard_map/zrbi,ziwc->wrbc/dot_general | solution.py:61
  24.6 2.3 %copy.99 = bf16[2,128,16,128]{3,1,0,2:T(8,128)(2,1)} copy(bf16[2,128,16,128]{1,3,2,0:T(8,128)(2,1)} %get-tuple-element.13) | data formatting | bytes 2097152
  26.9 3.0 %fusion.19 = f32[2,128,128,16,1]{2,1,4,3,0:T(8,128)} fusion(bf16[2,128,16,128]{3,1,0,2:T(8,128)(2,1)} %copy.99, bf16[9,1,128,2,128]{2,4,1,3,0:T(8,128)(2,1)S(1)} %get-tuple-element.28, bf16[9,1,128,2,128]{2,4,1,3,0:T(8,128)(2,1)S(1)} %get-tuple-element.27), kind=kOutput, calls=%fused_computation.50 | convolution fusion | flops 268697600 | bytes 4325376 | tf_op jit(solution)/shard_map/zrbi,ziwc->wrbc/dot_general | solution.py:61
  29.9 2.3 %copy.98 = bf16[2,128,16,128]{3,1,0,2:T(8,128)(2,1)} copy(bf16[2,128,16,128]{1,3,2,0:T(8,128)(2,1)} %get-tuple-element.14) | data formatting | bytes 2097152
  32.2 3.0 %fusion.21 = f32[2,128,128,16,1]{2,1,4,3,0:T(8,128)} fusion(bf16[2,128,16,128]{3,1,0,2:T(8,128)(2,1)} %copy.98, bf16[9,1,128,2,128]{2,4,1,3,0:T(8,128)(2,1)S(1)} %get-tuple-element.28, bf16[9,1,128,2,128]{2,4,1,3,0:T(8,128)(2,1)S(1)} %get-tuple-element.27), kind=kOutput, calls=%fused_computation.52 | convolution fusion | flops 268697600 | bytes 4325376 | tf_op jit(solution)/shard_map/zrbi,ziwc->wrbc/dot_general | solution.py:61
  35.2 2.3 %copy.97 = bf16[2,128,16,128]{3,1,0,2:T(8,128)(2,1)} copy(bf16[2,128,16,128]{1,3,2,0:T(8,128)(2,1)} %get-tuple-element.15) | data formatting | bytes 2097152
  37.5 3.0 %fusion.23 = f32[2,128,128,16,1]{2,1,4,3,0:T(8,128)} fusion(bf16[2,128,16,128]{3,1,0,2:T(8,128)(2,1)} %copy.97, bf16[9,1,128,2,128]{2,4,1,3,0:T(8,128)(2,1)S(1)} %get-tuple-element.28, bf16[9,1,128,2,128]{2,4,1,3,0:T(8,128)(2,1)S(1)} %get-tuple-element.27), kind=kOutput, calls=%fused_computation.54 | convolution fusion | flops 268697600 | bytes 4325376 | tf_op jit(solution)/shard_map/zrbi,ziwc->wrbc/dot_general | solution.py:61
  40.6 2.3 %copy.96 = bf16[2,128,16,128]{3,1,0,2:T(8,128)(2,1)} copy(bf16[2,128,16,128]{1,3,2,0:T(8,128)(2,1)} %get-tuple-element.16) | data formatting | bytes 2097152
  42.9 3.1 %fusion.25 = f32[2,128,128,16,1]{2,1,4,3,0:T(8,128)} fusion(bf16[2,128,16,128]{3,1,0,2:T(8,128)(2,1)} %copy.96, bf16[9,1,128,2,128]{2,4,1,3,0:T(8,128)(2,1)S(1)} %get-tuple-element.28, bf16[9,1,128,2,128]{2,4,1,3,0:T(8,128)(2,1)S(1)} %get-tuple-element.27), kind=kOutput, calls=%fused_computation.56 | convolution fusion | flops 268697600 | bytes 4325376 | tf_op jit(solution)/shard_map/zrbi,ziwc->wrbc/dot_general | solution.py:61
  45.9 2.3 %copy.95 = bf16[2,128,16,128]{3,1,0,2:T(8,128)(2,1)} copy(bf16[2,128,16,128]{1,3,2,0:T(8,128)(2,1)} %get-tuple-element.17) | data formatting | bytes 2097152
  48.2 3.1 %fusion.27 = f32[2,128,128,16,1]{2,1,4,3,0:T(8,128)} fusion(bf16[2,128,16,128]{3,1,0,2:T(8,128)(2,1)} %copy.95, bf16[9,1,128,2,128]{2,4,1,3,0:T(8,128)(2,1)S(1)} %get-tuple-element.28, bf16[9,1,128,2,128]{2,4,1,3,0:T(8,128)(2,1)S(1)} %get-tuple-element.27), kind=kOutput, calls=%fused_computation.58 | convolution fusion | flops 268697600 | bytes 4325376 | tf_op jit(solution)/shard_map/zrbi,ziwc->wrbc/dot_general | solution.py:61
  51.3 2.3 %copy.94 = bf16[2,128,16,128]{3,1,0,2:T(8,128)(2,1)} copy(bf16[2,128,16,128]{1,3,2,0:T(8,128)(2,1)} %get-tuple-element.18) | data formatting | bytes 2097152
  53.6 3.0 %fusion.29 = f32[2,128,128,16,1]{2,1,4,3,0:T(8,128)} fusion(bf16[2,128,16,128]{3,1,0,2:T(8,128)(2,1)} %copy.94, bf16[9,1,128,2,128]{2,4,1,3,0:T(8,128)(2,1)S(1)} %get-tuple-element.28, bf16[9,1,128,2,128]{2,4,1,3,0:T(8,128)(2,1)S(1)} %get-tuple-element.27), kind=kOutput, calls=%fused_computation.60 | convolution fusion | flops 268697600 | bytes 4325376 | tf_op jit(solution)/shard_map/zrbi,ziwc->wrbc/dot_general | solution.py:61
  56.6 2.3 %copy.102 = bf16[2,128,16,128]{3,1,0,2:T(8,128)(2,1)} copy(bf16[2,128,16,128]{1,3,2,0:T(8,128)(2,1)} %get-tuple-element.10) | data formatting | bytes 2097152
  58.9 6.8 %fusion = bf16[2,128,128,16]{2,1,3,0:T(8,128)(2,1)S(1)} fusion(f32[2,128,128,16,1]{2,1,4,3,0:T(8,128)S(1)} %fusion.15, f32[2,128,128,16,1]{2,1,4,3,0:T(8,128)} %fusion.17, f32[2,128,128,16,1]{2,1,4,3,0:T(8,128)} %fusion.19, f32[2,128,128,16,1]{2,1,4,3,0:T(8,128)} %fusion.21, f32[2,128,128,16,1]{2,1,4,3,0:T(8,128)} %fusion.23, ...), kind=kOutput, calls=%fused_computation.21 | convolution fusion | flops 273416192 | bytes 20054016 | tf_op jit(solution)/shard_map/zrbi,ziwc->wrbc/dot_general | solution.py:61
  65.7 1.9 %collective-permute-start.2 = (bf16[2,128,64]{1,2,0:T(8,128)(2,1)S(1)}, bf16[2,128,64]{1,2,0:T(8,128)(2,1)S(1)}, u32[]{:S(2)}, u32[]{:S(2)}) collective-permute-start(bf16[2,128,64]{1,2,0:T(8,128)(2,1)S(1)} %get-tuple-element.22), channel_id=1, source_target_pairs={{1,0},{2,1},{3,2},{5,4},{6,5},{7,6},{9,8},{10,9},{11,10},{13,12},{... | collective-permute-start | bytes 98312 | tf_op jit(solution)/shard_map/ppermute | solution.py:26
  67.7 3.6 %collective-permute-start.1 = (bf16[2,128,64]{1,2,0:T(8,128)(2,1)S(1)}, bf16[2,128,64]{1,2,0:T(8,128)(2,1)S(1)}, u32[]{:S(2)}, u32[]{:S(2)}) collective-permute-start(bf16[2,128,64]{1,2,0:T(8,128)(2,1)S(1)} %get-tuple-element.21), channel_id=1, source_target_pairs={{0,1},{1,2},{2,3},{4,5},{5,6},{6,7},{8,9},{9,10},{10,11},{12,13},{... | collective-permute-start | bytes 98312 | tf_op jit(solution)/shard_map/ppermute | solution.py:23
  72.3 2.0 %reshape.455 = bf16[16,32896]{1,0:T(8,128)(2,1)S(1)} reshape(bf16[16,128,257]{2,1,0:T(8,128)(2,1)S(1)} %pad.87) | data formatting | bytes 2105344 | tf_op jit(solution)/shard_map/reshape | solution.py:37
  74.7 0.9 copy-done.2
  77.1 1.1 copy.55
  78.1 5.6 %all-to-all-start = ((bf16[2,8,256,128]{3,2,0,1:T(8,128)(2,1)}), bf16[2,8,256,128]{3,2,0,1:T(8,128)(2,1)S(1)}, u32[]{:S(2)}, u32[]{:S(2)}) async-start(bf16[2,8,256,128]{3,2,0,1:T(8,128)(2,1)} %copy.55), calls=%async_computation | async-start | bytes 2097152 | tf_op jit(solution)/shard_map/all_to_all | solution.py:125
  83.8 1.1 reshape.452
  85.5 24.1 %all-to-all-done = bf16[2,8,256,128]{3,2,0,1:T(8,128)(2,1)S(1)} async-done(((bf16[2,8,256,128]{3,2,0,1:T(8,128)(2,1)}), bf16[2,8,256,128]{3,2,0,1:T(8,128)(2,1)S(1)}, u32[]{:S(2)}, u32[]{:S(2)}) %all-to-all-start) | async-done | bytes 1048608 | tf_op jit(solution)/shard_map/all_to_all | solution.py:125
  110.3 1.9 %fusion.110 = (bf16[2,256,8,128]{1,3,2,0:T(8,128)(2,1)}, bf16[2,256,8,128]{1,3,2,0:T(8,128)(2,1)S(1)}, bf16[2,256,8,128]{1,3,2,0:T(8,128)(2,1)S(1)}, bf16[2,256,8,128]{1,3,2,0:T(8,128)(2,1)}, bf16[2,256,8,128]{1,3,2,0:T(8,128)(2,1)}) fusion(bf16[2,256,12,128]{1,3,2,0:T(8,128)(2,1)S(1)} %bitcast.302), kind=kLoop, calls=%fused_computation.190 | loop fusion | bytes 10485760 | tf_op jit(solution)/shard_map/slice | solution.py:60
  112.2 1.3 copy.108
  113.5 1.3 copy.107
  114.9 1.8 %fusion.6 = f32[2,128,256,8,1]{2,1,4,3,0:T(8,128)S(1)} fusion(bf16[2,256,8,128]{3,1,0,2:T(8,128)(2,1)} %copy.108, bf16[5,1,128,2,128]{2,4,1,3,0:T(8,128)(2,1)S(1)} %get-tuple-element.30, bf16[5,1,128,2,128]{2,4,1,3,0:T(8,128)(2,1)S(1)} %get-tuple-element.29), kind=kOutput, calls=%fused_computation.37 | convolution fusion | flops 268697600 | bytes 3801088 | tf_op jit(solution)/shard_map/zrbi,ziwc->wrbc/dot_general | solution.py:61
  116.6 1.8 %fusion.8 = f32[2,128,256,8,1]{2,1,4,3,0:T(8,128)} fusion(bf16[2,256,8,128]{3,1,0,2:T(8,128)(2,1)S(1)} %copy-done.4, bf16[5,1,128,2,128]{2,4,1,3,0:T(8,128)(2,1)S(1)} %get-tuple-element.30, bf16[5,1,128,2,128]{2,4,1,3,0:T(8,128)(2,1)S(1)} %get-tuple-element.29), kind=kOutput, calls=%fused_computation.39 | convolution fusion | flops 268697600 | bytes 3801088 | tf_op jit(solution)/shard_map/zrbi,ziwc->wrbc/dot_general | solution.py:61
  118.4 2.3 %copy.106 = bf16[2,256,8,128]{3,1,0,2:T(8,128)(2,1)} copy(bf16[2,256,8,128]{1,3,2,0:T(8,128)(2,1)} %get-tuple-element.8) | data formatting | bytes 2097152
  120.7 3.0 %fusion.10 = f32[2,128,256,8,1]{2,1,4,3,0:T(8,128)} fusion(bf16[2,256,8,128]{3,1,0,2:T(8,128)(2,1)} %copy.106, bf16[5,1,128,2,128]{2,4,1,3,0:T(8,128)(2,1)S(1)} %get-tuple-element.30, bf16[5,1,128,2,128]{2,4,1,3,0:T(8,128)(2,1)S(1)} %get-tuple-element.29), kind=kOutput, calls=%fused_computation.41 | convolution fusion | flops 268697600 | bytes 3801088 | tf_op jit(solution)/shard_map/zrbi,ziwc->wrbc/dot_general | solution.py:61
  123.7 2.3 %copy.105 = bf16[2,256,8,128]{3,1,0,2:T(8,128)(2,1)} copy(bf16[2,256,8,128]{1,3,2,0:T(8,128)(2,1)} %get-tuple-element.9) | data formatting | bytes 2097152
  126.0 3.0 %fusion.12 = f32[2,128,256,8,1]{2,1,4,3,0:T(8,128)} fusion(bf16[2,256,8,128]{3,1,0,2:T(8,128)(2,1)} %copy.105, bf16[5,1,128,2,128]{2,4,1,3,0:T(8,128)(2,1)S(1)} %get-tuple-element.30, bf16[5,1,128,2,128]{2,4,1,3,0:T(8,128)(2,1)S(1)} %get-tuple-element.29), kind=kOutput, calls=%fused_computation.43 | convolution fusion | flops 268697600 | bytes 3801088 | tf_op jit(solution)/shard_map/zrbi,ziwc->wrbc/dot_general | solution.py:61
  129.0 2.3 %copy.109 = bf16[2,256,8,128]{3,1,0,2:T(8,128)(2,1)} copy(bf16[2,256,8,128]{1,3,2,0:T(8,128)(2,1)} %get-tuple-element.5) | data formatting | bytes 2097152
  131.3 5.1 %bitcast_add_fusion = f32[2,128,256,8]{2,1,3,0:T(8,128)} fusion(f32[2,128,256,8,1]{2,1,4,3,0:T(8,128)S(1)} %fusion.6, f32[2,128,256,8,1]{2,1,4,3,0:T(8,128)} %fusion.8, f32[2,128,256,8,1]{2,1,4,3,0:T(8,128)} %fusion.10, f32[2,128,256,8,1]{2,1,4,3,0:T(8,128)} %fusion.12, bf16[2,256,8,128]{3,1,0,2:T(8,128)(2,1)} %copy.109, ...), kind=kOutput, calls=%fused_computation.16 | convolution fusion | flops 270794752 | bytes 12189696 | tf_op jit(solution)/shard_map/zrbi,ziwc->wrbc/dot_general | solution.py:61
  136.4 2.9 %copy.62 = f32[2,1,256,1024]{3,2,1,0:T(8,128)} copy(f32[2,1,256,1024]{2,3,0,1:T(8,128)} %bitcast.304) | data formatting | bytes 4194304 | tf_op jit(solution)/shard_map/broadcast_in_dim;reshape | solution.py:124
  (54 shorter events, 7.3 us)
Async XLA Ops:
  0.0 4.4 %copy-start.7 = (bf16[2,1024]{1,0:T(2,128)(2,1)S(1)}, bf16[2,1024]{1,0:T(2,128)(2,1)}, u32[]{:S(2)}) copy-start(bf16[2,1024]{1,0:T(2,128)(2,1)} %param.6) | copy-start | bytes 12292
  2.5 11.7 %collective-permute-start = (bf16[2,128,1024]{1,2,0:T(8,128)(2,1)}, bf16[2,128,1024]{1,2,0:T(8,128)(2,1)}, u32[]{:S(2)}, u32[]{:S(2)}) collective-permute-start(bf16[2,128,1024]{1,2,0:T(8,128)(2,1)} %slice.209), channel_id=1, source_target_pairs={{1,0},{2,1},{3,2},{5,4},{6,5},{7,6},{9,8},{10,9},{11,10},{13,12},{... | collective-permute-start | bytes 1572872 | tf_op jit(solution)/shard_map/ppermute | solution.py:15
  7.2 1.0 copy-start.5
  7.4 1.2 copy-start.6
  21.0 1.8 %copy-start.3 = (bf16[2,128,16,128]{3,1,0,2:T(8,128)(2,1)S(1)}, bf16[2,128,16,128]{3,1,0,2:T(8,128)(2,1)}, u32[]{:S(2)}) copy-start(bf16[2,128,16,128]{3,1,0,2:T(8,128)(2,1)} %copy.100) | copy-start | bytes 3145732
  58.9 12.4 %copy-start = (bf16[16,96,128]{1,2,0:T(8,128)(2,1)S(1)}, bf16[16,96,128]{1,2,0:T(8,128)(2,1)}, u32[]{:S(2)}) copy-start(bf16[16,96,128]{1,2,0:T(8,128)(2,1)} %pad_select_fusion) | copy-start | bytes 1179652
  65.7 6.1 %copy-start.1 = (bf16[2,128,128,16]{2,1,3,0:T(8,128)(2,1)}, bf16[2,128,128,16]{2,1,3,0:T(8,128)(2,1)S(1)}, u32[]{:S(2)}) copy-start(bf16[2,128,128,16]{2,1,3,0:T(8,128)(2,1)S(1)} %fusion) | copy-start | bytes 3145732
  65.7 8.9 %collective-permute-start.2 = (bf16[2,128,64]{1,2,0:T(8,128)(2,1)S(1)}, bf16[2,128,64]{1,2,0:T(8,128)(2,1)S(1)}, u32[]{:S(2)}, u32[]{:S(2)}) collective-permute-start(bf16[2,128,64]{1,2,0:T(8,128)(2,1)S(1)} %get-tuple-element.22), channel_id=1, source_target_pairs={{1,0},{2,1},{3,2},{5,4},{6,5},{7,6},{9,8},{10,9},{11,10},{13,12},{... | collective-permute-start | bytes 98312 | tf_op jit(solution)/shard_map/ppermute | solution.py:26
  67.7 7.0 %collective-permute-start.1 = (bf16[2,128,64]{1,2,0:T(8,128)(2,1)S(1)}, bf16[2,128,64]{1,2,0:T(8,128)(2,1)S(1)}, u32[]{:S(2)}, u32[]{:S(2)}) collective-permute-start(bf16[2,128,64]{1,2,0:T(8,128)(2,1)S(1)} %get-tuple-element.21), channel_id=1, source_target_pairs={{0,1},{1,2},{2,3},{4,5},{5,6},{6,7},{8,9},{9,10},{10,11},{12,13},{... | collective-permute-start | bytes 98312 | tf_op jit(solution)/shard_map/ppermute | solution.py:23
  74.3 1.2 copy-start.2
  77.1 6.6 %copy-start.8 = (bf16[2,512]{1,0:T(2,128)(2,1)S(1)}, bf16[2,512]{1,0:T(2,128)(2,1)}, u32[]{:S(2)}) copy-start(bf16[2,512]{1,0:T(2,128)(2,1)} %param.9) | copy-start | bytes 6148
  78.1 31.5 %all-to-all-start = ((bf16[2,8,256,128]{3,2,0,1:T(8,128)(2,1)}), bf16[2,8,256,128]{3,2,0,1:T(8,128)(2,1)S(1)}, u32[]{:S(2)}, u32[]{:S(2)}) async-start(bf16[2,8,256,128]{3,2,0,1:T(8,128)(2,1)} %copy.55), calls=%async_computation | async-start | bytes 2097152 | tf_op jit(solution)/shard_map/all_to_all | solution.py:125
  114.9 1.8 %copy-start.4 = (bf16[2,256,8,128]{3,1,0,2:T(8,128)(2,1)S(1)}, bf16[2,256,8,128]{3,1,0,2:T(8,128)(2,1)}, u32[]{:S(2)}) copy-start(bf16[2,256,8,128]{3,1,0,2:T(8,128)(2,1)} %copy.107) | copy-start | bytes 3145732
where the time goes:
time: 140 us; the launch traced here: 139 us
  local copies, waits for them, and re-layouts  50.2 us (36%)
  matrix products  44.1 us (32%)
  waiting for transfers between devices  26.2 us (19%)
  starting transfers between devices  13.1 us (9%)
  other arithmetic  5.24 us (4%)
    dot_general x14, matrix products, correlate(): jnp.einsum('zrbi,ziwc->wrbc', window, kernel[tap_block], preferred_elemen...  43.3 us
    unnamed x34, local copies, waits for them, and re-layouts  31.6 us
    all_to_all x1, waiting for transfers between devices, per_device(): lax.all_to_all(grouped, 'pulse', split_axis=1, concat_axis=3, tiled=True)  24.1 us
    all_to_all x1, starting transfers between devices, per_device(): lax.all_to_all(grouped, 'pulse', split_axis=1, concat_axis=3, tiled=True)  5.56 us
    slice x2, local copies, waits for them, and re-layouts, correlate(): window = blocks[:, :, tap_block:tap_block + out_blocks]  5.04 us
    reshape x3, local copies, waits for them, and re-layouts, skew_rows(): padded.reshape(leading + (row_count * (row_length + row_count),))  4.79 us
    ppermute x1, starting transfers between devices, with_halo(): lax.ppermute(lax.slice_in_dim(block, block.shape[dim] - width, None, axis...  3.64 us
    select_n x5, other arithmetic, band_matrices(): placed = jnp.where(shifts // step_size % 2 == 1, shifted, placed)  3.29 us
  transfers between devices with their start and end apart: 4, of which 2 were waited for; matrix products, arithmetic and copies ran while one was open for 9% of the time, Pallas kernels for 0%

commit v1 on v0

v1 whole, which is shorter than its diff:
```python
import functools

import jax
import jax.numpy as jnp
from jax import lax
from jax.experimental import pallas as pl
from jax.experimental.pallas import tpu as pltpu
from jax.sharding import PartitionSpec as P

RT = 1024
AT = 512
BAND = 64
BLK = 128
HALF = BLK // 2
WIDE = 2 * BLK
RANGE_TILES = RT // BLK + 2
AZ_TILES = AT // BLK + 1
HEAD = RT // BLK + 1
GROUP = 2 * BLK
LIMIT = 24 * 1024 * 1024

VMEM = functools.partial(pl.BlockSpec, memory_space=pltpu.VMEM)
SMEM = functools.partial(pl.BlockSpec, memory_space=pltpu.SMEM)


def params():
    return pltpu.CompilerParams(vmem_limit_bytes=LIMIT)


def pack_head_body(echoes, head, last):
    for block in range(HEAD):
        for part in range(2):
            head[block, :, part * BLK : (part + 1) * BLK] = echoes[
                part, :, block * BLK : (block + 1) * BLK
            ]
    for part in range(2):
        last[0, :, part * BLK : (part + 1) * BLK] = echoes[part, :, -BLK:]


def pack_head(echoes):
    pulses = echoes.shape[1]
    return pl.pallas_call(
        pack_head_body,
        out_shape=(
            jax.ShapeDtypeStruct((HEAD, pulses, WIDE), jnp.bfloat16),
            jax.ShapeDtypeStruct((1, pulses, WIDE), jnp.bfloat16),
        ),
        in_specs=[VMEM()],
        out_specs=(VMEM(), VMEM()),
        compiler_params=params(),
        name="pack_head",
    )(echoes)


def toeplitz_tiles(taps, tiles, out):
    skewed = []
    for part in range(2):
        row = jnp.broadcast_to(taps[part : part + 1, :].astype(jnp.float32), (BLK, taps.shape[1]))
        skewed.append(pltpu.roll(row, 0, 1, stride=1, stride_axis=0))
    for tile in range(tiles):
        span = slice((tile + 1) * BLK, (tile + 2) * BLK)
        real = skewed[0][:, span].T
        imag = skewed[1][:, span].T
        out[tile, :BLK, :BLK] = real.astype(jnp.bfloat16)
        out[tile, :BLK, BLK:] = (-imag).astype(jnp.bfloat16)
        out[tile, BLK:, :BLK] = imag.astype(jnp.bfloat16)
        out[tile, BLK:, BLK:] = real.astype(jnp.bfloat16)


def prepare_body(first, range_taps, az_taps, weights, offsets, range_out, az_out, band_out):
    toeplitz_tiles(range_taps, RANGE_TILES, range_out)
    toeplitz_tiles(az_taps, AZ_TILES, az_out)
    bins = weights.shape[1]
    lane = lax.broadcasted_iota(jnp.int32, (BLK, WIDE), 1)
    for block in range(bins // BLK):
        span = slice(block * BLK, (block + 1) * BLK)
        placed = jnp.concatenate(
            [weights[:, span].astype(jnp.float32), jnp.zeros((BLK - BAND, BLK), jnp.float32)], axis=0
        )
        shifts = offsets[:, span]
        for bit in range((BAND // 2).bit_length()):
            chosen = jnp.broadcast_to((shifts >> bit) & 1, (BLK, BLK)) == 1
            placed = jnp.where(chosen, pltpu.roll(placed, 1 << bit, 0), placed)
        wide = jnp.concatenate([placed.T, jnp.zeros((BLK, BLK), jnp.float32)], axis=1)
        skewed = pltpu.roll(wide, BAND // 2, 1, stride=1, stride_axis=0)
        if block == 0:
            skewed = jnp.where((first[0] == 1) & (lane < HALF), 0.0, skewed)
        band_out[span, :] = skewed.astype(jnp.bfloat16)


def prepare(first, range_ref, azimuth_ref, weights, offsets):
    bins = weights.shape[1]
    range_taps = jnp.pad(range_ref, ((0, 0), (BLK + HALF, BLK + HALF)))
    az_taps = jnp.pad(azimuth_ref, ((0, 0), (BLK, BLK)))
    return pl.pallas_call(
        prepare_body,
        out_shape=(
            jax.ShapeDtypeStruct((RANGE_TILES, WIDE, WIDE), jnp.bfloat16),
            jax.ShapeDtypeStruct((AZ_TILES, WIDE, WIDE), jnp.bfloat16),
            jax.ShapeDtypeStruct((bins, WIDE), jnp.bfloat16),
        ),
        in_specs=[SMEM()] + [VMEM()] * 4,
        out_specs=(VMEM(),) * 3,
        compiler_params=params(),
        name="prepare",
    )(first, range_taps, az_taps, weights, offsets.reshape(1, bins))


def assemble_body(left, head, echoes, right, out):
    out[0] = left[0]
    out[1 : HEAD + 1] = head[...]
    blocks = echoes.shape[2] // BLK
    for block in range(HEAD, blocks):
        for part in range(2):
            out[block + 1, :, part * BLK : (part + 1) * BLK] = echoes[
                part, :, block * BLK : (block + 1) * BLK
            ]
    out[blocks + 1 :] = right[...]


def assemble(left, head, echoes, right):
    pulses = echoes.shape[1]
    blocks = 1 + echoes.shape[2] // BLK + HEAD
    return pl.pallas_call(
        assemble_body,
        out_shape=jax.ShapeDtypeStruct((blocks, pulses, WIDE), jnp.bfloat16),
        in_specs=[VMEM()] * 4,
        out_specs=VMEM(),
        compiler_params=params(),
        name="assemble",
    )(left, head, echoes, right)


def focus_range_body(which, samples, range_tiles, bands, *outs):
    pulses = samples.shape[1]
    for place, out in enumerate(outs):
        group = which[place]
        total = jnp.zeros((3 * pulses, WIDE), jnp.float32)
        for tile in range(RANGE_TILES):
            window = samples[pl.ds(2 * group + tile, 3)].reshape(3 * pulses, WIDE)
            total += jnp.dot(window, range_tiles[tile], preferred_element_type=jnp.float32)
        compressed = total.astype(jnp.bfloat16)
        for half in range(2):
            low = compressed[half * pulses : (half + 1) * pulses]
            high = compressed[(half + 1) * pulses : (half + 2) * pulses]
            reach = jnp.concatenate(
                [
                    jnp.concatenate([low[:, :BLK], high[:, :BLK]], axis=1),
                    jnp.concatenate([low[:, BLK:], high[:, BLK:]], axis=1),
                ],
                axis=0,
            )
            start = pl.multiple_of(group * GROUP + half * BLK, BLK)
            migrated = lax.dot_general(
                bands[pl.ds(start, BLK)],
                reach,
                (((1,), (1,)), ((), ())),
                preferred_element_type=jnp.float32,
            )
            out[half * BLK : (half + 1) * BLK, :] = migrated.astype(jnp.bfloat16)


def focus_range(groups, samples, range_tiles, bands):
    pulses = samples.shape[1]
    count = len(groups)
    return pl.pallas_call(
        focus_range_body,
        out_shape=(jax.ShapeDtypeStruct((GROUP, 2 * pulses), jnp.bfloat16),) * count,
        in_specs=[SMEM()] + [VMEM()] * 3,
        out_specs=(VMEM(),) * count,
        compiler_params=params(),
        name="focus_range",
    )(jnp.stack(groups).astype(jnp.int32), samples, range_tiles, bands)


def focus_azimuth_body(where, az_tiles, *rest):
    parts, out, rows = rest[:-2], rest[-2], rest[-1]
    count = len(parts)
    bins = parts[0].shape[0]
    edge = (AZ_TILES // 2) * bins
    rows[:edge] = jnp.zeros((edge, WIDE), jnp.bfloat16)
    rows[edge + count * bins :] = jnp.zeros((edge, WIDE), jnp.bfloat16)
    for place, part in enumerate(parts):
        start = pl.multiple_of(edge + where[place] * bins, bins)
        rows[pl.ds(start, bins)] = part[...]
    for block in range(count):
        total = jnp.zeros((bins, WIDE), jnp.float32)
        for tile in range(AZ_TILES):
            if 0 <= block + tile - AZ_TILES // 2 < count:
                total += jnp.dot(
                    rows[(block + tile) * bins : (block + tile + 1) * bins],
                    az_tiles[tile],
                    preferred_element_type=jnp.float32,
                )
        for part in range(2):
            out[part, 0, :, block * BLK : (block + 1) * BLK] = total[
                :, part * BLK : (part + 1) * BLK
            ]


def focus_azimuth(where, az_tiles, parts):
    count = len(parts)
    bins = parts[0].shape[0]
    return pl.pallas_call(
        focus_azimuth_body,
        out_shape=jax.ShapeDtypeStruct((2, 1, bins, count * BLK), jnp.float32),
        in_specs=[SMEM()] + [VMEM()] * (1 + count),
        out_specs=VMEM(),
        scratch_shapes=[pltpu.VMEM(((count + AZ_TILES - 1) * bins, WIDE), jnp.bfloat16)],
        compiler_params=params(),
        name="focus_azimuth",
    )(jnp.stack(where).astype(jnp.int32), az_tiles, *parts)


def per_device(echoes, range_ref, band_weights, band_offsets, azimuth_ref):
    quarter_len = echoes.shape[2]
    peers = lax.axis_size("pulse")
    quarters = lax.axis_size("rng")
    bins = quarter_len // peers
    me = lax.axis_index("pulse")
    down = [(i + 1, i) for i in range(quarters - 1)]
    up = [(i, i + 1) for i in range(quarters - 1)]

    head, last = pack_head(echoes)
    right = lax.ppermute(head, "rng", down)
    left = lax.ppermute(last, "rng", up)
    first = (lax.axis_index("rng") == 0).astype(jnp.int32).reshape(1)
    head, band_offsets = lax.optimization_barrier((head, band_offsets))
    range_tiles, az_tiles, bands = prepare(
        first, range_ref, azimuth_ref, band_weights, band_offsets
    )
    samples = assemble(left, head, echoes, right)

    if bins == GROUP and peers & (peers - 1) == 0:
        order = list(range(peers // 2, peers)) + list(range(1, peers // 2)) + [0]
        steps = [order[:1], order[1 : peers // 2], order[peers // 2 :]]
        parts, where = [], []
        for step in steps:
            groups = [me ^ k for k in step]
            made = focus_range(groups, samples, range_tiles, bands)
            for k, piece in zip(step, made):
                if k:
                    parts.append(lax.ppermute(piece, "pulse", [(i, i ^ k) for i in range(peers)]))
                else:
                    parts.append(piece)
                where.append(me ^ k)
            samples, made = lax.optimization_barrier((samples, made))
    else:
        made = focus_range(
            [jnp.int32(g) for g in range(quarter_len // GROUP)], samples, range_tiles, bands
        )
        migrated = jnp.concatenate(made, axis=0)
        swapped = lax.all_to_all(
            migrated.reshape(peers, bins, WIDE), "pulse", split_axis=0, concat_axis=0, tiled=True
        )
        parts = [swapped[i] for i in range(peers)]
        where = [jnp.int32(i) for i in range(peers)]
    return focus_azimuth(where, az_tiles, parts)


def solution(mesh):
    return jax.shard_map(
        per_device,
        mesh=mesh,
        in_specs=(P(None, "pulse", "rng"), P(), P(None, "rng"), P("rng"), P()),
        out_specs=P(None, "rng", "pulse", None),
        check_vma=False,
    )
```

time: 140 us -> 50.9 us (0.36)
  local copies, waits for them, and re-layouts: 50.2 us -> 4.41 us
  matrix products: 44.1 us -> 0 us
  Pallas kernels: 0 us -> 15.6 us
  waiting for transfers between devices: 26.2 us -> 14 us
  other arithmetic: 5.24 us -> 0.16 us
  starting transfers between devices: 13.1 us -> 16 us
    dot_general x16 -> x0, matrix products: 44.1 us -> none  [the longest x14 43.3 us: correlate(): jnp.einsum('zrbi,ziwc->wrbc', window, kernel[tap_block], preferred_elemen...]
    unnamed x34 -> x8, local copies, waits for them, and re-layouts: 31.6 us -> 2.88 us
    all_to_all x1 -> x0, waiting for transfers between devices: 24.1 us -> none  [per_device(): lax.all_to_all(grouped, 'pulse', split_axis=1, concat_axis=3, tiled=True)]
    pallas_call x0 -> x7, Pallas kernels: none -> 15.6 us  [the longest x3 10.4 us: focus_range(): pl.pallas_call(focus_range_body, out_shape=(jax.ShapeDtypeStruct((GROUP,...]
    ppermute x3 -> x9, waiting for transfers between devices: 2.09 us -> 14 us  [the longest x7 13.3 us: per_device(): lax.ppermute(piece, 'pulse', [(i, i ^ k) for i in range(peers)])]
    ppermute x3 -> x9, starting transfers between devices: 7.52 us -> 16 us  [the longest x7 9.46 us: per_device(): lax.ppermute(piece, 'pulse', [(i, i ^ k) for i in range(peers)])]
    slice x9 -> x0, local copies, waits for them, and re-layouts: 7.24 us -> none  [the longest x2 5.04 us: correlate(): window = blocks[:, :, tap_block:tap_block + out_blocks]]
    all_to_all x1 -> x0, starting transfers between devices: 5.56 us -> none  [per_device(): lax.all_to_all(grouped, 'pulse', split_axis=1, concat_axis=3, tiled=True)]
  transfers between devices with their start and end apart: 4 -> 9, of which waited for: 2 -> 5; matrix products, arithmetic and copies ran while one was open for 9% -> 3% of each run, Pallas kernels for 0% -> 22%
where the time goes in v1:
time: 50.9 us; the launch traced here: 50.2 us
  starting transfers between devices  16 us (31%)
  Pallas kernels  15.6 us (31%)
  waiting for transfers between devices  14 us (28%)
  local copies, waits for them, and re-layouts  4.41 us (9%)
    ppermute x7, waiting for transfers between devices, per_device(): lax.ppermute(piece, 'pulse', [(i, i ^ k) for i in range(peers)])  13.3 us
    pallas_call x3, Pallas kernels, focus_range(): pl.pallas_call(focus_range_body, out_shape=(jax.ShapeDtypeStruct((GROUP,...  10.4 us
    ppermute x7, starting transfers between devices, per_device(): lax.ppermute(piece, 'pulse', [(i, i ^ k) for i in range(peers)])  9.46 us
    ppermute x1, starting transfers between devices, per_device(): left = lax.ppermute(last, 'rng', up)  4.46 us
    pallas_call x1, Pallas kernels, focus_azimuth(): pl.pallas_call(focus_azimuth_body, out_shape=jax.ShapeDtypeStruct((2, 1,...  3.23 us
    unnamed x8, local copies, waits for them, and re-layouts  2.88 us
    ppermute x1, starting transfers between devices, per_device(): right = lax.ppermute(head, 'rng', down)  2.1 us
    pallas_call x1, Pallas kernels, prepare(): pl.pallas_call(prepare_body, out_shape=(jax.ShapeDtypeStruct((RANGE_TILES...  1.63 us
  transfers between devices with their start and end apart: 9, of which 5 were waited for; matrix products, arithmetic and copies ran while one was open for 3% of the time, Pallas kernels for 22%

profile of v1, /device:TPU:1, one launch (start us, length us, event | category | flops | bytes accessed | tf_op | source)
XLA Modules:
  0.0 50.2 jit_solution(9246571314839468166)
XLA Ops:
  0.0 0.0 copy-start
  0.0 1.2 %copy-done = bf16[2,128,2048]{2,1,0:T(8,128)(2,1)S(1)} copy-done((bf16[2,128,2048]{2,1,0:T(8,128)(2,1)S(1)}, bf16[2,128,2048]{2,1,0:T(8,128)(2,1)}, u32[]{:S(2)}) %copy-start) | copy-done | bytes 1048600
  1.2 0.0 copy-start.1
  1.2 0.1 pack_head.1
  1.3 2.1 %collective-permute-start.1 = (bf16[9,128,256]{2,1,0:T(8,128)(2,1)S(1)}, bf16[9,128,256]{2,1,0:T(8,128)(2,1)S(1)}, u32[]{:S(2)}, u32[]{:S(2)}) collective-permute-start(bf16[9,128,256]{2,1,0:T(8,128)(2,1)S(1)} %get-tuple-element.25.head), channel_id=1, source_target_pairs={{1,0},{2,1},{3,2},{5,4},{6,5},{7,6},{9,8},{10,9},{11,10},{13,12},{... | collective-permute-start | bytes 1769480 | tf_op jit(solution)/shard_map/ppermute | solution.py:225
  3.5 4.5 %collective-permute-start = (bf16[1,128,256]{2,1,0:T(8,128)(2,1)S(1)}, bf16[1,128,256]{2,1,0:T(8,128)(2,1)S(1)}, u32[]{:S(2)}, u32[]{:S(2)}) collective-permute-start(bf16[1,128,256]{2,1,0:T(8,128)(2,1)S(1)} %get-tuple-element.24), channel_id=1, source_target_pairs={{0,1},{1,2},{2,3},{4,5},{5,6},{6,7},{8,9},{9,10},{10,11},{12,13},{... | collective-permute-start | bytes 196616 | tf_op jit(solution)/shard_map/ppermute | solution.py:226
  7.9 0.7 %pad.9.az_taps = bf16[2,768]{1,0:T(2,128)(2,1)S(1)} pad(bf16[2,512]{1,0:T(2,128)(2,1)} %param.9, bf16[]{:T(256)} %constant.26.clone.1), padding=0_0x128_128 | pad | bytes 5122 | tf_op jit(solution)/shard_map/jit(_pad)/pad | solution.py:94
  8.6 0.8 %pad.8.range_taps = bf16[2,1408]{1,0:T(2,128)(2,1)S(1)} pad(bf16[2,1024]{1,0:T(2,128)(2,1)} %param.6, bf16[]{:T(256)} %constant.26.clone.1), padding=0_0x192_192 | pad | bytes 9730 | tf_op jit(solution)/shard_map/jit(_pad)/pad | solution.py:93
  9.4 0.0 copy-start.2
  9.4 0.9 %copy-done.2 = bf16[64,2048]{1,0:T(8,128)(2,1)S(1)} copy-done((bf16[64,2048]{1,0:T(8,128)(2,1)S(1)}, bf16[64,2048]{1,0:T(8,128)(2,1)}, u32[]{:S(2)}) %copy-start.2) | copy-done | bytes 262168
  10.3 0.0 copy-start.3
  10.3 0.7 %copy-done.3 = s32[2048]{0:T(1024)S(1)} copy-done((s32[2048]{0:T(1024)S(1)}, s32[2048]{0:T(1024)}, u32[]{:S(2)}) %copy-start.3) | copy-done | bytes 8216
  11.0 1.6 %prepare.1 = (bf16[10,256,256]{2,1,0:T(8,128)(2,1)S(1)}, bf16[5,256,256]{2,1,0:T(8,128)(2,1)S(1)}, bf16[2048,256]{1,0:T(8,128)(2,1)S(1)}) custom-call(s32[1]{0:T(128)} %bitcast.8.first, bf16[2,1408]{1,0:T(2,128)(2,1)S(1)} %pad.8.range_taps, bf16[2,768]{1,0:T(2,128)(2,1)S(1)} %pad.9.az_taps, bf16[64,2048]{1,0:T(8,128)(2,1)S(1)} %copy-done.2, ...), custom_call_target="tpu_custom_call" | custom-call | tf_op jit(solution)/shard_map/prepare/pallas_call | solution.py:95
  12.7 0.1 pad_add_fusion.which
  12.8 0.1 pad_add_fusion.1.which
  12.8 0.0 collective-permute-done.left
  12.8 0.7 %collective-permute-done.1.right = bf16[9,128,256]{2,1,0:T(8,128)(2,1)S(1)} collective-permute-done((bf16[9,128,256]{2,1,0:T(8,128)(2,1)S(1)}, bf16[9,128,256]{2,1,0:T(8,128)(2,1)S(1)}, u32[]{:S(2)}, u32[]{:S(2)}) %collective-permute-start.1) | collective-permute-done | bytes 589856 | tf_op jit(solution)/shard_map/ppermute | solution.py:225
  13.6 0.0 copy-done.1
  13.6 0.2 assemble.1.samples
  13.7 0.9 %focus_range.3 = bf16[256,256]{1,0:T(8,128)(2,1)S(1)} custom-call(s32[1]{0:T(128)} %bitcast.which, bf16[26,128,256]{2,1,0:T(8,128)(2,1)S(1)} %assemble.1.samples, bf16[10,256,256]{2,1,0:T(8,128)(2,1)S(1)} %get-tuple-element.26.range_tiles, bf16[2048,256]{1,0:T(8,128)(2,1)S(1)} %get-tuple-element.27.bands), custom_call_target="tpu_custom_call" | custom-call | tf_op jit(solution)/shard_map/focus_range/pallas_call | solution.py:166
  14.6 2.4 %collective-permute-start.2 = (bf16[256,256]{1,0:T(8,128)(2,1)S(1)}, bf16[256,256]{1,0:T(8,128)(2,1)S(1)}, u32[]{:S(2)}, u32[]{:S(2)}) collective-permute-start(bf16[256,256]{1,0:T(8,128)(2,1)S(1)} %focus_range.3), channel_id=1, source_target_pairs={{0,16},{4,20},{8,24},{12,28},{16,0},{20,4},{24,8},{28,12},{1,17},{... | collective-permute-start | bytes 393224 | tf_op jit(solution)/shard_map/ppermute | solution.py:243
  17.0 3.9 %focus_range.4 = (bf16[256,256]{1,0:T(8,128)(2,1)S(1)}, bf16[256,256]{1,0:T(8,128)(2,1)S(1)}, bf16[256,256]{1,0:T(8,128)(2,1)S(1)}) custom-call(s32[3]{0:T(128)S(1)} %pad_add_fusion.which, bf16[26,128,256]{2,1,0:T(8,128)(2,1)S(1)} %assemble.1.samples, bf16[10,256,256]{2,1,0:T(8,128)(2,1)S(1)} %get-tuple-element.26.range_tiles, ...), custom_call_target="tpu_custom_call" | custom-call | tf_op jit(solution)/shard_map/focus_range/pallas_call | solution.py:166
  20.9 5.6 %focus_range.5 = (bf16[256,256]{1,0:T(8,128)(2,1)S(1)}, bf16[256,256]{1,0:T(8,128)(2,1)S(1)}, bf16[256,256]{1,0:T(8,128)(2,1)S(1)}, bf16[256,256]{1,0:T(8,128)(2,1)S(1)}) custom-call(s32[4]{0:T(128)S(1)} %pad_add_fusion.1.which, bf16[26,128,256]{2,1,0:T(8,128)(2,1)S(1)} %assemble.1.samples, bf16[10,256,256]{2,1,0:T(8,128)(2,1)S(1)} %get-tuple-element.26.range_tiles, ...), custom_call_target="tpu_custom_call" | custom-call | tf_op jit(solution)/shard_map/focus_range/pallas_call | solution.py:166
  26.6 1.3 %collective-permute-start.6 = (bf16[256,256]{1,0:T(8,128)(2,1)S(1)}, bf16[256,256]{1,0:T(8,128)(2,1)S(1)}, u32[]{:S(2)}, u32[]{:S(2)}) collective-permute-start(bf16[256,256]{1,0:T(8,128)(2,1)S(1)} %get-tuple-element.33), channel_id=1, source_target_pairs={{0,4},{4,0},{8,12},{12,8},{16,20},{20,16},{24,28},{28,24},{1,5},{5... | collective-permute-start | bytes 393224 | tf_op jit(solution)/shard_map/ppermute | solution.py:243
  27.9 0.0 collective-permute-start.3
  27.9 1.3 %collective-permute-start.7 = (bf16[256,256]{1,0:T(8,128)(2,1)S(1)}, bf16[256,256]{1,0:T(8,128)(2,1)S(1)}, u32[]{:S(2)}, u32[]{:S(2)}) collective-permute-start(bf16[256,256]{1,0:T(8,128)(2,1)S(1)} %get-tuple-element.34), channel_id=1, source_target_pairs={{0,8},{4,12},{8,0},{12,4},{16,24},{20,28},{24,16},{28,20},{1,9},{5... | collective-permute-start | bytes 393224 | tf_op jit(solution)/shard_map/ppermute | solution.py:243
  29.2 1.1 %collective-permute-start.8 = (bf16[256,256]{1,0:T(8,128)(2,1)S(1)}, bf16[256,256]{1,0:T(8,128)(2,1)S(1)}, u32[]{:S(2)}, u32[]{:S(2)}) collective-permute-start(bf16[256,256]{1,0:T(8,128)(2,1)S(1)} %get-tuple-element.35), channel_id=1, source_target_pairs={{0,12},{4,8},{8,4},{12,0},{16,28},{20,24},{24,20},{28,16},{1,13},{... | collective-permute-start | bytes 393224 | tf_op jit(solution)/shard_map/ppermute | solution.py:243
  30.3 0.0 collective-permute-done.2.rest_0_
  30.3 3.3 %collective-permute-start.4 = (bf16[256,256]{1,0:T(8,128)(2,1)S(1)}, bf16[256,256]{1,0:T(8,128)(2,1)S(1)}, u32[]{:S(2)}, u32[]{:S(2)}) collective-permute-start(bf16[256,256]{1,0:T(8,128)(2,1)S(1)} %get-tuple-element.30), channel_id=1, source_target_pairs={{0,24},{4,28},{8,16},{12,20},{16,8},{20,12},{24,0},{28,4},{1,25},{... | collective-permute-start | bytes 393224 | tf_op jit(solution)/shard_map/ppermute | solution.py:243
  33.6 0.0 collective-permute-done.6.rest_4_
  33.6 0.0 collective-permute-start.5
  33.7 0.1 stack.49.where
  33.7 0.7 %collective-permute-done.7.rest_5_ = bf16[256,256]{1,0:T(8,128)(2,1)S(1)} collective-permute-done((bf16[256,256]{1,0:T(8,128)(2,1)S(1)}, bf16[256,256]{1,0:T(8,128)(2,1)S(1)}, u32[]{:S(2)}, u32[]{:S(2)}) %collective-permute-start.7) | collective-permute-done | bytes 131104 | tf_op jit(solution)/shard_map/ppermute | solution.py:243
  34.5 5.5 %collective-permute-done.8.rest_6_ = bf16[256,256]{1,0:T(8,128)(2,1)S(1)} collective-permute-done((bf16[256,256]{1,0:T(8,128)(2,1)S(1)}, bf16[256,256]{1,0:T(8,128)(2,1)S(1)}, u32[]{:S(2)}, u32[]{:S(2)}) %collective-permute-start.8) | collective-permute-done | bytes 131104 | tf_op jit(solution)/shard_map/ppermute | solution.py:243
  40.0 0.0 collective-permute-done.3.rest_1_
  40.0 3.6 %collective-permute-done.4.rest_2_ = bf16[256,256]{1,0:T(8,128)(2,1)S(1)} collective-permute-done((bf16[256,256]{1,0:T(8,128)(2,1)S(1)}, bf16[256,256]{1,0:T(8,128)(2,1)S(1)}, u32[]{:S(2)}, u32[]{:S(2)}) %collective-permute-start.4) | collective-permute-done | bytes 131104 | tf_op jit(solution)/shard_map/ppermute | solution.py:243
  43.5 3.5 %collective-permute-done.5.rest_3_ = bf16[256,256]{1,0:T(8,128)(2,1)S(1)} collective-permute-done((bf16[256,256]{1,0:T(8,128)(2,1)S(1)}, bf16[256,256]{1,0:T(8,128)(2,1)S(1)}, u32[]{:S(2)}, u32[]{:S(2)}) %collective-permute-start.5) | collective-permute-done | bytes 131104 | tf_op jit(solution)/shard_map/ppermute | solution.py:243
  47.0 3.2 %focus_azimuth.1 = f32[2,1,256,1024]{3,2,1,0:T(8,128)} custom-call(s32[8]{0:T(128)S(1)} %stack.49.where, bf16[5,256,256]{2,1,0:T(8,128)(2,1)S(1)} %get-tuple-element.23.az_tiles, bf16[256,256]{1,0:T(8,128)(2,1)S(1)} %collective-permute-done.2.rest_0_, bf16[256,256]{1,0:T(8,128)(2,1)S(1)} %collective-permute-done.3.rest_1_, ...), custom_call_target="tpu_custom_call" | custom-call | tf_op jit(solution)/shard_map/focus_azimuth/pallas_call | solution.py:204
Async XLA Ops:
  0.0 1.2 %copy-start = (bf16[2,128,2048]{2,1,0:T(8,128)(2,1)S(1)}, bf16[2,128,2048]{2,1,0:T(8,128)(2,1)}, u32[]{:S(2)}) copy-start(bf16[2,128,2048]{2,1,0:T(8,128)(2,1)} %echoes.3) | copy-start | bytes 3145732
  1.2 12.3 %copy-start.1 = (bf16[2,128,2048]{2,1,0:T(8,128)(2,1)S(1)}, bf16[2,128,2048]{2,1,0:T(8,128)(2,1)}, u32[]{:S(2)}) copy-start(bf16[2,128,2048]{2,1,0:T(8,128)(2,1)} %echoes.3) | copy-start | bytes 3145732
  1.3 12.2 %collective-permute-start.1 = (bf16[9,128,256]{2,1,0:T(8,128)(2,1)S(1)}, bf16[9,128,256]{2,1,0:T(8,128)(2,1)S(1)}, u32[]{:S(2)}, u32[]{:S(2)}) collective-permute-start(bf16[9,128,256]{2,1,0:T(8,128)(2,1)S(1)} %get-tuple-element.25.head), channel_id=1, source_target_pairs={{1,0},{2,1},{3,2},{5,4},{6,5},{7,6},{9,8},{10,9},{11,10},{13,12},{... | collective-permute-start | bytes 1769480 | tf_op jit(solution)/shard_map/ppermute | solution.py:225
  3.5 9.4 %collective-permute-start = (bf16[1,128,256]{2,1,0:T(8,128)(2,1)S(1)}, bf16[1,128,256]{2,1,0:T(8,128)(2,1)S(1)}, u32[]{:S(2)}, u32[]{:S(2)}) collective-permute-start(bf16[1,128,256]{2,1,0:T(8,128)(2,1)S(1)} %get-tuple-element.24), channel_id=1, source_target_pairs={{0,1},{1,2},{2,3},{4,5},{5,6},{6,7},{8,9},{9,10},{10,11},{12,13},{... | collective-permute-start | bytes 196616 | tf_op jit(solution)/shard_map/ppermute | solution.py:226
  9.4 1.0 %copy-start.2 = (bf16[64,2048]{1,0:T(8,128)(2,1)S(1)}, bf16[64,2048]{1,0:T(8,128)(2,1)}, u32[]{:S(2)}) copy-start(bf16[64,2048]{1,0:T(8,128)(2,1)} %weights.1) | copy-start | bytes 786436
  10.3 0.7 %copy-start.3 = (s32[2048]{0:T(1024)S(1)}, s32[2048]{0:T(1024)}, u32[]{:S(2)}) copy-start(s32[2048]{0:T(1024)} %param.8) | copy-start | bytes 24580
  14.6 15.7 %collective-permute-start.2 = (bf16[256,256]{1,0:T(8,128)(2,1)S(1)}, bf16[256,256]{1,0:T(8,128)(2,1)S(1)}, u32[]{:S(2)}, u32[]{:S(2)}) collective-permute-start(bf16[256,256]{1,0:T(8,128)(2,1)S(1)} %focus_range.3), channel_id=1, source_target_pairs={{0,16},{4,20},{8,24},{12,28},{16,0},{20,4},{24,8},{28,12},{1,17},{... | collective-permute-start | bytes 393224 | tf_op jit(solution)/shard_map/ppermute | solution.py:243
  26.6 7.1 %collective-permute-start.6 = (bf16[256,256]{1,0:T(8,128)(2,1)S(1)}, bf16[256,256]{1,0:T(8,128)(2,1)S(1)}, u32[]{:S(2)}, u32[]{:S(2)}) collective-permute-start(bf16[256,256]{1,0:T(8,128)(2,1)S(1)} %get-tuple-element.33), channel_id=1, source_target_pairs={{0,4},{4,0},{8,12},{12,8},{16,20},{20,16},{24,28},{28,24},{1,5},{5... | collective-permute-start | bytes 393224 | tf_op jit(solution)/shard_map/ppermute | solution.py:243
  27.9 12.1 %collective-permute-start.3 = (bf16[256,256]{1,0:T(8,128)(2,1)S(1)}, bf16[256,256]{1,0:T(8,128)(2,1)S(1)}, u32[]{:S(2)}, u32[]{:S(2)}) collective-permute-start(bf16[256,256]{1,0:T(8,128)(2,1)S(1)} %get-tuple-element.29), channel_id=1, source_target_pairs={{0,20},{4,16},{8,28},{12,24},{16,4},{20,0},{24,12},{28,8},{1,21},{... | collective-permute-start | bytes 393224 | tf_op jit(solution)/shard_map/ppermute | solution.py:243
  27.9 6.6 %collective-permute-start.7 = (bf16[256,256]{1,0:T(8,128)(2,1)S(1)}, bf16[256,256]{1,0:T(8,128)(2,1)S(1)}, u32[]{:S(2)}, u32[]{:S(2)}) collective-permute-start(bf16[256,256]{1,0:T(8,128)(2,1)S(1)} %get-tuple-element.34), channel_id=1, source_target_pairs={{0,8},{4,12},{8,0},{12,4},{16,24},{20,28},{24,16},{28,20},{1,9},{5... | collective-permute-start | bytes 393224 | tf_op jit(solution)/shard_map/ppermute | solution.py:243
  29.2 10.8 %collective-permute-start.8 = (bf16[256,256]{1,0:T(8,128)(2,1)S(1)}, bf16[256,256]{1,0:T(8,128)(2,1)S(1)}, u32[]{:S(2)}, u32[]{:S(2)}) collective-permute-start(bf16[256,256]{1,0:T(8,128)(2,1)S(1)} %get-tuple-element.35), channel_id=1, source_target_pairs={{0,12},{4,8},{8,4},{12,0},{16,28},{20,24},{24,20},{28,16},{1,13},{... | collective-permute-start | bytes 393224 | tf_op jit(solution)/shard_map/ppermute | solution.py:243
  30.3 13.2 %collective-permute-start.4 = (bf16[256,256]{1,0:T(8,128)(2,1)S(1)}, bf16[256,256]{1,0:T(8,128)(2,1)S(1)}, u32[]{:S(2)}, u32[]{:S(2)}) collective-permute-start(bf16[256,256]{1,0:T(8,128)(2,1)S(1)} %get-tuple-element.30), channel_id=1, source_target_pairs={{0,24},{4,28},{8,16},{12,20},{16,8},{20,12},{24,0},{28,4},{1,25},{... | collective-permute-start | bytes 393224 | tf_op jit(solution)/shard_map/ppermute | solution.py:243
  33.6 13.4 %collective-permute-start.5 = (bf16[256,256]{1,0:T(8,128)(2,1)S(1)}, bf16[256,256]{1,0:T(8,128)(2,1)S(1)}, u32[]{:S(2)}, u32[]{:S(2)}) collective-permute-start(bf16[256,256]{1,0:T(8,128)(2,1)S(1)} %get-tuple-element.31), channel_id=1, source_target_pairs={{0,28},{4,24},{8,20},{12,16},{16,12},{20,8},{24,4},{28,0},{1,29},{... | collective-permute-start | bytes 393224 | tf_op jit(solution)/shard_map/ppermute | solution.py:243

commit v2 on v0

v2 whole, which is shorter than its diff:
```python
import functools

import jax
import jax.numpy as jnp
from jax import lax
from jax.experimental import pallas as pl
from jax.experimental.pallas import tpu as pltpu
from jax.sharding import PartitionSpec as P

RT = 1024
AT = 512
BAND = 64
BLK = 128
HALF = BLK // 2
WIDE = 2 * BLK
RANGE_TILES = RT // BLK + 2
AZ_TILES = AT // BLK + 1
HEAD = RT // BLK + 1
GROUP = 2 * BLK
LIMIT = 24 * 1024 * 1024

VMEM = functools.partial(pl.BlockSpec, memory_space=pltpu.VMEM)
SMEM = functools.partial(pl.BlockSpec, memory_space=pltpu.SMEM)
HBM = functools.partial(pl.BlockSpec, memory_space=pltpu.HBM)


def call(body, name, out_shape, in_specs, out_specs, scratch_shapes=()):
    return pl.pallas_call(
        body,
        out_shape=out_shape,
        in_specs=in_specs,
        out_specs=out_specs,
        scratch_shapes=scratch_shapes,
        compiler_params=pltpu.CompilerParams(vmem_limit_bytes=LIMIT),
        cost_estimate=pl.CostEstimate(flops=0, bytes_accessed=0, transcendentals=0),
        name=name,
    )


def bf16(*shape):
    return jax.ShapeDtypeStruct(shape, jnp.bfloat16)


def pack_body(place, echoes, near, far):
    odd = place[0] % 2 == 1

    def fill(down, up):
        for part in range(2):
            lanes = slice(part * BLK, (part + 1) * BLK)
            for block in range(HEAD):
                down[block, :, lanes] = echoes[part, :, block * BLK : (block + 1) * BLK]
            up[0, :, lanes] = echoes[part, :, echoes.shape[2] - BLK :]

    pl.when(odd)(lambda: fill(near, far))
    pl.when(jnp.logical_not(odd))(lambda: fill(far, near))


def pack(place, echoes):
    return call(
        pack_body,
        "pack",
        (bf16(HEAD, echoes.shape[1], WIDE),) * 2,
        [SMEM(), VMEM()],
        (VMEM(),) * 2,
    )(place, echoes)


def toeplitz_tiles(taps, tiles, shift, out):
    width = (tiles + 1) * BLK
    skewed = []
    for part in range(2):
        row = jnp.concatenate(
            [
                jnp.zeros((1, BLK), jnp.float32),
                taps[part : part + 1, :].astype(jnp.float32),
                jnp.zeros((1, width - BLK - taps.shape[1]), jnp.float32),
            ],
            axis=1,
        )
        row = jnp.broadcast_to(row, (BLK, width))
        skewed.append(pltpu.roll(row, shift, 1, stride=1, stride_axis=0))
    for tile in range(tiles):
        span = slice((tile + 1) * BLK, (tile + 2) * BLK)
        real = skewed[0][:, span].T
        imag = skewed[1][:, span].T
        out[tile, :BLK, :BLK] = real.astype(jnp.bfloat16)
        out[tile, :BLK, BLK:] = (-imag).astype(jnp.bfloat16)
        out[tile, BLK:, :BLK] = imag.astype(jnp.bfloat16)
        out[tile, BLK:, BLK:] = real.astype(jnp.bfloat16)


def prepare_body(place, range_taps, weights, offsets, range_out, band_out):
    toeplitz_tiles(range_taps, RANGE_TILES, HALF, range_out)
    bins = weights.shape[1]
    lane = lax.broadcasted_iota(jnp.int32, (BLK, WIDE), 1)
    for block in range(bins // BLK):
        span = slice(block * BLK, (block + 1) * BLK)
        placed = jnp.concatenate(
            [weights[:, span].astype(jnp.float32), jnp.zeros((BLK - BAND, BLK), jnp.float32)], axis=0
        )
        shifts = offsets[:, span]
        for bit in range((BAND // 2).bit_length()):
            chosen = jnp.broadcast_to((shifts >> bit) & 1, (BLK, BLK)) == 1
            placed = jnp.where(chosen, pltpu.roll(placed, 1 << bit, 0), placed)
        wide = jnp.concatenate([placed.T, jnp.zeros((BLK, BLK), jnp.float32)], axis=1)
        skewed = pltpu.roll(wide, BAND // 2, 1, stride=1, stride_axis=0)
        if block == 0:
            skewed = jnp.where((place[0] == 0) & (lane < HALF), 0.0, skewed)
        band_out[span, :] = skewed.astype(jnp.bfloat16)


def prepare(place, range_ref, weights, offsets):
    return call(
        prepare_body,
        "prepare",
        (bf16(RANGE_TILES, WIDE, WIDE), bf16(weights.shape[1], WIDE)),
        [SMEM()] + [VMEM()] * 3,
        (VMEM(),) * 2,
    )(place, range_ref, weights, offsets)


def assemble(place, echoes, near, far, out):
    blocks = echoes.shape[2] // BLK
    for block in range(blocks):
        for part in range(2):
            out[block + 1, :, part * BLK : (part + 1) * BLK] = echoes[
                part, :, block * BLK : (block + 1) * BLK
            ]

    def ends(low, high):
        out[0] = low[0]
        out[blocks + 1 :] = high[...]

    odd = place[0] % 2 == 1
    pl.when(odd)(lambda: ends(near, far))
    pl.when(jnp.logical_not(odd))(lambda: ends(far, near))


def spots(place, near, count, direct):
    me = place[1]
    if not direct:
        first = 0 if near else count
        return first, [first + i for i in range(count)]
    side = me // count if near else 1 - me // count
    return side * count, [side * count + (me % count ^ i) for i in range(count)]


def focus_range(first, groups, samples, range_tiles, bands, turned, outs):
    pulses = samples.shape[1]
    count = len(outs)
    for block in range(2 * count + 1):
        window = jnp.concatenate(
            [samples[2 * first + block + tile] for tile in range(RANGE_TILES)], axis=1
        )
        total = jnp.dot(
            window,
            range_tiles[...].reshape(RANGE_TILES * WIDE, WIDE),
            preferred_element_type=jnp.float32,
        ).astype(jnp.bfloat16)
        turned[block * BLK : (block + 1) * BLK, :] = jnp.concatenate(
            [total[:, :BLK].T, total[:, BLK:].T], axis=1
        )
    for place, out in enumerate(outs):
        group = groups[place]
        for half in range(2):
            reach = pl.multiple_of((group - first) * GROUP + half * BLK, BLK)
            start = pl.multiple_of(group * GROUP + half * BLK, BLK)
            out[half * BLK : (half + 1) * BLK, :] = jnp.dot(
                bands[pl.ds(start, BLK)],
                turned[pl.ds(reach, WIDE)],
                preferred_element_type=jnp.float32,
            ).astype(jnp.bfloat16)


def first_range_body(direct, place, echoes, near, far, range_tiles, bands, samples, *rest):
    outs, turned = rest[:-1], rest[-1]
    assemble(place, echoes, near, far, samples)
    first, groups = spots(place, not direct, len(outs), direct)
    focus_range(first, groups, samples, range_tiles, bands, turned, outs)


def second_range_body(
    direct, place, after, samples, range_tiles, bands, az_taps, az_out, *rest
):
    outs, turned = rest[:-1], rest[-1]
    toeplitz_tiles(az_taps, AZ_TILES, 0, az_out)
    first, groups = spots(place, direct, len(outs), direct)
    focus_range(first, groups, samples, range_tiles, bands, turned, outs)


def first_range(direct, place, echoes, near, far, range_tiles, bands):
    pulses = echoes.shape[1]
    count = echoes.shape[2] // GROUP // 2
    blocks = 1 + echoes.shape[2] // BLK + HEAD
    samples, *made = call(
        functools.partial(first_range_body, direct),
        "first_range",
        (bf16(blocks, pulses, WIDE),) + (bf16(GROUP, 2 * pulses),) * count,
        [SMEM()] + [VMEM()] * 5,
        (VMEM(),) * (1 + count),
        [pltpu.VMEM(((2 * count + 1) * BLK, 2 * pulses), jnp.bfloat16)],
    )(place, echoes, near, far, range_tiles, bands)
    return samples, made


def second_range(direct, place, after, samples, range_tiles, bands, azimuth_ref):
    pulses = samples.shape[1]
    count = bands.shape[0] // GROUP // 2
    az_tiles, *made = call(
        functools.partial(second_range_body, direct),
        "second_range",
        (bf16(AZ_TILES, WIDE, WIDE),) + (bf16(GROUP, 2 * pulses),) * count,
        [SMEM()] + [VMEM()] * 5,
        (VMEM(),) * (1 + count),
        [pltpu.VMEM(((2 * count + 1) * BLK, 2 * pulses), jnp.bfloat16)],
    )(place, after, samples, range_tiles, bands, azimuth_ref)
    return az_tiles, made


def focus_azimuth_body(direct, place, az_tiles, *rest):
    parts, out, rows, image, sems = rest[:-4], rest[-4], rest[-3], rest[-2], rest[-1]
    count = len(parts)
    where = range(count)
    if direct:
        where = [
            group for near in (False, True) for group in spots(place, near, count // 2, True)[1]
        ]
    bins = parts[0].shape[0]
    reach = AZ_TILES // 2
    for place, part in enumerate(parts):
        start = pl.multiple_of(where[place] * bins, bins)
        rows[pl.ds(start, bins)] = part[...]
    for block in range(count):
        low, high = max(0, reach - block), min(AZ_TILES, count + reach - block)
        window = jnp.concatenate(
            [
                rows[(block + tile - reach) * bins : (block + tile - reach + 1) * bins]
                for tile in range(low, high)
            ],
            axis=1,
        )
        total = jnp.dot(
            window,
            az_tiles[low:high].reshape((high - low) * WIDE, WIDE),
            preferred_element_type=jnp.float32,
        )
        span = pl.ds(block * BLK, BLK)
        for part in range(2):
            image[part, 0, :, span] = total[:, part * BLK : (part + 1) * BLK]
        pltpu.make_async_copy(
            image.at[:, :, :, span], out.at[:, :, :, span], sems.at[block]
        ).start()
    for block in range(count):
        span = pl.ds(block * BLK, BLK)
        pltpu.make_async_copy(
            image.at[:, :, :, span], out.at[:, :, :, span], sems.at[block]
        ).wait()


def focus_azimuth(direct, place, az_tiles, parts):
    count = len(parts)
    bins = parts[0].shape[0]
    shape = (2, 1, bins, count * BLK)
    return call(
        functools.partial(focus_azimuth_body, direct),
        "focus_azimuth",
        jax.ShapeDtypeStruct(shape, jnp.float32),
        [SMEM()] + [VMEM()] * (1 + count),
        HBM(),
        [
            pltpu.VMEM((count * bins, WIDE), jnp.bfloat16),
            pltpu.VMEM(shape, jnp.float32),
            pltpu.SemaphoreType.DMA((count,)),
        ],
    )(place, az_tiles, *parts)


def per_device(echoes, range_ref, band_weights, band_offsets, azimuth_ref):
    quarter_len = echoes.shape[2]
    peers = lax.axis_size("pulse")
    quarters = lax.axis_size("rng")
    bins = quarter_len // peers
    place = jnp.stack([lax.axis_index("rng"), lax.axis_index("pulse")]).astype(jnp.int32)

    near, far = pack(place, echoes)

    def swaps(start):
        pairs = [(i, i + 1) for i in range(start, quarters - 1, 2)]
        return pairs + [(j, i) for i, j in pairs]

    far = lax.ppermute(far, "rng", swaps(1))
    near = lax.ppermute(near, "rng", swaps(0))
    range_tiles, bands = prepare(
        place, range_ref, band_weights, band_offsets.reshape(1, quarter_len)
    )

    direct = bins == GROUP and peers & (peers - 1) == 0

    def send(pieces, start):
        return [
            lax.ppermute(piece, "pulse", [(i, i ^ k) for i in range(peers)]) if k else piece
            for k, piece in enumerate(pieces, start)
        ]

    samples, first = first_range(direct, place, echoes, near, far, range_tiles, bands)
    if direct:
        first = send(first, peers // 2)
    az_tiles, second = second_range(
        direct, place, first[0], samples, range_tiles, bands, azimuth_ref
    )
    if direct:
        return focus_azimuth(direct, place, az_tiles, first + send(second, 0))
    swapped = lax.all_to_all(
        jnp.concatenate(first + second, axis=0).reshape(peers, bins, WIDE),
        "pulse",
        split_axis=0,
        concat_axis=0,
        tiled=True,
    )
    return focus_azimuth(direct, place, az_tiles, [swapped[i] for i in range(peers)])


def solution(mesh):
    return jax.shard_map(
        per_device,
        mesh=mesh,
        in_specs=(P(None, "pulse", "rng"), P(), P(None, "rng"), P("rng"), P()),
        out_specs=P(None, "rng", "pulse", None),
        check_vma=False,
    )
```

time: 140 us -> 45.1 us (0.32)
  local copies, waits for them, and re-layouts: 50.2 us -> 3.56 us
  matrix products: 44.1 us -> 0 us
  Pallas kernels: 0 us -> 11.2 us
  waiting for transfers between devices: 26.2 us -> 15.3 us
  other arithmetic: 5.24 us -> 0.07 us
  starting transfers between devices: 13.1 us -> 14.6 us
    dot_general x16 -> x0, matrix products: 44.1 us -> none  [the longest x14 43.3 us: correlate(): jnp.einsum('zrbi,ziwc->wrbc', window, kernel[tap_block], preferred_elemen...]
    unnamed x34 -> x12, local copies, waits for them, and re-layouts: 31.6 us -> 3.56 us
    all_to_all x1 -> x0, waiting for transfers between devices: 24.1 us -> none  [per_device(): lax.all_to_all(grouped, 'pulse', split_axis=1, concat_axis=3, tiled=True)]
    ppermute x3 -> x9, waiting for transfers between devices: 2.09 us -> 15.3 us  [the longest x7 12 us: send(): lax.ppermute(piece, 'pulse', [(i, i ^ k) for i in range(peers)])]
    pallas_call x0 -> x5, Pallas kernels: none -> 11.2 us  [the longest x1 3.08 us: first_range(): call(functools.partial(first_range_body, direct), 'first_range', (bf16(bl...]
    slice x9 -> x0, local copies, waits for them, and re-layouts: 7.24 us -> none  [the longest x2 5.04 us: correlate(): window = blocks[:, :, tap_block:tap_block + out_blocks]]
    ppermute x3 -> x9, starting transfers between devices: 7.52 us -> 14.6 us  [the longest x7 10 us: send(): lax.ppermute(piece, 'pulse', [(i, i ^ k) for i in range(peers)])]
    all_to_all x1 -> x0, starting transfers between devices: 5.56 us -> none  [per_device(): lax.all_to_all(grouped, 'pulse', split_axis=1, concat_axis=3, tiled=True)]
  transfers between devices with their start and end apart: 4 -> 9, of which waited for: 2 -> 4; matrix products, arithmetic and copies ran while one was open for 9% -> 0% of each run, Pallas kernels for 0% -> 10%
where the time goes in v2:
time: 45.1 us; the launch traced here: 44.9 us
  waiting for transfers between devices  15.3 us (34%)
  starting transfers between devices  14.6 us (32%)
  Pallas kernels  11.2 us (25%)
  local copies, waits for them, and re-layouts  3.56 us (8%)
    ppermute x7, waiting for transfers between devices, send(): lax.ppermute(piece, 'pulse', [(i, i ^ k) for i in range(peers)])  12 us
    ppermute x7, starting transfers between devices, send(): lax.ppermute(piece, 'pulse', [(i, i ^ k) for i in range(peers)])  10 us
    ppermute x1, starting transfers between devices, per_device(): far = lax.ppermute(far, 'rng', swaps(1))  4.47 us
    unnamed x12, local copies, waits for them, and re-layouts  3.56 us
    ppermute x1, waiting for transfers between devices, per_device(): far = lax.ppermute(far, 'rng', swaps(1))  3.38 us
    pallas_call x1, Pallas kernels, first_range(): call(functools.partial(first_range_body, direct), 'first_range', (bf16(bl...  3.08 us
    pallas_call x1, Pallas kernels, second_range(): call(functools.partial(second_range_body, direct), 'second_range', (bf16(...  2.85 us
    pallas_call x1, Pallas kernels, focus_azimuth(): call(functools.partial(focus_azimuth_body, direct), 'focus_azimuth', jax....  2.78 us
  transfers between devices with their start and end apart: 9, of which 4 were waited for; matrix products, arithmetic and copies ran while one was open for 0% of the time, Pallas kernels for 10%

profile of v2, /device:TPU:1, one launch (start us, length us, event | category | flops | bytes accessed | tf_op | source)
XLA Modules:
  0.0 44.9 jit_solution(9723964945496216960)
XLA Ops:
  0.0 0.1 pad_add_fusion.place
  0.1 0.0 copy-start
  0.1 1.2 %copy-done = bf16[2,128,2048]{2,1,0:T(8,128)(2,1)S(1)} copy-done((bf16[2,128,2048]{2,1,0:T(8,128)(2,1)S(1)}, bf16[2,128,2048]{2,1,0:T(8,128)(2,1)}, u32[]{:S(2)}) %copy-start) | copy-done | bytes 1048600
  1.3 0.0 copy-start.1
  1.3 0.7 %pack.1 = (bf16[9,128,256]{2,1,0:T(8,128)(2,1)S(1)}, bf16[9,128,256]{2,1,0:T(8,128)(2,1)S(1)}) custom-call(s32[2]{0:T(128)S(1)} %pad_add_fusion.place, bf16[2,128,2048]{2,1,0:T(8,128)(2,1)S(1)} %copy-done), custom_call_target="tpu_custom_call" | custom-call | tf_op jit(solution)/shard_map/pack/pallas_call | solution.py:59
  2.0 0.1 collective-permute-start
  2.1 4.5 %collective-permute-start.1 = (bf16[9,128,256]{2,1,0:T(8,128)(2,1)S(1)}, bf16[9,128,256]{2,1,0:T(8,128)(2,1)S(1)}, u32[]{:S(2)}, u32[]{:S(2)}) collective-permute-start(bf16[9,128,256]{2,1,0:T(8,128)(2,1)S(1)} %get-tuple-element.20), channel_id=1, source_target_pairs={{1,2},{2,1},{5,6},{6,5},{9,10},{10,9},{13,14},{14,13},{17,18},{18,... | collective-permute-start | bytes 1769480 | tf_op jit(solution)/shard_map/ppermute | solution.py:291
  6.6 0.0 copy-start.2
  6.6 0.9 %copy-done.2 = bf16[64,2048]{1,0:T(8,128)(2,1)S(1)} copy-done((bf16[64,2048]{1,0:T(8,128)(2,1)S(1)}, bf16[64,2048]{1,0:T(8,128)(2,1)}, u32[]{:S(2)}) %copy-start.2) | copy-done | bytes 262168
  7.5 0.0 copy-start.3
  7.5 0.7 %copy-done.3 = s32[2048]{0:T(1024)S(1)} copy-done((s32[2048]{0:T(1024)S(1)}, s32[2048]{0:T(1024)}, u32[]{:S(2)}) %copy-start.3) | copy-done | bytes 8216
  8.2 0.0 copy-start.4
  8.2 0.7 %copy-done.4 = bf16[2,1024]{1,0:T(2,128)(2,1)S(1)} copy-done((bf16[2,1024]{1,0:T(2,128)(2,1)S(1)}, bf16[2,1024]{1,0:T(2,128)(2,1)}, u32[]{:S(2)}) %copy-start.4) | copy-done | bytes 4120
  8.9 1.8 %prepare.1 = (bf16[10,256,256]{2,1,0:T(8,128)(2,1)S(1)}, bf16[2048,256]{1,0:T(8,128)(2,1)S(1)}) custom-call(s32[2]{0:T(128)S(1)} %pad_add_fusion.place, bf16[2,1024]{1,0:T(2,128)(2,1)S(1)} %copy-done.4, bf16[64,2048]{1,0:T(8,128)(2,1)S(1)} %copy-done.2, s32[1,2048]{1,0:T(1,128)S(1)} %bitcast.3), custom_call_target="tpu_custom_call" | custom-call | tf_op jit(solution)/shard_map/prepare/pallas_call | solution.py:113
  10.7 0.0 collective-permute-done.near
  10.7 3.4 %collective-permute-done.1.far = bf16[9,128,256]{2,1,0:T(8,128)(2,1)S(1)} collective-permute-done((bf16[9,128,256]{2,1,0:T(8,128)(2,1)S(1)}, bf16[9,128,256]{2,1,0:T(8,128)(2,1)S(1)}, u32[]{:S(2)}, u32[]{:S(2)}) %collective-permute-start.1) | collective-permute-done | bytes 589856 | tf_op jit(solution)/shard_map/ppermute | solution.py:291
  14.1 0.0 copy-done.1
  14.1 0.0 copy-start.5
  14.1 3.1 %first_range.1 = (bf16[26,128,256]{2,1,0:T(8,128)(2,1)S(1)}, bf16[256,256]{1,0:T(8,128)(2,1)S(1)}, bf16[256,256]{1,0:T(8,128)(2,1)S(1)}, bf16[256,256]{1,0:T(8,128)(2,1)S(1)}, bf16[256,256]{1,0:T(8,128)(2,1)S(1)}) custom-call(s32[2]{0:T(128)S(1)} %pad_add_fusion.place, bf16[2,128,2048]{2,1,0:T(8,128)(2,1)S(1)} %copy-done.1, ...), custom_call_target="tpu_custom_call" | custom-call | tf_op jit(solution)/shard_map/first_range/pallas_call | solution.py:195
  17.2 3.0 %collective-permute-start.2 = (bf16[256,256]{1,0:T(8,128)(2,1)S(1)}, bf16[256,256]{1,0:T(8,128)(2,1)S(1)}, u32[]{:S(2)}, u32[]{:S(2)}) collective-permute-start(bf16[256,256]{1,0:T(8,128)(2,1)S(1)} %get-tuple-element.23), channel_id=1, source_target_pairs={{0,16},{4,20},{8,24},{12,28},{16,0},{20,4},{24,8},{28,12},{1,17},{... | collective-permute-start | bytes 393224 | tf_op jit(solution)/shard_map/ppermute | solution.py:301
  20.2 1.0 %collective-permute-start.3 = (bf16[256,256]{1,0:T(8,128)(2,1)S(1)}, bf16[256,256]{1,0:T(8,128)(2,1)S(1)}, u32[]{:S(2)}, u32[]{:S(2)}) collective-permute-start(bf16[256,256]{1,0:T(8,128)(2,1)S(1)} %get-tuple-element.26), channel_id=1, source_target_pairs={{0,20},{4,16},{8,28},{12,24},{16,4},{20,0},{24,12},{28,8},{1,21},{... | collective-permute-start | bytes 393224 | tf_op jit(solution)/shard_map/ppermute | solution.py:301
  21.2 3.3 %collective-permute-start.4 = (bf16[256,256]{1,0:T(8,128)(2,1)S(1)}, bf16[256,256]{1,0:T(8,128)(2,1)S(1)}, u32[]{:S(2)}, u32[]{:S(2)}) collective-permute-start(bf16[256,256]{1,0:T(8,128)(2,1)S(1)} %get-tuple-element.27), channel_id=1, source_target_pairs={{0,24},{4,28},{8,16},{12,20},{16,8},{20,12},{24,0},{28,4},{1,25},{... | collective-permute-start | bytes 393224 | tf_op jit(solution)/shard_map/ppermute | solution.py:301
  24.5 0.0 collective-permute-start.5
  24.5 8.2 %collective-permute-done.2.after.rest_0_ = bf16[256,256]{1,0:T(8,128)(2,1)S(1)} collective-permute-done((bf16[256,256]{1,0:T(8,128)(2,1)S(1)}, bf16[256,256]{1,0:T(8,128)(2,1)S(1)}, u32[]{:S(2)}, u32[]{:S(2)}) %collective-permute-start.2) | collective-permute-done | bytes 131104 | tf_op jit(solution)/shard_map/ppermute | solution.py:301
  32.8 0.0 copy-done.5
  32.8 2.8 %second_range.1 = (bf16[5,256,256]{2,1,0:T(8,128)(2,1)S(1)}, bf16[256,256]{1,0:T(8,128)(2,1)S(1)}, bf16[256,256]{1,0:T(8,128)(2,1)S(1)}, bf16[256,256]{1,0:T(8,128)(2,1)S(1)}, bf16[256,256]{1,0:T(8,128)(2,1)S(1)}) custom-call(s32[2]{0:T(128)S(1)} %pad_add_fusion.place, bf16[256,256]{1,0:T(8,128)(2,1)S(1)} %collective-permute-done.2.after.rest_0_, ...), custom_call_target="tpu_custom_call" | custom-call | tf_op jit(solution)/shard_map/second_range/pallas_call | solution.py:209
  35.6 0.3 collective-permute-start.6
  35.9 0.0 collective-permute-start.7
  35.9 0.0 collective-permute-done.3.rest_1_
  35.9 2.4 %collective-permute-start.8 = (bf16[256,256]{1,0:T(8,128)(2,1)S(1)}, bf16[256,256]{1,0:T(8,128)(2,1)S(1)}, u32[]{:S(2)}, u32[]{:S(2)}) collective-permute-start(bf16[256,256]{1,0:T(8,128)(2,1)S(1)} %get-tuple-element.32), channel_id=1, source_target_pairs={{0,12},{4,8},{8,4},{12,0},{16,28},{20,24},{24,20},{28,16},{1,13},{... | collective-permute-start | bytes 393224 | tf_op jit(solution)/shard_map/ppermute | solution.py:301
  38.3 0.0 collective-permute-done.4.rest_2_
  38.3 0.0 collective-permute-done.5.rest_3_
  38.3 2.1 %collective-permute-done.6.rest_5_ = bf16[256,256]{1,0:T(8,128)(2,1)S(1)} collective-permute-done((bf16[256,256]{1,0:T(8,128)(2,1)S(1)}, bf16[256,256]{1,0:T(8,128)(2,1)S(1)}, u32[]{:S(2)}, u32[]{:S(2)}) %collective-permute-start.6) | collective-permute-done | bytes 131104 | tf_op jit(solution)/shard_map/ppermute | solution.py:301
  40.5 0.0 collective-permute-done.7.rest_6_
  40.5 1.6 %collective-permute-done.8.rest_7_ = bf16[256,256]{1,0:T(8,128)(2,1)S(1)} collective-permute-done((bf16[256,256]{1,0:T(8,128)(2,1)S(1)}, bf16[256,256]{1,0:T(8,128)(2,1)S(1)}, u32[]{:S(2)}, u32[]{:S(2)}) %collective-permute-start.8) | collective-permute-done | bytes 131104 | tf_op jit(solution)/shard_map/ppermute | solution.py:301
  42.1 2.8 %focus_azimuth.1 = f32[2,1,256,1024]{3,2,1,0:T(8,128)} custom-call(s32[2]{0:T(128)S(1)} %pad_add_fusion.place, bf16[5,256,256]{2,1,0:T(8,128)(2,1)S(1)} %get-tuple-element.25.az_tiles, bf16[256,256]{1,0:T(8,128)(2,1)S(1)} %collective-permute-done.2.after.rest_0_, bf16[256,256]{1,0:T(8,128)(2,1)S(1)} %collective-permute-done.3.rest_1_, ...), custom_call_target="tpu_custom_call" | custom-call | tf_op jit(solution)/shard_map/focus_azimuth/pallas_call | solution.py:264
Async XLA Ops:
  0.1 1.2 %copy-start = (bf16[2,128,2048]{2,1,0:T(8,128)(2,1)S(1)}, bf16[2,128,2048]{2,1,0:T(8,128)(2,1)}, u32[]{:S(2)}) copy-start(bf16[2,128,2048]{2,1,0:T(8,128)(2,1)} %echoes.3) | copy-start | bytes 3145732
  1.3 12.8 %copy-start.1 = (bf16[2,128,2048]{2,1,0:T(8,128)(2,1)S(1)}, bf16[2,128,2048]{2,1,0:T(8,128)(2,1)}, u32[]{:S(2)}) copy-start(bf16[2,128,2048]{2,1,0:T(8,128)(2,1)} %echoes.3) | copy-start | bytes 3145732
  2.0 8.8 %collective-permute-start = (bf16[9,128,256]{2,1,0:T(8,128)(2,1)S(1)}, bf16[9,128,256]{2,1,0:T(8,128)(2,1)S(1)}, u32[]{:S(2)}, u32[]{:S(2)}) collective-permute-start(bf16[9,128,256]{2,1,0:T(8,128)(2,1)S(1)} %get-tuple-element.19), channel_id=1, source_target_pairs={{0,1},{2,3},{1,0},{3,2},{4,5},{6,7},{5,4},{7,6},{8,9},{10,11},{9,8... | collective-permute-start | bytes 1769480 | tf_op jit(solution)/shard_map/ppermute | solution.py:292
  2.1 12.0 %collective-permute-start.1 = (bf16[9,128,256]{2,1,0:T(8,128)(2,1)S(1)}, bf16[9,128,256]{2,1,0:T(8,128)(2,1)S(1)}, u32[]{:S(2)}, u32[]{:S(2)}) collective-permute-start(bf16[9,128,256]{2,1,0:T(8,128)(2,1)S(1)} %get-tuple-element.20), channel_id=1, source_target_pairs={{1,2},{2,1},{5,6},{6,5},{9,10},{10,9},{13,14},{14,13},{17,18},{18,... | collective-permute-start | bytes 1769480 | tf_op jit(solution)/shard_map/ppermute | solution.py:291
  6.6 1.0 %copy-start.2 = (bf16[64,2048]{1,0:T(8,128)(2,1)S(1)}, bf16[64,2048]{1,0:T(8,128)(2,1)}, u32[]{:S(2)}) copy-start(bf16[64,2048]{1,0:T(8,128)(2,1)} %weights.1) | copy-start | bytes 786436
  7.5 0.7 %copy-start.3 = (s32[2048]{0:T(1024)S(1)}, s32[2048]{0:T(1024)}, u32[]{:S(2)}) copy-start(s32[2048]{0:T(1024)} %param.8) | copy-start | bytes 24580
  8.2 0.7 %copy-start.4 = (bf16[2,1024]{1,0:T(2,128)(2,1)S(1)}, bf16[2,1024]{1,0:T(2,128)(2,1)}, u32[]{:S(2)}) copy-start(bf16[2,1024]{1,0:T(2,128)(2,1)} %range_taps.1) | copy-start | bytes 12292
  14.1 18.6 %copy-start.5 = (bf16[2,512]{1,0:T(2,128)(2,1)S(1)}, bf16[2,512]{1,0:T(2,128)(2,1)}, u32[]{:S(2)}) copy-start(bf16[2,512]{1,0:T(2,128)(2,1)} %az_taps.1) | copy-start | bytes 6148
  17.2 15.5 %collective-permute-start.2 = (bf16[256,256]{1,0:T(8,128)(2,1)S(1)}, bf16[256,256]{1,0:T(8,128)(2,1)S(1)}, u32[]{:S(2)}, u32[]{:S(2)}) collective-permute-start(bf16[256,256]{1,0:T(8,128)(2,1)S(1)} %get-tuple-element.23), channel_id=1, source_target_pairs={{0,16},{4,20},{8,24},{12,28},{16,0},{20,4},{24,8},{28,12},{1,17},{... | collective-permute-start | bytes 393224 | tf_op jit(solution)/shard_map/ppermute | solution.py:301
  20.2 15.7 %collective-permute-start.3 = (bf16[256,256]{1,0:T(8,128)(2,1)S(1)}, bf16[256,256]{1,0:T(8,128)(2,1)S(1)}, u32[]{:S(2)}, u32[]{:S(2)}) collective-permute-start(bf16[256,256]{1,0:T(8,128)(2,1)S(1)} %get-tuple-element.26), channel_id=1, source_target_pairs={{0,20},{4,16},{8,28},{12,24},{16,4},{20,0},{24,12},{28,8},{1,21},{... | collective-permute-start | bytes 393224 | tf_op jit(solution)/shard_map/ppermute | solution.py:301
  21.2 17.1 %collective-permute-start.4 = (bf16[256,256]{1,0:T(8,128)(2,1)S(1)}, bf16[256,256]{1,0:T(8,128)(2,1)S(1)}, u32[]{:S(2)}, u32[]{:S(2)}) collective-permute-start(bf16[256,256]{1,0:T(8,128)(2,1)S(1)} %get-tuple-element.27), channel_id=1, source_target_pairs={{0,24},{4,28},{8,16},{12,20},{16,8},{20,12},{24,0},{28,4},{1,25},{... | collective-permute-start | bytes 393224 | tf_op jit(solution)/shard_map/ppermute | solution.py:301
  24.5 13.8 %collective-permute-start.5 = (bf16[256,256]{1,0:T(8,128)(2,1)S(1)}, bf16[256,256]{1,0:T(8,128)(2,1)S(1)}, u32[]{:S(2)}, u32[]{:S(2)}) collective-permute-start(bf16[256,256]{1,0:T(8,128)(2,1)S(1)} %get-tuple-element.28), channel_id=1, source_target_pairs={{0,28},{4,24},{8,20},{12,16},{16,12},{20,8},{24,4},{28,0},{1,29},{... | collective-permute-start | bytes 393224 | tf_op jit(solution)/shard_map/ppermute | solution.py:301
  35.6 4.8 %collective-permute-start.6 = (bf16[256,256]{1,0:T(8,128)(2,1)S(1)}, bf16[256,256]{1,0:T(8,128)(2,1)S(1)}, u32[]{:S(2)}, u32[]{:S(2)}) collective-permute-start(bf16[256,256]{1,0:T(8,128)(2,1)S(1)} %get-tuple-element.30), channel_id=1, source_target_pairs={{0,4},{4,0},{8,12},{12,8},{16,20},{20,16},{24,28},{28,24},{1,5},{5... | collective-permute-start | bytes 393224 | tf_op jit(solution)/shard_map/ppermute | solution.py:301
  35.9 4.6 %collective-permute-start.7 = (bf16[256,256]{1,0:T(8,128)(2,1)S(1)}, bf16[256,256]{1,0:T(8,128)(2,1)S(1)}, u32[]{:S(2)}, u32[]{:S(2)}) collective-permute-start(bf16[256,256]{1,0:T(8,128)(2,1)S(1)} %get-tuple-element.31), channel_id=1, source_target_pairs={{0,8},{4,12},{8,0},{12,4},{16,24},{20,28},{24,16},{28,20},{1,9},{5... | collective-permute-start | bytes 393224 | tf_op jit(solution)/shard_map/ppermute | solution.py:301
  35.9 6.2 %collective-permute-start.8 = (bf16[256,256]{1,0:T(8,128)(2,1)S(1)}, bf16[256,256]{1,0:T(8,128)(2,1)S(1)}, u32[]{:S(2)}, u32[]{:S(2)}) collective-permute-start(bf16[256,256]{1,0:T(8,128)(2,1)S(1)} %get-tuple-element.32), channel_id=1, source_target_pairs={{0,12},{4,8},{8,4},{12,0},{16,28},{20,24},{24,20},{28,16},{1,13},{... | collective-permute-start | bytes 393224 | tf_op jit(solution)/shard_map/ppermute | solution.py:301

commit v3 on v2

v3 whole, which is shorter than its diff:
```python
import functools

import jax
import jax.numpy as jnp
from jax import lax
from jax.experimental import pallas as pl
from jax.experimental.pallas import tpu as pltpu
from jax.sharding import PartitionSpec as P

RT = 1024
AT = 512
BAND = 64
BLK = 128
HALF = BLK // 2
WIDE = 2 * BLK
RANGE_TILES = RT // BLK + 2
AZ_TILES = AT // BLK + 1
HEAD = RT // BLK + 1
GROUP = 2 * BLK
LIMIT = 24 * 1024 * 1024

VMEM = functools.partial(pl.BlockSpec, memory_space=pltpu.VMEM)
HBM = functools.partial(pl.BlockSpec, memory_space=pltpu.HBM)


def call(body, name, out_shape, in_specs, out_specs, scratch_shapes=()):
    return pl.pallas_call(
        body,
        out_shape=out_shape,
        in_specs=in_specs,
        out_specs=out_specs,
        scratch_shapes=scratch_shapes,
        compiler_params=pltpu.CompilerParams(vmem_limit_bytes=LIMIT),
        cost_estimate=pl.CostEstimate(flops=0, bytes_accessed=0, transcendentals=0),
        name=name,
    )


def bf16(*shape):
    return jax.ShapeDtypeStruct(shape, jnp.bfloat16)


def pack_body(echoes, near, far):
    odd = lax.axis_index("rng") % 2 == 1

    def fill(down, up):
        for part in range(2):
            lanes = slice(part * BLK, (part + 1) * BLK)
            for block in range(HEAD):
                down[block, :, lanes] = echoes[part, :, block * BLK : (block + 1) * BLK]
            up[0, :, lanes] = echoes[part, :, echoes.shape[2] - BLK :]

    pl.when(odd)(lambda: fill(near, far))
    pl.when(jnp.logical_not(odd))(lambda: fill(far, near))


def pack(echoes):
    return call(
        pack_body,
        "pack",
        (bf16(HEAD, echoes.shape[1], WIDE),) * 2,
        [VMEM()],
        (VMEM(),) * 2,
    )(echoes)


OFFSET_ROW = BAND
RANGE_ROW = BAND + 8
AZ_ROW = BAND + 16
TABLE_ROWS = BAND + 24


def join_small(weights, offsets, range_ref, azimuth_ref):
    bins = weights.shape[1]

    def rows(value):
        return jnp.pad(value, ((0, 8 - value.shape[0]), (0, bins - value.shape[1])))

    return jnp.concatenate(
        [weights, rows(offsets.astype(jnp.bfloat16)[None]), rows(range_ref), rows(azimuth_ref)],
        axis=0,
    )


def toeplitz_tiles(table, start, tap_total, tiles, shift, out):
    width = (tiles + 1) * BLK
    skewed = []
    for part in range(2):
        row = jnp.concatenate(
            [
                jnp.zeros((1, BLK), jnp.float32),
                table[start : start + 8, :tap_total].astype(jnp.float32)[part : part + 1],
                jnp.zeros((1, width - BLK - tap_total), jnp.float32),
            ],
            axis=1,
        )
        row = jnp.broadcast_to(row, (BLK, width))
        skewed.append(pltpu.roll(row, shift, 1, stride=1, stride_axis=0))
    for tile in range(tiles):
        span = slice((tile + 1) * BLK, (tile + 2) * BLK)
        real = skewed[0][:, span].T
        imag = skewed[1][:, span].T
        out[tile, :BLK, :BLK] = real.astype(jnp.bfloat16)
        out[tile, :BLK, BLK:] = (-imag).astype(jnp.bfloat16)
        out[tile, BLK:, :BLK] = imag.astype(jnp.bfloat16)
        out[tile, BLK:, BLK:] = real.astype(jnp.bfloat16)


def prepare_body(table, range_out, band_out):
    toeplitz_tiles(table, RANGE_ROW, RT, RANGE_TILES, HALF, range_out)
    lowest = lax.axis_index("rng") == 0
    lane = lax.broadcasted_iota(jnp.int32, (BLK, WIDE), 1)
    for block in range(table.shape[1] // BLK):
        span = slice(block * BLK, (block + 1) * BLK)
        placed = jnp.concatenate(
            [
                table[:BAND, span].astype(jnp.float32),
                jnp.zeros((BLK - BAND, BLK), jnp.float32),
            ],
            axis=0,
        )
        shifts = table[OFFSET_ROW : OFFSET_ROW + 8, span].astype(jnp.float32).astype(jnp.int32)[:1]
        for bit in range((BAND // 2).bit_length()):
            chosen = jnp.broadcast_to((shifts >> bit) & 1, (BLK, BLK)) == 1
            placed = jnp.where(chosen, pltpu.roll(placed, 1 << bit, 0), placed)
        wide = jnp.concatenate([placed.T, jnp.zeros((BLK, BLK), jnp.float32)], axis=1)
        skewed = pltpu.roll(wide, BAND // 2, 1, stride=1, stride_axis=0)
        if block == 0:
            skewed = jnp.where(lowest & (lane < HALF), 0.0, skewed)
        band_out[span, :] = skewed.astype(jnp.bfloat16)


def prepare(table):
    return call(
        prepare_body,
        "prepare",
        (bf16(RANGE_TILES, WIDE, WIDE), bf16(table.shape[1], WIDE)),
        [VMEM()],
        (VMEM(),) * 2,
    )(table)


def assemble(echoes, near, far, out):
    blocks = echoes.shape[2] // BLK
    for block in range(blocks):
        for part in range(2):
            out[block + 1, :, part * BLK : (part + 1) * BLK] = echoes[
                part, :, block * BLK : (block + 1) * BLK
            ]

    def ends(low, high):
        out[0] = low[0]
        out[blocks + 1 :] = high[...]

    odd = lax.axis_index("rng") % 2 == 1
    pl.when(odd)(lambda: ends(near, far))
    pl.when(jnp.logical_not(odd))(lambda: ends(far, near))


def compress(samples, range_tiles, block):
    window = jnp.concatenate([samples[block + tile] for tile in range(RANGE_TILES)], axis=1)
    total = jnp.dot(
        window,
        range_tiles[...].reshape(RANGE_TILES * WIDE, WIDE),
        preferred_element_type=jnp.float32,
    ).astype(jnp.bfloat16)
    return jnp.concatenate([total[:, :BLK].T, total[:, BLK:].T], axis=1)


def migrate(bands, turned, first, place):
    reach = pl.multiple_of(place * BLK, BLK)
    start = pl.multiple_of((first + place) * BLK, BLK)
    return jnp.dot(
        bands[pl.ds(start, BLK)], turned[pl.ds(reach, WIDE)], preferred_element_type=jnp.float32
    ).astype(jnp.bfloat16)


def groups_of(first, count, spots, samples, range_tiles, bands, turned, outs):
    for block in range(count + 1):
        turned[block * BLK : (block + 1) * BLK, :] = compress(samples, range_tiles, first + block)
    for spot, out in zip(spots, outs):
        for block in range(GROUP // BLK):
            out[block * BLK : (block + 1) * BLK, :] = migrate(
                bands, turned, first, spot * (GROUP // BLK) + block
            )


def far_pair(step, samples, range_tiles, bands, turned, outs):
    me = lax.axis_index("pulse")
    first = 4 * (me // 2 ^ step)
    groups_of(first, 4, [me % 2, me % 2 ^ 1], samples, range_tiles, bands, turned, outs)


def first_far_body(step, echoes, near, far, range_tiles, bands, samples, *rest):
    assemble(echoes, near, far, samples)
    far_pair(step, samples, range_tiles, bands, rest[-1], rest[:-1])


def first_far(step, echoes, near, far, range_tiles, bands):
    pulses = echoes.shape[1]
    blocks = 1 + echoes.shape[2] // BLK + HEAD
    samples, *made = call(
        functools.partial(first_far_body, step),
        "first_far",
        (bf16(blocks, pulses, WIDE),) + (bf16(GROUP, 2 * pulses),) * 2,
        [VMEM()] * 5,
        (VMEM(),) * 3,
        [pltpu.VMEM((5 * BLK, 2 * pulses), jnp.bfloat16)],
    )(echoes, near, far, range_tiles, bands)
    return samples, made


def rest_body(step, count, after, samples, range_tiles, bands, table, *rest):
    *outs, az_out, turned = rest
    far_pair(step, samples, range_tiles, bands, turned, outs[:2])
    me = lax.axis_index("pulse")
    groups_of(
        me // count * count * (GROUP // BLK),
        count * (GROUP // BLK),
        [me % count ^ k for k in range(count)],
        samples,
        range_tiles,
        bands,
        turned.at[pl.ds(5 * BLK, (count * (GROUP // BLK) + 1) * BLK)],
        outs[2:],
    )
    toeplitz_tiles(table, AZ_ROW, AT, AZ_TILES, 0, az_out)


def rest_range(step, after, samples, range_tiles, bands, table):
    pulses = samples.shape[1]
    count = bands.shape[0] // GROUP // 2
    *made, az_tiles = call(
        functools.partial(rest_body, step, count),
        "rest_range",
        (bf16(GROUP, 2 * pulses),) * (2 + count) + (bf16(AZ_TILES, WIDE, WIDE),),
        [VMEM()] * 5,
        (VMEM(),) * (3 + count),
        [pltpu.VMEM(((count * (GROUP // BLK) + 6) * BLK, 2 * pulses), jnp.bfloat16)],
    )(after, samples, range_tiles, bands, table)
    return made[:2], made[2:], az_tiles


def gate_body(*refs):
    pass


def gate(values, after):
    whole = pl.BlockSpec(memory_space=pl.ANY)
    return pl.pallas_call(
        gate_body,
        out_shape=tuple(jax.ShapeDtypeStruct(value.shape, value.dtype) for value in values),
        in_specs=[whole] * (len(values) + len(after)),
        out_specs=(whole,) * len(values),
        input_output_aliases={i: i for i in range(len(values))},
        compiler_params=pltpu.CompilerParams(vmem_limit_bytes=LIMIT),
        name="gate",
    )(*values, *after)


def whole_body(count, echoes, near, far, range_tiles, bands, table, out, az_out, samples, turned):
    assemble(echoes, near, far, samples)
    for block in range(count + 1):
        turned[block * BLK : (block + 1) * BLK, :] = compress(samples, range_tiles, block)
    for block in range(count):
        out[block * BLK : (block + 1) * BLK, :] = migrate(bands, turned, 0, block)
    toeplitz_tiles(table, AZ_ROW, AT, AZ_TILES, 0, az_out)


def whole_quarter(echoes, near, far, range_tiles, bands, table):
    pulses = echoes.shape[1]
    count = bands.shape[0] // BLK
    return call(
        functools.partial(whole_body, count),
        "whole_quarter",
        (bf16(count * BLK, 2 * pulses), bf16(AZ_TILES, WIDE, WIDE)),
        [VMEM()] * 6,
        (VMEM(),) * 2,
        [
            pltpu.VMEM((1 + count + HEAD, pulses, WIDE), jnp.bfloat16),
            pltpu.VMEM(((count + 1) * BLK, 2 * pulses), jnp.bfloat16),
        ],
    )(echoes, near, far, range_tiles, bands, table)


def focus_azimuth_body(steps, count, az_tiles, *rest):
    parts, out, rows, image, sems = rest[:-4], rest[-4], rest[-3], rest[-2], rest[-1]
    bins = image.shape[2]
    reach = AZ_TILES // 2
    me = lax.axis_index("pulse")
    if steps:
        starts = [me ^ step for step in steps]
    else:
        starts = [0]
    for start, part in zip(starts, parts):
        rows[pl.ds(pl.multiple_of(start * bins, bins), part.shape[0])] = part[...]
    for block in range(count):
        low, high = max(0, reach - block), min(AZ_TILES, count + reach - block)
        window = jnp.concatenate(
            [
                rows[(block + tile - reach) * bins : (block + tile - reach + 1) * bins]
                for tile in range(low, high)
            ],
            axis=1,
        )
        total = jnp.dot(
            window,
            az_tiles[low:high].reshape((high - low) * WIDE, WIDE),
            preferred_element_type=jnp.float32,
        )
        span = pl.ds(block * BLK, BLK)
        for part in range(2):
            image[part, 0, :, span] = total[:, part * BLK : (part + 1) * BLK]
        pltpu.make_async_copy(
            image.at[:, :, :, span], out.at[:, :, :, span], sems.at[block]
        ).start()
    for block in range(count):
        span = pl.ds(block * BLK, BLK)
        pltpu.make_async_copy(
            image.at[:, :, :, span], out.at[:, :, :, span], sems.at[block]
        ).wait()


def focus_azimuth(steps, az_tiles, parts):
    count = lax.axis_size("pulse")
    bins = sum(part.shape[0] for part in parts) // count
    shape = (2, 1, bins, count * BLK)
    return call(
        functools.partial(focus_azimuth_body, steps, count),
        "focus_azimuth",
        jax.ShapeDtypeStruct(shape, jnp.float32),
        [VMEM()] * (1 + len(parts)),
        HBM(),
        [
            pltpu.VMEM((count * bins, WIDE), jnp.bfloat16),
            pltpu.VMEM(shape, jnp.float32),
            pltpu.SemaphoreType.DMA((count,)),
        ],
    )(az_tiles, *parts)


def per_device(echoes, range_ref, band_weights, band_offsets, azimuth_ref):
    quarter_len = echoes.shape[2]
    peers = lax.axis_size("pulse")
    quarters = lax.axis_size("rng")
    bins = quarter_len // peers
    near, far = pack(echoes)

    def swaps(start):
        pairs = [(i, i + 1) for i in range(start, quarters - 1, 2)]
        return pairs + [(j, i) for i, j in pairs]

    far = lax.ppermute(far, "rng", swaps(1))
    near = lax.ppermute(near, "rng", swaps(0))
    table = join_small(band_weights, band_offsets, range_ref, azimuth_ref)
    range_tiles, bands = prepare(table)

    if bins != GROUP or peers != 8:
        mine, az_tiles = whole_quarter(echoes, near, far, range_tiles, bands, table)
        swapped = lax.all_to_all(
            mine.reshape(peers, bins, WIDE), "pulse", split_axis=0, concat_axis=0, tiled=True
        )
        return focus_azimuth(None, az_tiles, [swapped.reshape(mine.shape)])

    half = peers // 2

    def send(piece, k):
        return lax.ppermute(piece, "pulse", [(i, i ^ k) for i in range(peers)])

    samples, made = first_far(half // 2, echoes, near, far, range_tiles, bands)
    parts = [send(piece, half + k) for k, piece in enumerate(made)]
    made, mine, az_tiles = rest_range(half // 2 + 1, made[0], samples, range_tiles, bands, table)
    more = [send(piece, half + 2 + k) for k, piece in enumerate(made)]
    held = gate(mine[1:], parts)
    mine = mine[:1] + [send(piece, 1 + k) for k, piece in enumerate(held)]
    return focus_azimuth(
        list(range(half)) + list(range(half, peers)), az_tiles, mine + parts + more
    )


def solution(mesh):
    return jax.shard_map(
        per_device,
        mesh=mesh,
        in_specs=(P(None, "pulse", "rng"), P(), P(None, "rng"), P("rng"), P()),
        out_specs=P(None, "rng", "pulse", None),
        check_vma=False,
    )
```

time: 45.1 us -> 43 us (0.953)
  local copies, waits for them, and re-layouts: 3.56 us -> 1.24 us
  Pallas kernels: 11.2 us -> 8.94 us
  other arithmetic: 0.07 us -> 1.71 us
  waiting for transfers between devices: 15.3 us -> 16.1 us
    unnamed x12 -> x4, local copies, waits for them, and re-layouts: 3.56 us -> 1.23 us
    pallas_call x5 -> x6, Pallas kernels: 11.2 us -> 8.94 us  [the longest x1 3.65 us: rest_range(): call(functools.partial(rest_body, step, count), 'rest_range', (bf16(GROUP...]
    ppermute x1, waiting for transfers between devices: 3.38 us -> 4.82 us  [per_device(): far = lax.ppermute(far, 'rng', swaps(1))]
    concatenate x0 -> x1, other arithmetic: none -> 1.01 us  [join_small(): jnp.concatenate([weights, rows(offsets.astype(jnp.bfloat16)[None]), rows(...]
    convert_element_type x0 -> x1, other arithmetic: none -> 0.7 us  [join_small(): offsets.astype(jnp.bfloat16)[None]]
    ppermute x7, waiting for transfers between devices: 12 us -> 11.3 us  [send(): return lax.ppermute(piece, 'pulse', [(i, i ^ k) for i in range(peers)])]
  transfers between devices with their start and end apart: 9 -> 9, of which waited for: 4 -> 6; matrix products, arithmetic and copies ran while one was open for 0% -> 4% of each run, Pallas kernels for 10% -> 12%
where the time goes in v3:
time: 43 us; the launch traced here: 42.7 us
  waiting for transfers between devices  16.1 us (37%)
  starting transfers between devices  14.6 us (34%)
  Pallas kernels  8.94 us (21%)
  other arithmetic  1.71 us (4%)
  local copies, waits for them, and re-layouts  1.24 us (3%)
    ppermute x7, waiting for transfers between devices, send(): return lax.ppermute(piece, 'pulse', [(i, i ^ k) for i in range(peers)])  11.3 us
    ppermute x7, starting transfers between devices, send(): return lax.ppermute(piece, 'pulse', [(i, i ^ k) for i in range(peers)])  9.92 us
    ppermute x1, waiting for transfers between devices, per_device(): far = lax.ppermute(far, 'rng', swaps(1))  4.82 us
    ppermute x1, starting transfers between devices, per_device(): far = lax.ppermute(far, 'rng', swaps(1))  4.6 us
    pallas_call x1, Pallas kernels, rest_range(): call(functools.partial(rest_body, step, count), 'rest_range', (bf16(GROUP...  3.65 us
    pallas_call x1, Pallas kernels, focus_azimuth(): call(functools.partial(focus_azimuth_body, steps, count), 'focus_azimuth'...  2.23 us
    pallas_call x1, Pallas kernels, first_far(): call(functools.partial(first_far_body, step), 'first_far', (bf16(blocks,...  1.67 us
    pallas_call x1, Pallas kernels, prepare(): call(prepare_body, 'prepare', (bf16(RANGE_TILES, WIDE, WIDE), bf16(table....  1.28 us
  transfers between devices with their start and end apart: 9, of which 6 were waited for; matrix products, arithmetic and copies ran while one was open for 4% of the time, Pallas kernels for 12%

profile of v3, /device:TPU:1, one launch (start us, length us, event | category | flops | bytes accessed | tf_op | source)
XLA Modules:
  0.0 42.7 jit_solution(13503509415214359210)
XLA Ops:
  0.0 0.0 copy-start
  0.0 1.2 %copy-done = bf16[2,128,2048]{2,1,0:T(8,128)(2,1)S(1)} copy-done((bf16[2,128,2048]{2,1,0:T(8,128)(2,1)S(1)}, bf16[2,128,2048]{2,1,0:T(8,128)(2,1)}, u32[]{:S(2)}) %copy-start) | copy-done | bytes 1048600
  1.2 0.0 copy-start.1
  1.2 0.1 pack.1
  1.4 0.1 collective-permute-start
  1.5 4.6 %collective-permute-start.1 = (bf16[9,128,256]{2,1,0:T(8,128)(2,1)S(1)}, bf16[9,128,256]{2,1,0:T(8,128)(2,1)S(1)}, u32[]{:S(2)}, u32[]{:S(2)}) collective-permute-start(bf16[9,128,256]{2,1,0:T(8,128)(2,1)S(1)} %get-tuple-element.23), channel_id=1, source_target_pairs={{1,2},{2,1},{5,6},{6,5},{9,10},{10,9},{13,14},{14,13},{17,18},{18,... | collective-permute-start | bytes 1769480 | tf_op jit(solution)/shard_map/ppermute | solution.py:353
  6.1 0.7 %convert_element_type.9 = bf16[2048]{0:T(1024)(128)(2,1)S(1)} convert(s32[2048]{0:T(1024)} %param.8) | non-fusion elementwise | flops 2048 | bytes 12288 | tf_op jit(solution)/shard_map/convert_element_type | solution.py:80
  6.8 1.0 %fusion.6.table = bf16[88,2048]{1,0:T(8,128)(2,1)S(1)} fusion(bf16[2,512]{1,0:T(2,128)(2,1)} %param.9, bf16[2,1024]{1,0:T(2,128)(2,1)} %param.6, bf16[1,2048]{1,0:T(2,128)(2,1)S(1)} %broadcast_in_dim.3, bf16[64,2048]{1,0:T(8,128)(2,1)} %param.7), kind=kLoop, calls=%fused_computation.11 | loop fusion | flops 3244032 | bytes 632832 | tf_op jit(solution)/shard_map/concatenate | solution.py:79
  7.8 1.3 %prepare.1 = (bf16[10,256,256]{2,1,0:T(8,128)(2,1)S(1)}, bf16[2048,256]{1,0:T(8,128)(2,1)S(1)}) custom-call(bf16[88,2048]{1,0:T(8,128)(2,1)S(1)} %fusion.6.table), custom_call_target="tpu_custom_call" | custom-call | tf_op jit(solution)/shard_map/prepare/pallas_call | solution.py:134
  9.1 0.0 collective-permute-done.near
  9.1 4.8 %collective-permute-done.1.far = bf16[9,128,256]{2,1,0:T(8,128)(2,1)S(1)} collective-permute-done((bf16[9,128,256]{2,1,0:T(8,128)(2,1)S(1)}, bf16[9,128,256]{2,1,0:T(8,128)(2,1)S(1)}, u32[]{:S(2)}, u32[]{:S(2)}) %collective-permute-start.1) | collective-permute-done | bytes 589856 | tf_op jit(solution)/shard_map/ppermute | solution.py:353
  13.9 0.0 copy-done.1
  13.9 1.7 %first_far.1 = (bf16[26,128,256]{2,1,0:T(8,128)(2,1)S(1)}, bf16[256,256]{1,0:T(8,128)(2,1)S(1)}, bf16[256,256]{1,0:T(8,128)(2,1)S(1)}) custom-call(bf16[2,128,2048]{2,1,0:T(8,128)(2,1)S(1)} %copy-done.1, bf16[9,128,256]{2,1,0:T(8,128)(2,1)S(1)} %collective-permute-done.near, bf16[9,128,256]{2,1,0:T(8,128)(2,1)S(1)} %collective-permute-done.1.far, ...), custom_call_target="tpu_custom_call" | custom-call | tf_op jit(solution)/shard_map/first_far/pallas_call | solution.py:202
  15.6 3.8 %collective-permute-start.3 = (bf16[256,256]{1,0:T(8,128)(2,1)S(1)}, bf16[256,256]{1,0:T(8,128)(2,1)S(1)}, u32[]{:S(2)}, u32[]{:S(2)}) collective-permute-start(bf16[256,256]{1,0:T(8,128)(2,1)S(1)} %get-tuple-element.33), channel_id=1, source_target_pairs={{0,20},{4,16},{8,28},{12,24},{16,4},{20,0},{24,12},{28,8},{1,21},{... | collective-permute-start | bytes 393224 | tf_op jit(solution)/shard_map/ppermute | solution.py:368
  19.4 0.1 collective-permute-start.2
  19.5 3.7 %rest_range.1 = (bf16[256,256]{1,0:T(8,128)(2,1)S(1)}, bf16[256,256]{1,0:T(8,128)(2,1)S(1)}, bf16[256,256]{1,0:T(8,128)(2,1)S(1)}, bf16[256,256]{1,0:T(8,128)(2,...) custom-call(bf16[256,256]{1,0:T(8,128)(2,1)S(1)} %get-tuple-element.26.after, ...), custom_call_target="tpu_custom_call" | custom-call | tf_op jit(solution)/shard_map/rest_range/pallas_call | solution.py:233
  23.1 3.4 %collective-permute-start.7 = (bf16[256,256]{1,0:T(8,128)(2,1)S(1)}, bf16[256,256]{1,0:T(8,128)(2,1)S(1)}, u32[]{:S(2)}, u32[]{:S(2)}) collective-permute-start(bf16[256,256]{1,0:T(8,128)(2,1)S(1)} %get-tuple-element.37), channel_id=1, source_target_pairs={{0,24},{4,28},{8,16},{12,20},{16,8},{20,12},{24,0},{28,4},{1,25},{... | collective-permute-start | bytes 393224 | tf_op jit(solution)/shard_map/ppermute | solution.py:368
  26.5 0.0 collective-permute-start.8
  26.5 3.6 %collective-permute-done.3.refs_4_.rest_5_ = bf16[256,256]{1,0:T(8,128)(2,1)S(1)} collective-permute-done((bf16[256,256]{1,0:T(8,128)(2,1)S(1)}, bf16[256,256]{1,0:T(8,128)(2,1)S(1)}, u32[]{:S(2)}, u32[]{:S(2)}) %collective-permute-start.3) | collective-permute-done | bytes 131104 | tf_op jit(solution)/shard_map/ppermute | solution.py:368
  30.1 4.0 %collective-permute-done.2.refs_3_.rest_4_ = bf16[256,256]{1,0:T(8,128)(2,1)S(1)} collective-permute-done((bf16[256,256]{1,0:T(8,128)(2,1)S(1)}, bf16[256,256]{1,0:T(8,128)(2,1)S(1)}, u32[]{:S(2)}, u32[]{:S(2)}) %collective-permute-start.2) | collective-permute-done | bytes 131104 | tf_op jit(solution)/shard_map/ppermute | solution.py:368
  34.1 0.6 %collective-permute-start.4 = (bf16[256,256]{1,0:T(8,128)(2,1)S(1)}, bf16[256,256]{1,0:T(8,128)(2,1)S(1)}, u32[]{:S(2)}, u32[]{:S(2)}) collective-permute-start(bf16[256,256]{1,0:T(8,128)(2,1)S(1)} %get-tuple-element.34), channel_id=1, source_target_pairs={{0,4},{4,0},{8,12},{12,8},{16,20},{20,16},{24,28},{28,24},{1,5},{5... | collective-permute-start | bytes 393224 | tf_op jit(solution)/shard_map/ppermute | solution.py:368
  34.7 0.0 collective-permute-start.5
  34.7 2.1 %collective-permute-start.6 = (bf16[256,256]{1,0:T(8,128)(2,1)S(1)}, bf16[256,256]{1,0:T(8,128)(2,1)S(1)}, u32[]{:S(2)}, u32[]{:S(2)}) collective-permute-start(bf16[256,256]{1,0:T(8,128)(2,1)S(1)} %get-tuple-element.36), channel_id=1, source_target_pairs={{0,12},{4,8},{8,4},{12,0},{16,28},{20,24},{24,20},{28,16},{1,13},{... | collective-permute-start | bytes 393224 | tf_op jit(solution)/shard_map/ppermute | solution.py:368
  36.8 0.0 collective-permute-done.7.rest_6_
  36.8 0.0 collective-permute-done.8.rest_7_
  36.8 1.2 %collective-permute-done.4.rest_1_ = bf16[256,256]{1,0:T(8,128)(2,1)S(1)} collective-permute-done((bf16[256,256]{1,0:T(8,128)(2,1)S(1)}, bf16[256,256]{1,0:T(8,128)(2,1)S(1)}, u32[]{:S(2)}, u32[]{:S(2)}) %collective-permute-start.4) | collective-permute-done | bytes 131104 | tf_op jit(solution)/shard_map/ppermute | solution.py:368
  37.9 0.6 %collective-permute-done.5.rest_2_ = bf16[256,256]{1,0:T(8,128)(2,1)S(1)} collective-permute-done((bf16[256,256]{1,0:T(8,128)(2,1)S(1)}, bf16[256,256]{1,0:T(8,128)(2,1)S(1)}, u32[]{:S(2)}, u32[]{:S(2)}) %collective-permute-start.5) | collective-permute-done | bytes 131104 | tf_op jit(solution)/shard_map/ppermute | solution.py:368
  38.5 2.0 %collective-permute-done.6.rest_3_ = bf16[256,256]{1,0:T(8,128)(2,1)S(1)} collective-permute-done((bf16[256,256]{1,0:T(8,128)(2,1)S(1)}, bf16[256,256]{1,0:T(8,128)(2,1)S(1)}, u32[]{:S(2)}, u32[]{:S(2)}) %collective-permute-start.6) | collective-permute-done | bytes 131104 | tf_op jit(solution)/shard_map/ppermute | solution.py:368
  40.5 2.2 %focus_azimuth.1 = f32[2,1,256,1024]{3,2,1,0:T(8,128)} custom-call(bf16[5,256,256]{2,1,0:T(8,128)(2,1)S(1)} %get-tuple-element.28.az_tiles, bf16[256,256]{1,0:T(8,128)(2,1)S(1)} %get-tuple-element.29.rest_0_, bf16[256,256]{1,0:T(8,128)(2,1)S(1)} %collective-permute-done.4.rest_1_, bf16[256,256]{1,0:T(8,128)(2,1)S(1)} %collective-permute-done.5.rest_2_, ...), custom_call_target="tpu_custom_call" | custom-call | tf_op jit(solution)/shard_map/focus_azimuth/pallas_call | solution.py:328
  (2 shorter events, 0.0 us)
Async XLA Ops:
  0.0 1.2 %copy-start = (bf16[2,128,2048]{2,1,0:T(8,128)(2,1)S(1)}, bf16[2,128,2048]{2,1,0:T(8,128)(2,1)}, u32[]{:S(2)}) copy-start(bf16[2,128,2048]{2,1,0:T(8,128)(2,1)} %echoes.3) | copy-start | bytes 3145732
  1.2 12.7 %copy-start.1 = (bf16[2,128,2048]{2,1,0:T(8,128)(2,1)S(1)}, bf16[2,128,2048]{2,1,0:T(8,128)(2,1)}, u32[]{:S(2)}) copy-start(bf16[2,128,2048]{2,1,0:T(8,128)(2,1)} %echoes.3) | copy-start | bytes 3145732
  1.4 7.7 %collective-permute-start = (bf16[9,128,256]{2,1,0:T(8,128)(2,1)S(1)}, bf16[9,128,256]{2,1,0:T(8,128)(2,1)S(1)}, u32[]{:S(2)}, u32[]{:S(2)}) collective-permute-start(bf16[9,128,256]{2,1,0:T(8,128)(2,1)S(1)} %get-tuple-element.22), channel_id=1, source_target_pairs={{0,1},{2,3},{1,0},{3,2},{4,5},{6,7},{5,4},{7,6},{8,9},{10,11},{9,8... | collective-permute-start | bytes 1769480 | tf_op jit(solution)/shard_map/ppermute | solution.py:354
  1.5 12.5 %collective-permute-start.1 = (bf16[9,128,256]{2,1,0:T(8,128)(2,1)S(1)}, bf16[9,128,256]{2,1,0:T(8,128)(2,1)S(1)}, u32[]{:S(2)}, u32[]{:S(2)}) collective-permute-start(bf16[9,128,256]{2,1,0:T(8,128)(2,1)S(1)} %get-tuple-element.23), channel_id=1, source_target_pairs={{1,2},{2,1},{5,6},{6,5},{9,10},{10,9},{13,14},{14,13},{17,18},{18,... | collective-permute-start | bytes 1769480 | tf_op jit(solution)/shard_map/ppermute | solution.py:353
  15.6 14.5 %collective-permute-start.3 = (bf16[256,256]{1,0:T(8,128)(2,1)S(1)}, bf16[256,256]{1,0:T(8,128)(2,1)S(1)}, u32[]{:S(2)}, u32[]{:S(2)}) collective-permute-start(bf16[256,256]{1,0:T(8,128)(2,1)S(1)} %get-tuple-element.33), channel_id=1, source_target_pairs={{0,20},{4,16},{8,28},{12,24},{16,4},{20,0},{24,12},{28,8},{1,21},{... | collective-permute-start | bytes 393224 | tf_op jit(solution)/shard_map/ppermute | solution.py:368
  19.4 14.7 %collective-permute-start.2 = (bf16[256,256]{1,0:T(8,128)(2,1)S(1)}, bf16[256,256]{1,0:T(8,128)(2,1)S(1)}, u32[]{:S(2)}, u32[]{:S(2)}) collective-permute-start(bf16[256,256]{1,0:T(8,128)(2,1)S(1)} %get-tuple-element.26.after), channel_id=1, source_target_pairs={{0,16},{4,20},{8,24},{12,28},{16,0},{20,4},{24,8},{28,12},{1,17},{... | collective-permute-start | bytes 393224 | tf_op jit(solution)/shard_map/ppermute | solution.py:368
  23.1 13.6 %collective-permute-start.7 = (bf16[256,256]{1,0:T(8,128)(2,1)S(1)}, bf16[256,256]{1,0:T(8,128)(2,1)S(1)}, u32[]{:S(2)}, u32[]{:S(2)}) collective-permute-start(bf16[256,256]{1,0:T(8,128)(2,1)S(1)} %get-tuple-element.37), channel_id=1, source_target_pairs={{0,24},{4,28},{8,16},{12,20},{16,8},{20,12},{24,0},{28,4},{1,25},{... | collective-permute-start | bytes 393224 | tf_op jit(solution)/shard_map/ppermute | solution.py:368
  26.5 10.2 %collective-permute-start.8 = (bf16[256,256]{1,0:T(8,128)(2,1)S(1)}, bf16[256,256]{1,0:T(8,128)(2,1)S(1)}, u32[]{:S(2)}, u32[]{:S(2)}) collective-permute-start(bf16[256,256]{1,0:T(8,128)(2,1)S(1)} %get-tuple-element.38), channel_id=1, source_target_pairs={{0,28},{4,24},{8,20},{12,16},{16,12},{20,8},{24,4},{28,0},{1,29},{... | collective-permute-start | bytes 393224 | tf_op jit(solution)/shard_map/ppermute | solution.py:368
  34.1 3.8 %collective-permute-start.4 = (bf16[256,256]{1,0:T(8,128)(2,1)S(1)}, bf16[256,256]{1,0:T(8,128)(2,1)S(1)}, u32[]{:S(2)}, u32[]{:S(2)}) collective-permute-start(bf16[256,256]{1,0:T(8,128)(2,1)S(1)} %get-tuple-element.34), channel_id=1, source_target_pairs={{0,4},{4,0},{8,12},{12,8},{16,20},{20,16},{24,28},{28,24},{1,5},{5... | collective-permute-start | bytes 393224 | tf_op jit(solution)/shard_map/ppermute | solution.py:368
  34.7 3.8 %collective-permute-start.5 = (bf16[256,256]{1,0:T(8,128)(2,1)S(1)}, bf16[256,256]{1,0:T(8,128)(2,1)S(1)}, u32[]{:S(2)}, u32[]{:S(2)}) collective-permute-start(bf16[256,256]{1,0:T(8,128)(2,1)S(1)} %get-tuple-element.35), channel_id=1, source_target_pairs={{0,8},{4,12},{8,0},{12,4},{16,24},{20,28},{24,16},{28,20},{1,9},{5... | collective-permute-start | bytes 393224 | tf_op jit(solution)/shard_map/ppermute | solution.py:368
  34.7 5.8 %collective-permute-start.6 = (bf16[256,256]{1,0:T(8,128)(2,1)S(1)}, bf16[256,256]{1,0:T(8,128)(2,1)S(1)}, u32[]{:S(2)}, u32[]{:S(2)}) collective-permute-start(bf16[256,256]{1,0:T(8,128)(2,1)S(1)} %get-tuple-element.36), channel_id=1, source_target_pairs={{0,12},{4,8},{8,4},{12,0},{16,28},{20,24},{24,20},{28,16},{1,13},{... | collective-permute-start | bytes 393224 | tf_op jit(solution)/shard_map/ppermute | solution.py:368

commit v4 on v3

--- a/solution.py
+++ b/solution.py
@@ -18,12 +18,13 @@
 HEAD = RT // BLK + 1
 GROUP = 2 * BLK
 LIMIT = 24 * 1024 * 1024
+PACK_FLOPS = 2 * 10**9
 
 VMEM = functools.partial(pl.BlockSpec, memory_space=pltpu.VMEM)
 HBM = functools.partial(pl.BlockSpec, memory_space=pltpu.HBM)
 
 
-def call(body, name, out_shape, in_specs, out_specs, scratch_shapes=()):
+def call(body, name, out_shape, in_specs, out_specs, scratch_shapes=(), flops=0):
     return pl.pallas_call(
         body,
         out_shape=out_shape,
@@ -31,7 +32,7 @@
         out_specs=out_specs,
         scratch_shapes=scratch_shapes,
         compiler_params=pltpu.CompilerParams(vmem_limit_bytes=LIMIT),
-        cost_estimate=pl.CostEstimate(flops=0, bytes_accessed=0, transcendentals=0),
+        cost_estimate=pl.CostEstimate(flops=flops, bytes_accessed=0, transcendentals=0),
         name=name,
     )
 
@@ -61,35 +62,19 @@
         (bf16(HEAD, echoes.shape[1], WIDE),) * 2,
         [VMEM()],
         (VMEM(),) * 2,
+        flops=PACK_FLOPS,
     )(echoes)
 
 
-OFFSET_ROW = BAND
-RANGE_ROW = BAND + 8
-AZ_ROW = BAND + 16
-TABLE_ROWS = BAND + 24
-
-
-def join_small(weights, offsets, range_ref, azimuth_ref):
-    bins = weights.shape[1]
-
-    def rows(value):
-        return jnp.pad(value, ((0, 8 - value.shape[0]), (0, bins - value.shape[1])))
-
-    return jnp.concatenate(
-        [weights, rows(offsets.astype(jnp.bfloat16)[None]), rows(range_ref), rows(azimuth_ref)],
-        axis=0,
-    )
-
-
-def toeplitz_tiles(table, start, tap_total, tiles, shift, out):
+def toeplitz_tiles(taps, tiles, shift, out):
     width = (tiles + 1) * BLK
+    tap_total = taps.shape[1]
     skewed = []
     for part in range(2):
         row = jnp.concatenate(
             [
                 jnp.zeros((1, BLK), jnp.float32),
-                table[start : start + 8, :tap_total].astype(jnp.float32)[part : part + 1],
+                taps[part : part + 1, :].astype(jnp.float32),
                 jnp.zeros((1, width - BLK - tap_total), jnp.float32),
             ],
             axis=1,
@@ -106,20 +91,20 @@
         out[tile, BLK:, BLK:] = real.astype(jnp.bfloat16)
 
 
-def prepare_body(table, range_out, band_out):
-    toeplitz_tiles(table, RANGE_ROW, RT, RANGE_TILES, HALF, range_out)
+def prepare_body(range_ref, weights, offsets, range_out, band_out):
+    toeplitz_tiles(range_ref, RANGE_TILES, HALF, range_out)
     lowest = lax.axis_index("rng") == 0
     lane = lax.broadcasted_iota(jnp.int32, (BLK, WIDE), 1)
-    for block in range(table.shape[1] // BLK):
+    for block in range(weights.shape[1] // BLK):
         span = slice(block * BLK, (block + 1) * BLK)
         placed = jnp.concatenate(
             [
-                table[:BAND, span].astype(jnp.float32),
+                weights[:, span].astype(jnp.float32),
                 jnp.zeros((BLK - BAND, BLK), jnp.float32),
             ],
             axis=0,
         )
-        shifts = table[OFFSET_ROW : OFFSET_ROW + 8, span].astype(jnp.float32).astype(jnp.int32)[:1]
+        shifts = offsets[block : block + 1, :]
         for bit in range((BAND // 2).bit_length()):
             chosen = jnp.broadcast_to((shifts >> bit) & 1, (BLK, BLK)) == 1
             placed = jnp.where(chosen, pltpu.roll(placed, 1 << bit, 0), placed)
@@ -130,14 +115,14 @@
         band_out[span, :] = skewed.astype(jnp.bfloat16)
 
 
-def prepare(table):
+def prepare(range_ref, weights, offsets):
     return call(
         prepare_body,
         "prepare",
-        (bf16(RANGE_TILES, WIDE, WIDE), bf16(table.shape[1], WIDE)),
-        [VMEM()],
-        (VMEM(),) * 2,
-    )(table)
+        (bf16(RANGE_TILES, WIDE, WIDE), bf16(weights.shape[1], WIDE)),
+        [VMEM()] * 3,
+        (VMEM(),) * 2,
+    )(range_ref, weights, offsets.reshape(-1, BLK))
 
 
 def assemble(echoes, near, far, out):
@@ -178,7 +163,8 @@
 def groups_of(first, count, spots, samples, range_tiles, bands, turned, outs):
     for block in range(count + 1):
         turned[block * BLK : (block + 1) * BLK, :] = compress(samples, range_tiles, first + block)
-    for spot, out in zip(spots, outs):
+    rows = [out.at[pl.ds(i, GROUP)] for out in outs for i in range(0, out.shape[0], GROUP)]
+    for spot, out in zip(spots, rows):
         for block in range(GROUP // BLK):
             out[block * BLK : (block + 1) * BLK, :] = migrate(
                 bands, turned, first, spot * (GROUP // BLK) + block
@@ -210,43 +196,57 @@
     return samples, made
 
 
-def rest_body(step, count, after, samples, range_tiles, bands, table, *rest):
-    *outs, az_out, turned = rest
-    far_pair(step, samples, range_tiles, bands, turned, outs[:2])
+def next_far_body(step, samples, range_tiles, bands, *rest):
+    far_pair(step, samples, range_tiles, bands, rest[-1], rest[:-1])
+
+
+def next_far(step, samples, range_tiles, bands):
+    pulses = samples.shape[1]
+    return call(
+        functools.partial(next_far_body, step),
+        "next_far",
+        (bf16(GROUP, 2 * pulses),) * 2,
+        [VMEM()] * 3,
+        (VMEM(),) * 2,
+        [pltpu.VMEM((5 * BLK, 2 * pulses), jnp.bfloat16)],
+    )(samples, range_tiles, bands)
+
+
+def near_body(count, after, samples, range_tiles, bands, az_taps, out, az_out, turned):
     me = lax.axis_index("pulse")
     groups_of(
         me // count * count * (GROUP // BLK),
         count * (GROUP // BLK),
-        [me % count ^ k for k in range(count)],
+        list(range(count)),
         samples,
         range_tiles,
         bands,
-        turned.at[pl.ds(5 * BLK, (count * (GROUP // BLK) + 1) * BLK)],
-        outs[2:],
+        turned,
+        [out],
     )
-    toeplitz_tiles(table, AZ_ROW, AT, AZ_TILES, 0, az_out)
-
-
-def rest_range(step, after, samples, range_tiles, bands, table):
+    toeplitz_tiles(az_taps, AZ_TILES, 0, az_out)
+
+
+def near_half(after, samples, range_tiles, bands, azimuth_ref):
     pulses = samples.shape[1]
     count = bands.shape[0] // GROUP // 2
-    *made, az_tiles = call(
-        functools.partial(rest_body, step, count),
-        "rest_range",
-        (bf16(GROUP, 2 * pulses),) * (2 + count) + (bf16(AZ_TILES, WIDE, WIDE),),
+    return call(
+        functools.partial(near_body, count),
+        "near_half",
+        (bf16(count * GROUP, 2 * pulses), bf16(AZ_TILES, WIDE, WIDE)),
         [VMEM()] * 5,
-        (VMEM(),) * (3 + count),
-        [pltpu.VMEM(((count * (GROUP // BLK) + 6) * BLK, 2 * pulses), jnp.bfloat16)],
-    )(after, samples, range_tiles, bands, table)
-    return made[:2], made[2:], az_tiles
+        (VMEM(),) * 2,
+        [pltpu.VMEM(((count * (GROUP // BLK) + 1) * BLK, 2 * pulses), jnp.bfloat16)],
+    )(after, samples, range_tiles, bands, azimuth_ref)
 
 
 def gate_body(*refs):
     pass
 
 
-def gate(values, after):
+def gate(values, after=(), flops=0):
     whole = pl.BlockSpec(memory_space=pl.ANY)
+    values = list(values)
     return pl.pallas_call(
         gate_body,
         out_shape=tuple(jax.ShapeDtypeStruct(value.shape, value.dtype) for value in values),
@@ -254,20 +254,21 @@
         out_specs=(whole,) * len(values),
         input_output_aliases={i: i for i in range(len(values))},
         compiler_params=pltpu.CompilerParams(vmem_limit_bytes=LIMIT),
+        cost_estimate=pl.CostEstimate(flops=flops, bytes_accessed=0, transcendentals=0),
         name="gate",
     )(*values, *after)
 
 
-def whole_body(count, echoes, near, far, range_tiles, bands, table, out, az_out, samples, turned):
+def whole_body(count, echoes, near, far, range_tiles, bands, az_taps, out, az_out, samples, turned):
     assemble(echoes, near, far, samples)
     for block in range(count + 1):
         turned[block * BLK : (block + 1) * BLK, :] = compress(samples, range_tiles, block)
     for block in range(count):
         out[block * BLK : (block + 1) * BLK, :] = migrate(bands, turned, 0, block)
-    toeplitz_tiles(table, AZ_ROW, AT, AZ_TILES, 0, az_out)
-
-
-def whole_quarter(echoes, near, far, range_tiles, bands, table):
+    toeplitz_tiles(az_taps, AZ_TILES, 0, az_out)
+
+
+def whole_quarter(echoes, near, far, range_tiles, bands, azimuth_ref):
     pulses = echoes.shape[1]
     count = bands.shape[0] // BLK
     return call(
@@ -280,7 +281,7 @@
             pltpu.VMEM((1 + count + HEAD, pulses, WIDE), jnp.bfloat16),
             pltpu.VMEM(((count + 1) * BLK, 2 * pulses), jnp.bfloat16),
         ],
-    )(echoes, near, far, range_tiles, bands, table)
+    )(echoes, near, far, range_tiles, bands, azimuth_ref)
 
 
 def focus_azimuth_body(steps, count, az_tiles, *rest):
@@ -289,11 +290,13 @@
     reach = AZ_TILES // 2
     me = lax.axis_index("pulse")
     if steps:
-        starts = [me ^ step for step in steps]
+        half = steps[0]
+        start = pl.multiple_of(me // half * half * bins, half * bins)
+        rows[pl.ds(start, half * bins)] = parts[0][...]
+        for part, step in zip(parts[1:], steps[1:]):
+            rows[pl.ds(pl.multiple_of((me ^ step) * bins, bins), bins)] = part[...]
     else:
-        starts = [0]
-    for start, part in zip(starts, parts):
-        rows[pl.ds(pl.multiple_of(start * bins, bins), part.shape[0])] = part[...]
+        rows[...] = parts[0][...]
     for block in range(count):
         low, high = max(0, reach - block), min(AZ_TILES, count + reach - block)
         window = jnp.concatenate(
@@ -321,9 +324,8 @@
         ).wait()
 
 
-def focus_azimuth(steps, az_tiles, parts):
+def focus_azimuth(steps, bins, az_tiles, parts):
     count = lax.axis_size("pulse")
-    bins = sum(part.shape[0] for part in parts) // count
     shape = (2, 1, bins, count * BLK)
     return call(
         functools.partial(focus_azimuth_body, steps, count),
@@ -352,15 +354,14 @@
 
     far = lax.ppermute(far, "rng", swaps(1))
     near = lax.ppermute(near, "rng", swaps(0))
-    table = join_small(band_weights, band_offsets, range_ref, azimuth_ref)
-    range_tiles, bands = prepare(table)
+    range_tiles, bands = prepare(range_ref, band_weights, band_offsets)
 
     if bins != GROUP or peers != 8:
-        mine, az_tiles = whole_quarter(echoes, near, far, range_tiles, bands, table)
+        mine, az_tiles = whole_quarter(echoes, near, far, range_tiles, bands, azimuth_ref)
         swapped = lax.all_to_all(
             mine.reshape(peers, bins, WIDE), "pulse", split_axis=0, concat_axis=0, tiled=True
         )
-        return focus_azimuth(None, az_tiles, [swapped.reshape(mine.shape)])
+        return focus_azimuth(None, bins, az_tiles, [swapped.reshape(mine.shape)])
 
     half = peers // 2
 
@@ -369,13 +370,19 @@
 
     samples, made = first_far(half // 2, echoes, near, far, range_tiles, bands)
     parts = [send(piece, half + k) for k, piece in enumerate(made)]
-    made, mine, az_tiles = rest_range(half // 2 + 1, made[0], samples, range_tiles, bands, table)
-    more = [send(piece, half + 2 + k) for k, piece in enumerate(made)]
-    held = gate(mine[1:], parts)
-    mine = mine[:1] + [send(piece, 1 + k) for k, piece in enumerate(held)]
-    return focus_azimuth(
-        list(range(half)) + list(range(half, peers)), az_tiles, mine + parts + more
-    )
+    made = next_far(half // 2 + 1, samples, range_tiles, bands)
+    parts += [send(piece, half + 2 + k) for k, piece in enumerate(made)]
+    mine, az_tiles = near_half(made[0], samples, range_tiles, bands, azimuth_ref)
+    mine = lax.all_to_all(
+        mine.reshape(half, bins, WIDE),
+        "pulse",
+        split_axis=0,
+        concat_axis=0,
+        axis_index_groups=[list(range(half)), list(range(half, peers))],
+        tiled=True,
+    ).reshape(mine.shape)
+    parts = gate(gate(parts[:2], (), 500000000) + tuple(parts[2:]), (), 20000000000)
+    return focus_azimuth([half] + list(range(half, peers)), bins, az_tiles, [mine, *parts])
 
 
 def solution(mesh):

time: 43 us -> 39.4 us (0.916)
  the two profiles are of different devices: /device:TPU:1 before, /device:TPU:18 now
where the time goes in v4:
time: 39.4 us; the launch traced here: 39.1 us
  starting transfers between devices  14.2 us (36%)
  waiting for transfers between devices  14 us (36%)
  Pallas kernels  9.58 us (24%)
  local copies, waits for them, and re-layouts  1.24 us (3%)
    ppermute x1, waiting for transfers between devices, per_device(): far = lax.ppermute(far, 'rng', swaps(1))  7.46 us
    ppermute x4, starting transfers between devices, send(): return lax.ppermute(piece, 'pulse', [(i, i ^ k) for i in range(peers)])  5.98 us
    all_to_all x1, starting transfers between devices, per_device(): lax.all_to_all(mine.reshape(half, bins, WIDE), 'pulse', split_axis=0, con...  5.6 us
    all_to_all x1, waiting for transfers between devices, per_device(): lax.all_to_all(mine.reshape(half, bins, WIDE), 'pulse', split_axis=0, con...  5.16 us
    pallas_call x1, Pallas kernels, near_half(): call(functools.partial(near_body, count), 'near_half', (bf16(count * GROU...  2.84 us
    ppermute x1, starting transfers between devices, per_device(): far = lax.ppermute(far, 'rng', swaps(1))  2.53 us
    pallas_call x1, Pallas kernels, focus_azimuth(): call(functools.partial(focus_azimuth_body, steps, count), 'focus_azimuth'...  2.23 us
    pallas_call x1, Pallas kernels, first_far(): call(functools.partial(first_far_body, step), 'first_far', (bf16(blocks,...  1.66 us
  transfers between devices with their start and end apart: 7, of which 4 were waited for; matrix products, arithmetic and copies ran while one was open for 0% of the time, Pallas kernels for 14%

profile of v4, /device:TPU:18, one launch (start us, length us, event | category | flops | bytes accessed | tf_op | source)
XLA Modules:
  0.0 39.1 jit_solution(3845849347069311377)
XLA Ops:
  0.0 0.0 copy-start
  0.0 1.2 %copy-done = bf16[2,128,2048]{2,1,0:T(8,128)(2,1)S(1)} copy-done((bf16[2,128,2048]{2,1,0:T(8,128)(2,1)S(1)}, bf16[2,128,2048]{2,1,0:T(8,128)(2,1)}, u32[]{:S(2)}) %copy-start) | copy-done | bytes 1048600
  1.2 0.0 copy-start.2
  1.2 0.0 copy-start.3
  1.2 0.0 copy-start.4
  1.2 0.0 copy-start.1
  1.2 0.1 pack.1
  1.4 0.1 collective-permute-start
  1.5 2.5 %collective-permute-start.1 = (bf16[9,128,256]{2,1,0:T(8,128)(2,1)S(1)}, bf16[9,128,256]{2,1,0:T(8,128)(2,1)S(1)}, u32[]{:S(2)}, u32[]{:S(2)}) collective-permute-start(bf16[9,128,256]{2,1,0:T(8,128)(2,1)S(1)} %get-tuple-element.23), channel_id=1, source_target_pairs={{1,2},{2,1},{5,6},{6,5},{9,10},{10,9},{13,14},{14,13},{17,18},{18,... | collective-permute-start | bytes 1769480 | tf_op jit(solution)/shard_map/ppermute | solution.py:355
  4.0 0.0 copy-done.2
  4.0 0.0 copy-done.3
  4.0 0.0 copy-done.4
  4.0 1.3 %prepare.1 = (bf16[10,256,256]{2,1,0:T(8,128)(2,1)S(1)}, bf16[2048,256]{1,0:T(8,128)(2,1)S(1)}) custom-call(bf16[2,1024]{1,0:T(2,128)(2,1)S(1)} %copy-done.4, bf16[64,2048]{1,0:T(8,128)(2,1)S(1)} %copy-done.2, s32[16,128]{1,0:T(8,128)S(1)} %bitcast.4), custom_call_target="tpu_custom_call" | custom-call | tf_op jit(solution)/shard_map/prepare/pallas_call | solution.py:119
  5.3 0.0 collective-permute-done.near
  5.3 7.5 %collective-permute-done.1.far = bf16[9,128,256]{2,1,0:T(8,128)(2,1)S(1)} collective-permute-done((bf16[9,128,256]{2,1,0:T(8,128)(2,1)S(1)}, bf16[9,128,256]{2,1,0:T(8,128)(2,1)S(1)}, u32[]{:S(2)}, u32[]{:S(2)}) %collective-permute-start.1) | collective-permute-done | bytes 589856 | tf_op jit(solution)/shard_map/ppermute | solution.py:355
  12.8 0.0 copy-done.1
  12.8 1.7 %first_far.1 = (bf16[26,128,256]{2,1,0:T(8,128)(2,1)S(1)}, bf16[256,256]{1,0:T(8,128)(2,1)S(1)}, bf16[256,256]{1,0:T(8,128)(2,1)S(1)}) custom-call(bf16[2,128,2048]{2,1,0:T(8,128)(2,1)S(1)} %copy-done.1, bf16[9,128,256]{2,1,0:T(8,128)(2,1)S(1)} %collective-permute-done.near, bf16[9,128,256]{2,1,0:T(8,128)(2,1)S(1)} %collective-permute-done.1.far, ...), custom_call_target="tpu_custom_call" | custom-call | tf_op jit(solution)/shard_map/first_far/pallas_call | solution.py:188
  14.5 0.4 %collective-permute-start.2 = (bf16[256,256]{1,0:T(8,128)(2,1)S(1)}, bf16[256,256]{1,0:T(8,128)(2,1)S(1)}, u32[]{:S(2)}, u32[]{:S(2)}) collective-permute-start(bf16[256,256]{1,0:T(8,128)(2,1)S(1)} %get-tuple-element.30), channel_id=1, source_target_pairs={{0,16},{4,20},{8,24},{12,28},{16,0},{20,4},{24,8},{28,12},{1,17},{... | collective-permute-start | bytes 393224 | tf_op jit(solution)/shard_map/ppermute | solution.py:369
  14.9 3.6 %collective-permute-start.3 = (bf16[256,256]{1,0:T(8,128)(2,1)S(1)}, bf16[256,256]{1,0:T(8,128)(2,1)S(1)}, u32[]{:S(2)}, u32[]{:S(2)}) collective-permute-start(bf16[256,256]{1,0:T(8,128)(2,1)S(1)} %get-tuple-element.31), channel_id=1, source_target_pairs={{0,20},{4,16},{8,28},{12,24},{16,4},{20,0},{24,12},{28,8},{1,21},{... | collective-permute-start | bytes 393224 | tf_op jit(solution)/shard_map/ppermute | solution.py:369
  18.4 0.0 copy-start.5
  18.4 1.4 %next_far.1 = (bf16[256,256]{1,0:T(8,128)(2,1)S(1)}, bf16[256,256]{1,0:T(8,128)(2,1)S(1)}) custom-call(bf16[26,128,256]{2,1,0:T(8,128)(2,1)S(1)} %get-tuple-element.26.samples, bf16[10,256,256]{2,1,0:T(8,128)(2,1)S(1)} %get-tuple-element.24.range_tiles, bf16[2048,256]{1,0:T(8,128)(2,1)S(1)} %get-tuple-element.25.bands), custom_call_target="tpu_custom_call" | custom-call | tf_op jit(solution)/shard_map/next_far/pallas_call | solution.py:205
  19.9 0.5 %collective-permute-start.5 = (bf16[256,256]{1,0:T(8,128)(2,1)S(1)}, bf16[256,256]{1,0:T(8,128)(2,1)S(1)}, u32[]{:S(2)}, u32[]{:S(2)}) collective-permute-start(bf16[256,256]{1,0:T(8,128)(2,1)S(1)} %get-tuple-element.34), channel_id=1, source_target_pairs={{0,28},{4,24},{8,20},{12,16},{16,12},{20,8},{24,4},{28,0},{1,29},{... | collective-permute-start | bytes 393224 | tf_op jit(solution)/shard_map/ppermute | solution.py:369
  20.3 1.6 %collective-permute-start.4 = (bf16[256,256]{1,0:T(8,128)(2,1)S(1)}, bf16[256,256]{1,0:T(8,128)(2,1)S(1)}, u32[]{:S(2)}, u32[]{:S(2)}) collective-permute-start(bf16[256,256]{1,0:T(8,128)(2,1)S(1)} %get-tuple-element.27.after), channel_id=1, source_target_pairs={{0,24},{4,28},{8,16},{12,20},{16,8},{20,12},{24,0},{28,4},{1,25},{... | collective-permute-start | bytes 393224 | tf_op jit(solution)/shard_map/ppermute | solution.py:369
  21.9 0.0 copy-done.5
  21.9 2.8 %near_half.1 = (bf16[1024,256]{1,0:T(8,128)(2,1)}, bf16[5,256,256]{2,1,0:T(8,128)(2,1)S(1)}) custom-call(bf16[256,256]{1,0:T(8,128)(2,1)S(1)} %get-tuple-element.27.after, bf16[26,128,256]{2,1,0:T(8,128)(2,1)S(1)} %get-tuple-element.26.samples, bf16[10,256,256]{2,1,0:T(8,128)(2,1)S(1)} %get-tuple-element.24.range_tiles, ...), custom_call_target="tpu_custom_call" | custom-call | tf_op jit(solution)/shard_map/near_half/pallas_call | solution.py:233
  24.7 5.6 %all-to-all-start = ((bf16[4,256,256]{2,1,0:T(8,128)(2,1)}), bf16[4,256,256]{2,1,0:T(8,128)(2,1)S(1)}, u32[]{:S(2)}, u32[]{:S(2)}) async-start(bf16[4,256,256]{2,1,0:T(8,128)(2,1)} %bitcast.1), calls=%async_computation | async-start | bytes 1048576 | tf_op jit(solution)/shard_map/all_to_all | solution.py:376
  30.3 0.0 collective-permute-done.2.refs_0_
  30.3 0.0 collective-permute-done.3.refs_1_
  30.4 1.0 %collective-permute-done.5.refs_3_ = bf16[256,256]{1,0:T(8,128)(2,1)S(1)} collective-permute-done((bf16[256,256]{1,0:T(8,128)(2,1)S(1)}, bf16[256,256]{1,0:T(8,128)(2,1)S(1)}, u32[]{:S(2)}, u32[]{:S(2)}) %collective-permute-start.5) | collective-permute-done | bytes 131104 | tf_op jit(solution)/shard_map/ppermute | solution.py:369
  31.3 0.4 %collective-permute-done.4.refs_2_ = bf16[256,256]{1,0:T(8,128)(2,1)S(1)} collective-permute-done((bf16[256,256]{1,0:T(8,128)(2,1)S(1)}, bf16[256,256]{1,0:T(8,128)(2,1)S(1)}, u32[]{:S(2)}, u32[]{:S(2)}) %collective-permute-start.4) | collective-permute-done | bytes 131104 | tf_op jit(solution)/shard_map/ppermute | solution.py:369
  31.8 5.2 %all-to-all-done = bf16[4,256,256]{2,1,0:T(8,128)(2,1)S(1)} async-done(((bf16[4,256,256]{2,1,0:T(8,128)(2,1)}), bf16[4,256,256]{2,1,0:T(8,128)(2,1)S(1)}, u32[]{:S(2)}, u32[]{:S(2)}) %all-to-all-start) | async-done | bytes 524320 | tf_op jit(solution)/shard_map/all_to_all | solution.py:376
  36.9 2.2 %focus_azimuth.1 = f32[2,1,256,1024]{3,2,1,0:T(8,128)} custom-call(bf16[5,256,256]{2,1,0:T(8,128)(2,1)S(1)} %get-tuple-element.28.az_tiles, bf16[1024,256]{1,0:T(8,128)(2,1)S(1)} %bitcast.3, bf16[256,256]{1,0:T(8,128)(2,1)S(1)} %get-tuple-element.35.rest_1_, bf16[256,256]{1,0:T(8,128)(2,1)S(1)} %get-tuple-element.36.rest_2_, ...), custom_call_target="tpu_custom_call" | custom-call | tf_op jit(solution)/shard_map/focus_azimuth/pallas_call | solution.py:330
  (2 shorter events, 0.0 us)
Async XLA Ops:
  0.0 1.2 %copy-start = (bf16[2,128,2048]{2,1,0:T(8,128)(2,1)S(1)}, bf16[2,128,2048]{2,1,0:T(8,128)(2,1)}, u32[]{:S(2)}) copy-start(bf16[2,128,2048]{2,1,0:T(8,128)(2,1)} %echoes.3) | copy-start | bytes 3145732
  1.2 2.8 %copy-start.2 = (bf16[64,2048]{1,0:T(8,128)(2,1)S(1)}, bf16[64,2048]{1,0:T(8,128)(2,1)}, u32[]{:S(2)}) copy-start(bf16[64,2048]{1,0:T(8,128)(2,1)} %weights.1) | copy-start | bytes 786436
  1.2 2.8 %copy-start.3 = (s32[2048]{0:T(1024)S(1)}, s32[2048]{0:T(1024)}, u32[]{:S(2)}) copy-start(s32[2048]{0:T(1024)} %param.8) | copy-start | bytes 24580
  1.2 2.8 %copy-start.4 = (bf16[2,1024]{1,0:T(2,128)(2,1)S(1)}, bf16[2,1024]{1,0:T(2,128)(2,1)}, u32[]{:S(2)}) copy-start(bf16[2,1024]{1,0:T(2,128)(2,1)} %range_ref.1) | copy-start | bytes 12292
  1.2 11.6 %copy-start.1 = (bf16[2,128,2048]{2,1,0:T(8,128)(2,1)S(1)}, bf16[2,128,2048]{2,1,0:T(8,128)(2,1)}, u32[]{:S(2)}) copy-start(bf16[2,128,2048]{2,1,0:T(8,128)(2,1)} %echoes.3) | copy-start | bytes 3145732
  1.4 3.9 %collective-permute-start = (bf16[9,128,256]{2,1,0:T(8,128)(2,1)S(1)}, bf16[9,128,256]{2,1,0:T(8,128)(2,1)S(1)}, u32[]{:S(2)}, u32[]{:S(2)}) collective-permute-start(bf16[9,128,256]{2,1,0:T(8,128)(2,1)S(1)} %get-tuple-element.22), channel_id=1, source_target_pairs={{0,1},{2,3},{1,0},{3,2},{4,5},{6,7},{5,4},{7,6},{8,9},{10,11},{9,8... | collective-permute-start | bytes 1769480 | tf_op jit(solution)/shard_map/ppermute | solution.py:356
  1.5 11.3 %collective-permute-start.1 = (bf16[9,128,256]{2,1,0:T(8,128)(2,1)S(1)}, bf16[9,128,256]{2,1,0:T(8,128)(2,1)S(1)}, u32[]{:S(2)}, u32[]{:S(2)}) collective-permute-start(bf16[9,128,256]{2,1,0:T(8,128)(2,1)S(1)} %get-tuple-element.23), channel_id=1, source_target_pairs={{1,2},{2,1},{5,6},{6,5},{9,10},{10,9},{13,14},{14,13},{17,18},{18,... | collective-permute-start | bytes 1769480 | tf_op jit(solution)/shard_map/ppermute | solution.py:355
  14.5 15.9 %collective-permute-start.2 = (bf16[256,256]{1,0:T(8,128)(2,1)S(1)}, bf16[256,256]{1,0:T(8,128)(2,1)S(1)}, u32[]{:S(2)}, u32[]{:S(2)}) collective-permute-start(bf16[256,256]{1,0:T(8,128)(2,1)S(1)} %get-tuple-element.30), channel_id=1, source_target_pairs={{0,16},{4,20},{8,24},{12,28},{16,0},{20,4},{24,8},{28,12},{1,17},{... | collective-permute-start | bytes 393224 | tf_op jit(solution)/shard_map/ppermute | solution.py:369
  14.9 15.5 %collective-permute-start.3 = (bf16[256,256]{1,0:T(8,128)(2,1)S(1)}, bf16[256,256]{1,0:T(8,128)(2,1)S(1)}, u32[]{:S(2)}, u32[]{:S(2)}) collective-permute-start(bf16[256,256]{1,0:T(8,128)(2,1)S(1)} %get-tuple-element.31), channel_id=1, source_target_pairs={{0,20},{4,16},{8,28},{12,24},{16,4},{20,0},{24,12},{28,8},{1,21},{... | collective-permute-start | bytes 393224 | tf_op jit(solution)/shard_map/ppermute | solution.py:369
  18.4 3.5 %copy-start.5 = (bf16[2,512]{1,0:T(2,128)(2,1)S(1)}, bf16[2,512]{1,0:T(2,128)(2,1)}, u32[]{:S(2)}) copy-start(bf16[2,512]{1,0:T(2,128)(2,1)} %az_taps.1) | copy-start | bytes 6148
  19.9 11.4 %collective-permute-start.5 = (bf16[256,256]{1,0:T(8,128)(2,1)S(1)}, bf16[256,256]{1,0:T(8,128)(2,1)S(1)}, u32[]{:S(2)}, u32[]{:S(2)}) collective-permute-start(bf16[256,256]{1,0:T(8,128)(2,1)S(1)} %get-tuple-element.34), channel_id=1, source_target_pairs={{0,28},{4,24},{8,20},{12,16},{16,12},{20,8},{24,4},{28,0},{1,29},{... | collective-permute-start | bytes 393224 | tf_op jit(solution)/shard_map/ppermute | solution.py:369
  20.3 11.4 %collective-permute-start.4 = (bf16[256,256]{1,0:T(8,128)(2,1)S(1)}, bf16[256,256]{1,0:T(8,128)(2,1)S(1)}, u32[]{:S(2)}, u32[]{:S(2)}) collective-permute-start(bf16[256,256]{1,0:T(8,128)(2,1)S(1)} %get-tuple-element.27.after), channel_id=1, source_target_pairs={{0,24},{4,28},{8,16},{12,20},{16,8},{20,12},{24,0},{28,4},{1,25},{... | collective-permute-start | bytes 393224 | tf_op jit(solution)/shard_map/ppermute | solution.py:369
  24.7 12.2 %all-to-all-start = ((bf16[4,256,256]{2,1,0:T(8,128)(2,1)}), bf16[4,256,256]{2,1,0:T(8,128)(2,1)S(1)}, u32[]{:S(2)}, u32[]{:S(2)}) async-start(bf16[4,256,256]{2,1,0:T(8,128)(2,1)} %bitcast.1), calls=%async_computation | async-start | bytes 1048576 | tf_op jit(solution)/shard_map/all_to_all | solution.py:376

commit v5 on v4

--- a/solution.py
+++ b/solution.py
@@ -171,23 +171,27 @@
             )
 
 
-def far_pair(step, samples, range_tiles, bands, turned, outs):
+def group_sends(steps, samples, range_tiles, bands, turned, outs):
     me = lax.axis_index("pulse")
-    first = 4 * (me // 2 ^ step)
-    groups_of(first, 4, [me % 2, me % 2 ^ 1], samples, range_tiles, bands, turned, outs)
-
-
-def first_far_body(step, echoes, near, far, range_tiles, bands, samples, *rest):
+    blocks = GROUP // BLK
+    if len(steps) == 1:
+        first, spots = blocks * (me ^ steps[0]), [0]
+    else:
+        first, spots = 2 * blocks * (me // 2 ^ steps[0] // 2), [me % 2 ^ k % 2 for k in steps]
+    groups_of(first, blocks * len(steps), spots, samples, range_tiles, bands, turned, outs)
+
+
+def first_range_body(steps, echoes, near, far, range_tiles, bands, samples, *rest):
     assemble(echoes, near, far, samples)
-    far_pair(step, samples, range_tiles, bands, rest[-1], rest[:-1])
-
-
-def first_far(step, echoes, near, far, range_tiles, bands):
+    group_sends(steps, samples, range_tiles, bands, rest[-1], rest[:-1])
+
+
+def first_range(steps, echoes, near, far, range_tiles, bands):
     pulses = echoes.shape[1]
     blocks = 1 + echoes.shape[2] // BLK + HEAD
     samples, *made = call(
-        functools.partial(first_far_body, step),
-        "first_far",
+        functools.partial(first_range_body, steps),
+        "first_range",
         (bf16(blocks, pulses, WIDE),) + (bf16(GROUP, 2 * pulses),) * 2,
         [VMEM()] * 5,
         (VMEM(),) * 3,
@@ -196,47 +200,50 @@
     return samples, made
 
 
-def next_far_body(step, samples, range_tiles, bands, *rest):
-    far_pair(step, samples, range_tiles, bands, rest[-1], rest[:-1])
-
-
-def next_far(step, samples, range_tiles, bands):
+def next_range_body(steps, after, samples, range_tiles, bands, *rest):
+    *outs, turned = rest
+    done = row = 0
+    for some in steps:
+        size = len(some) * (GROUP // BLK) + 1
+        group_sends(
+            some,
+            samples,
+            range_tiles,
+            bands,
+            turned.at[pl.ds(row * BLK, size * BLK)],
+            outs[done : done + len(some)],
+        )
+        done, row = done + len(some), row + size
+
+
+def next_range(steps, after, samples, range_tiles, bands):
     pulses = samples.shape[1]
-    return call(
-        functools.partial(next_far_body, step),
-        "next_far",
-        (bf16(GROUP, 2 * pulses),) * 2,
-        [VMEM()] * 3,
-        (VMEM(),) * 2,
-        [pltpu.VMEM((5 * BLK, 2 * pulses), jnp.bfloat16)],
-    )(samples, range_tiles, bands)
-
-
-def near_body(count, after, samples, range_tiles, bands, az_taps, out, az_out, turned):
-    me = lax.axis_index("pulse")
-    groups_of(
-        me // count * count * (GROUP // BLK),
-        count * (GROUP // BLK),
-        list(range(count)),
-        samples,
-        range_tiles,
-        bands,
-        turned,
-        [out],
-    )
+    count = sum(map(len, steps))
+    size = count * (GROUP // BLK) + len(steps)
+    return call(
+        functools.partial(next_range_body, steps),
+        "next_range",
+        (bf16(GROUP, 2 * pulses),) * count,
+        [VMEM()] * 4,
+        (VMEM(),) * count,
+        [pltpu.VMEM((size * BLK, 2 * pulses), jnp.bfloat16)],
+    )(after, samples, range_tiles, bands)
+
+
+def own_range_body(after, samples, range_tiles, bands, az_taps, out, az_out, turned):
+    group_sends([0], samples, range_tiles, bands, turned, [out])
     toeplitz_tiles(az_taps, AZ_TILES, 0, az_out)
 
 
-def near_half(after, samples, range_tiles, bands, azimuth_ref):
+def own_range(after, samples, range_tiles, bands, azimuth_ref):
     pulses = samples.shape[1]
-    count = bands.shape[0] // GROUP // 2
-    return call(
-        functools.partial(near_body, count),
-        "near_half",
-        (bf16(count * GROUP, 2 * pulses), bf16(AZ_TILES, WIDE, WIDE)),
+    return call(
+        own_range_body,
+        "own_range",
+        (bf16(GROUP, 2 * pulses), bf16(AZ_TILES, WIDE, WIDE)),
         [VMEM()] * 5,
         (VMEM(),) * 2,
-        [pltpu.VMEM(((count * (GROUP // BLK) + 1) * BLK, 2 * pulses), jnp.bfloat16)],
+        [pltpu.VMEM((3 * BLK, 2 * pulses), jnp.bfloat16)],
     )(after, samples, range_tiles, bands, azimuth_ref)
 
 
@@ -290,10 +297,7 @@
     reach = AZ_TILES // 2
     me = lax.axis_index("pulse")
     if steps:
-        half = steps[0]
-        start = pl.multiple_of(me // half * half * bins, half * bins)
-        rows[pl.ds(start, half * bins)] = parts[0][...]
-        for part, step in zip(parts[1:], steps[1:]):
+        for part, step in zip(parts, steps):
             rows[pl.ds(pl.multiple_of((me ^ step) * bins, bins), bins)] = part[...]
     else:
         rows[...] = parts[0][...]
@@ -363,26 +367,18 @@
         )
         return focus_azimuth(None, bins, az_tiles, [swapped.reshape(mine.shape)])
 
-    half = peers // 2
-
     def send(piece, k):
         return lax.ppermute(piece, "pulse", [(i, i ^ k) for i in range(peers)])
 
-    samples, made = first_far(half // 2, echoes, near, far, range_tiles, bands)
-    parts = [send(piece, half + k) for k, piece in enumerate(made)]
-    made = next_far(half // 2 + 1, samples, range_tiles, bands)
-    parts += [send(piece, half + 2 + k) for k, piece in enumerate(made)]
-    mine, az_tiles = near_half(made[0], samples, range_tiles, bands, azimuth_ref)
-    mine = lax.all_to_all(
-        mine.reshape(half, bins, WIDE),
-        "pulse",
-        split_axis=0,
-        concat_axis=0,
-        axis_index_groups=[list(range(half)), list(range(half, peers))],
-        tiled=True,
-    ).reshape(mine.shape)
-    parts = gate(gate(parts[:2], (), 500000000) + tuple(parts[2:]), (), 20000000000)
-    return focus_azimuth([half] + list(range(half, peers)), bins, az_tiles, [mine, *parts])
+    samples, made = first_range([4, 5], echoes, near, far, range_tiles, bands)
+    parts = {4: send(made[0], 4), 5: send(made[1], 5)}
+    made = next_range([[6, 7], [1]], made[0], samples, range_tiles, bands)
+    parts.update({k: send(piece, k) for k, piece in zip((6, 7, 1), made)})
+    made = next_range([[2, 3]], made[0], samples, range_tiles, bands)
+    made = gate(made, (parts[4], parts[5]))
+    parts.update({k: send(piece, k) for k, piece in zip((2, 3), made)})
+    parts[0], az_tiles = own_range(made[0], samples, range_tiles, bands, azimuth_ref)
+    return focus_azimuth(list(parts), bins, az_tiles, list(parts.values()))
 
 
 def solution(mesh):

time: 39.4 us -> 38.6 us (0.980)
  the two profiles are of different devices: /device:TPU:18 before, /device:TPU:1 now
where the time goes in v5:
time: 38.6 us; the launch traced here: 38 us
  starting transfers between devices  15.1 us (39%)
  waiting for transfers between devices  11.4 us (30%)
  Pallas kernels  10.1 us (26%)
  local copies, waits for them, and re-layouts  1.25 us (3%)
    ppermute x7, starting transfers between devices, send(): return lax.ppermute(piece, 'pulse', [(i, i ^ k) for i in range(peers)])  10.4 us
    ppermute x1, waiting for transfers between devices, per_device(): far = lax.ppermute(far, 'rng', swaps(1))  6.52 us
    ppermute x7, waiting for transfers between devices, send(): return lax.ppermute(piece, 'pulse', [(i, i ^ k) for i in range(peers)])  4.86 us
    ppermute x1, starting transfers between devices, per_device(): far = lax.ppermute(far, 'rng', swaps(1))  4.6 us
    pallas_call x2, Pallas kernels, next_range(): call(functools.partial(next_range_body, steps), 'next_range', (bf16(GROUP...  3.87 us
    pallas_call x1, Pallas kernels, focus_azimuth(): call(functools.partial(focus_azimuth_body, steps, count), 'focus_azimuth'...  2.23 us
    pallas_call x1, Pallas kernels, first_range(): call(functools.partial(first_range_body, steps), 'first_range', (bf16(blo...  1.66 us
    pallas_call x1, Pallas kernels, prepare(): call(prepare_body, 'prepare', (bf16(RANGE_TILES, WIDE, WIDE), bf16(weight...  1.28 us
  transfers between devices with their start and end apart: 9, of which 5 were waited for; matrix products, arithmetic and copies ran while one was open for 0% of the time, Pallas kernels for 16%

profile of v5, /device:TPU:1, one launch (start us, length us, event | category | flops | bytes accessed | tf_op | source)
XLA Modules:
  0.0 38.0 jit_solution(14543831837153355221)
XLA Ops:
  0.0 0.0 copy-start
  0.0 1.2 %copy-done = bf16[2,128,2048]{2,1,0:T(8,128)(2,1)S(1)} copy-done((bf16[2,128,2048]{2,1,0:T(8,128)(2,1)S(1)}, bf16[2,128,2048]{2,1,0:T(8,128)(2,1)}, u32[]{:S(2)}) %copy-start) | copy-done | bytes 1048600
  1.2 0.0 copy-start.2
  1.2 0.0 copy-start.3
  1.2 0.0 copy-start.4
  1.2 0.0 copy-start.1
  1.2 0.1 pack.1
  1.4 0.1 collective-permute-start
  1.5 4.6 %collective-permute-start.1 = (bf16[9,128,256]{2,1,0:T(8,128)(2,1)S(1)}, bf16[9,128,256]{2,1,0:T(8,128)(2,1)S(1)}, u32[]{:S(2)}, u32[]{:S(2)}) collective-permute-start(bf16[9,128,256]{2,1,0:T(8,128)(2,1)S(1)} %get-tuple-element.22), channel_id=1, source_target_pairs={{1,2},{2,1},{5,6},{6,5},{9,10},{10,9},{13,14},{14,13},{17,18},{18,... | collective-permute-start | bytes 1769480 | tf_op jit(solution)/shard_map/ppermute | solution.py:359
  6.1 0.0 copy-done.2
  6.1 0.0 copy-done.3
  6.1 0.0 copy-done.4
  6.1 1.3 %prepare.1 = (bf16[10,256,256]{2,1,0:T(8,128)(2,1)S(1)}, bf16[2048,256]{1,0:T(8,128)(2,1)S(1)}) custom-call(bf16[2,1024]{1,0:T(2,128)(2,1)S(1)} %copy-done.4, bf16[64,2048]{1,0:T(8,128)(2,1)S(1)} %copy-done.2, s32[16,128]{1,0:T(8,128)S(1)} %bitcast.1), custom_call_target="tpu_custom_call" | custom-call | tf_op jit(solution)/shard_map/prepare/pallas_call | solution.py:119
  7.4 0.0 collective-permute-done.near
  7.4 6.5 %collective-permute-done.1.far = bf16[9,128,256]{2,1,0:T(8,128)(2,1)S(1)} collective-permute-done((bf16[9,128,256]{2,1,0:T(8,128)(2,1)S(1)}, bf16[9,128,256]{2,1,0:T(8,128)(2,1)S(1)}, u32[]{:S(2)}, u32[]{:S(2)}) %collective-permute-start.1) | collective-permute-done | bytes 589856 | tf_op jit(solution)/shard_map/ppermute | solution.py:359
  14.0 0.0 copy-done.1
  14.0 1.7 %first_range.1 = (bf16[26,128,256]{2,1,0:T(8,128)(2,1)S(1)}, bf16[256,256]{1,0:T(8,128)(2,1)S(1)}, bf16[256,256]{1,0:T(8,128)(2,1)S(1)}) custom-call(bf16[2,128,2048]{2,1,0:T(8,128)(2,1)S(1)} %copy-done.1, bf16[9,128,256]{2,1,0:T(8,128)(2,1)S(1)} %collective-permute-done.near, bf16[9,128,256]{2,1,0:T(8,128)(2,1)S(1)} %collective-permute-done.1.far, ...), custom_call_target="tpu_custom_call" | custom-call | tf_op jit(solution)/shard_map/first_range/pallas_call | solution.py:192
  15.6 3.5 %collective-permute-start.3 = (bf16[256,256]{1,0:T(8,128)(2,1)S(1)}, bf16[256,256]{1,0:T(8,128)(2,1)S(1)}, u32[]{:S(2)}, u32[]{:S(2)}) collective-permute-start(bf16[256,256]{1,0:T(8,128)(2,1)S(1)} %get-tuple-element.30), channel_id=1, source_target_pairs={{0,20},{4,16},{8,28},{12,24},{16,4},{20,0},{24,12},{28,8},{1,21},{... | collective-permute-start | bytes 393224 | tf_op jit(solution)/shard_map/ppermute | solution.py:371
  19.1 0.4 collective-permute-start.2
  19.5 2.4 %next_range.2 = (bf16[256,256]{1,0:T(8,128)(2,1)S(1)}, bf16[256,256]{1,0:T(8,128)(2,1)S(1)}, bf16[256,256]{1,0:T(8,128)(2,1)S(1)}) custom-call(bf16[256,256]{1,0:T(8,128)(2,1)S(1)} %get-tuple-element.25.after, bf16[26,128,256]{2,1,0:T(8,128)(2,1)S(1)} %get-tuple-element.26.samples, bf16[10,256,256]{2,1,0:T(8,128)(2,1)S(1)} %get-tuple-element.23.range_tiles, ...), custom_call_target="tpu_custom_call" | custom-call | tf_op jit(solution)/shard_map/next_range/pallas_call | solution.py:223
  21.9 0.0 copy-start.5
  22.0 3.4 %collective-permute-start.4 = (bf16[256,256]{1,0:T(8,128)(2,1)S(1)}, bf16[256,256]{1,0:T(8,128)(2,1)S(1)}, u32[]{:S(2)}, u32[]{:S(2)}) collective-permute-start(bf16[256,256]{1,0:T(8,128)(2,1)S(1)} %get-tuple-element.27.after), channel_id=1, source_target_pairs={{0,24},{4,28},{8,16},{12,20},{16,8},{20,12},{24,0},{28,4},{1,25},{... | collective-permute-start | bytes 393224 | tf_op jit(solution)/shard_map/ppermute | solution.py:371
  25.3 1.4 %next_range.3 = (bf16[256,256]{1,0:T(8,128)(2,1)S(1)}, bf16[256,256]{1,0:T(8,128)(2,1)S(1)}) custom-call(bf16[256,256]{1,0:T(8,128)(2,1)S(1)} %get-tuple-element.27.after, bf16[26,128,256]{2,1,0:T(8,128)(2,1)S(1)} %get-tuple-element.26.samples, bf16[10,256,256]{2,1,0:T(8,128)(2,1)S(1)} %get-tuple-element.23.range_tiles, ...), custom_call_target="tpu_custom_call" | custom-call | tf_op jit(solution)/shard_map/next_range/pallas_call | solution.py:223
  26.8 0.1 collective-permute-start.5
  26.9 1.2 %collective-permute-start.6 = (bf16[256,256]{1,0:T(8,128)(2,1)S(1)}, bf16[256,256]{1,0:T(8,128)(2,1)S(1)}, u32[]{:S(2)}, u32[]{:S(2)}) collective-permute-start(bf16[256,256]{1,0:T(8,128)(2,1)S(1)} %get-tuple-element.34), channel_id=1, source_target_pairs={{0,4},{4,0},{8,12},{12,8},{16,20},{20,16},{24,28},{28,24},{1,5},{5... | collective-permute-start | bytes 393224 | tf_op jit(solution)/shard_map/ppermute | solution.py:371
  28.0 0.0 collective-permute-done.3.refs_3_.rest_1_
  28.0 2.1 %collective-permute-done.2.refs_2_.rest_0_ = bf16[256,256]{1,0:T(8,128)(2,1)S(1)} collective-permute-done((bf16[256,256]{1,0:T(8,128)(2,1)S(1)}, bf16[256,256]{1,0:T(8,128)(2,1)S(1)}, u32[]{:S(2)}, u32[]{:S(2)}) %collective-permute-start.2) | collective-permute-done | bytes 131104 | tf_op jit(solution)/shard_map/ppermute | solution.py:371
  30.1 1.8 %collective-permute-start.8 = (bf16[256,256]{1,0:T(8,128)(2,1)S(1)}, bf16[256,256]{1,0:T(8,128)(2,1)S(1)}, u32[]{:S(2)}, u32[]{:S(2)}) collective-permute-start(bf16[256,256]{1,0:T(8,128)(2,1)S(1)} %get-tuple-element.35), channel_id=1, source_target_pairs={{0,12},{4,8},{8,4},{12,0},{16,28},{20,24},{24,20},{28,16},{1,13},{... | collective-permute-start | bytes 393224 | tf_op jit(solution)/shard_map/ppermute | solution.py:371
  31.9 0.1 collective-permute-start.7
  32.0 0.0 copy-done.5
  32.0 0.9 %own_range.1 = (bf16[256,256]{1,0:T(8,128)(2,1)S(1)}, bf16[5,256,256]{2,1,0:T(8,128)(2,1)S(1)}) custom-call(bf16[256,256]{1,0:T(8,128)(2,1)S(1)} %get-tuple-element.31.after, bf16[26,128,256]{2,1,0:T(8,128)(2,1)S(1)} %get-tuple-element.26.samples, bf16[10,256,256]{2,1,0:T(8,128)(2,1)S(1)} %get-tuple-element.23.range_tiles, ...), custom_call_target="tpu_custom_call" | custom-call | tf_op jit(solution)/shard_map/own_range/pallas_call | solution.py:240
  32.9 0.5 %collective-permute-done.5.rest_3_ = bf16[256,256]{1,0:T(8,128)(2,1)S(1)} collective-permute-done((bf16[256,256]{1,0:T(8,128)(2,1)S(1)}, bf16[256,256]{1,0:T(8,128)(2,1)S(1)}, u32[]{:S(2)}, u32[]{:S(2)}) %collective-permute-start.5) | collective-permute-done | bytes 131104 | tf_op jit(solution)/shard_map/ppermute | solution.py:371
  33.5 0.0 collective-permute-done.6.rest_4_
  33.5 0.0 collective-permute-done.4.rest_2_
  33.5 1.4 %collective-permute-done.8.rest_6_ = bf16[256,256]{1,0:T(8,128)(2,1)S(1)} collective-permute-done((bf16[256,256]{1,0:T(8,128)(2,1)S(1)}, bf16[256,256]{1,0:T(8,128)(2,1)S(1)}, u32[]{:S(2)}, u32[]{:S(2)}) %collective-permute-start.8) | collective-permute-done | bytes 131104 | tf_op jit(solution)/shard_map/ppermute | solution.py:371
  34.9 0.9 %collective-permute-done.7.rest_5_ = bf16[256,256]{1,0:T(8,128)(2,1)S(1)} collective-permute-done((bf16[256,256]{1,0:T(8,128)(2,1)S(1)}, bf16[256,256]{1,0:T(8,128)(2,1)S(1)}, u32[]{:S(2)}, u32[]{:S(2)}) %collective-permute-start.7) | collective-permute-done | bytes 131104 | tf_op jit(solution)/shard_map/ppermute | solution.py:371
  35.7 2.2 %focus_azimuth.1 = f32[2,1,256,1024]{3,2,1,0:T(8,128)} custom-call(bf16[5,256,256]{2,1,0:T(8,128)(2,1)S(1)} %get-tuple-element.32.az_tiles, bf16[256,256]{1,0:T(8,128)(2,1)S(1)} %collective-permute-done.2.refs_2_.rest_0_, bf16[256,256]{1,0:T(8,128)(2,1)S(1)} %collective-permute-done.3.refs_3_.rest_1_, bf16[256,256]{1,0:T(8,128)(2,1)S(1)} %collective-permute-done.4.rest_2_, ...), custom_call_target="tpu_custom_call" | custom-call | tf_op jit(solution)/shard_map/focus_azimuth/pallas_call | solution.py:334
  (1 shorter events, 0.0 us)
Async XLA Ops:
  0.0 1.2 %copy-start = (bf16[2,128,2048]{2,1,0:T(8,128)(2,1)S(1)}, bf16[2,128,2048]{2,1,0:T(8,128)(2,1)}, u32[]{:S(2)}) copy-start(bf16[2,128,2048]{2,1,0:T(8,128)(2,1)} %echoes.3) | copy-start | bytes 3145732
  1.2 4.9 %copy-start.2 = (bf16[64,2048]{1,0:T(8,128)(2,1)S(1)}, bf16[64,2048]{1,0:T(8,128)(2,1)}, u32[]{:S(2)}) copy-start(bf16[64,2048]{1,0:T(8,128)(2,1)} %weights.1) | copy-start | bytes 786436
  1.2 4.9 %copy-start.3 = (s32[2048]{0:T(1024)S(1)}, s32[2048]{0:T(1024)}, u32[]{:S(2)}) copy-start(s32[2048]{0:T(1024)} %param.8) | copy-start | bytes 24580
  1.2 4.9 %copy-start.4 = (bf16[2,1024]{1,0:T(2,128)(2,1)S(1)}, bf16[2,1024]{1,0:T(2,128)(2,1)}, u32[]{:S(2)}) copy-start(bf16[2,1024]{1,0:T(2,128)(2,1)} %range_ref.1) | copy-start | bytes 12292
  1.2 12.7 %copy-start.1 = (bf16[2,128,2048]{2,1,0:T(8,128)(2,1)S(1)}, bf16[2,128,2048]{2,1,0:T(8,128)(2,1)}, u32[]{:S(2)}) copy-start(bf16[2,128,2048]{2,1,0:T(8,128)(2,1)} %echoes.3) | copy-start | bytes 3145732
  1.4 6.0 %collective-permute-start = (bf16[9,128,256]{2,1,0:T(8,128)(2,1)S(1)}, bf16[9,128,256]{2,1,0:T(8,128)(2,1)S(1)}, u32[]{:S(2)}, u32[]{:S(2)}) collective-permute-start(bf16[9,128,256]{2,1,0:T(8,128)(2,1)S(1)} %get-tuple-element.21), channel_id=1, source_target_pairs={{0,1},{2,3},{1,0},{3,2},{4,5},{6,7},{5,4},{7,6},{8,9},{10,11},{9,8... | collective-permute-start | bytes 1769480 | tf_op jit(solution)/shard_map/ppermute | solution.py:360
  1.5 12.5 %collective-permute-start.1 = (bf16[9,128,256]{2,1,0:T(8,128)(2,1)S(1)}, bf16[9,128,256]{2,1,0:T(8,128)(2,1)S(1)}, u32[]{:S(2)}, u32[]{:S(2)}) collective-permute-start(bf16[9,128,256]{2,1,0:T(8,128)(2,1)S(1)} %get-tuple-element.22), channel_id=1, source_target_pairs={{1,2},{2,1},{5,6},{6,5},{9,10},{10,9},{13,14},{14,13},{17,18},{18,... | collective-permute-start | bytes 1769480 | tf_op jit(solution)/shard_map/ppermute | solution.py:359
  15.6 12.4 %collective-permute-start.3 = (bf16[256,256]{1,0:T(8,128)(2,1)S(1)}, bf16[256,256]{1,0:T(8,128)(2,1)S(1)}, u32[]{:S(2)}, u32[]{:S(2)}) collective-permute-start(bf16[256,256]{1,0:T(8,128)(2,1)S(1)} %get-tuple-element.30), channel_id=1, source_target_pairs={{0,20},{4,16},{8,28},{12,24},{16,4},{20,0},{24,12},{28,8},{1,21},{... | collective-permute-start | bytes 393224 | tf_op jit(solution)/shard_map/ppermute | solution.py:371
  19.1 11.0 %collective-permute-start.2 = (bf16[256,256]{1,0:T(8,128)(2,1)S(1)}, bf16[256,256]{1,0:T(8,128)(2,1)S(1)}, u32[]{:S(2)}, u32[]{:S(2)}) collective-permute-start(bf16[256,256]{1,0:T(8,128)(2,1)S(1)} %get-tuple-element.25.after), channel_id=1, source_target_pairs={{0,16},{4,20},{8,24},{12,28},{16,0},{20,4},{24,8},{28,12},{1,17},{... | collective-permute-start | bytes 393224 | tf_op jit(solution)/shard_map/ppermute | solution.py:371
  21.9 10.0 %copy-start.5 = (bf16[2,512]{1,0:T(2,128)(2,1)S(1)}, bf16[2,512]{1,0:T(2,128)(2,1)}, u32[]{:S(2)}) copy-start(bf16[2,512]{1,0:T(2,128)(2,1)} %az_taps.1) | copy-start | bytes 6148
  22.0 11.5 %collective-permute-start.4 = (bf16[256,256]{1,0:T(8,128)(2,1)S(1)}, bf16[256,256]{1,0:T(8,128)(2,1)S(1)}, u32[]{:S(2)}, u32[]{:S(2)}) collective-permute-start(bf16[256,256]{1,0:T(8,128)(2,1)S(1)} %get-tuple-element.27.after), channel_id=1, source_target_pairs={{0,24},{4,28},{8,16},{12,20},{16,8},{20,12},{24,0},{28,4},{1,25},{... | collective-permute-start | bytes 393224 | tf_op jit(solution)/shard_map/ppermute | solution.py:371
  26.8 6.7 %collective-permute-start.5 = (bf16[256,256]{1,0:T(8,128)(2,1)S(1)}, bf16[256,256]{1,0:T(8,128)(2,1)S(1)}, u32[]{:S(2)}, u32[]{:S(2)}) collective-permute-start(bf16[256,256]{1,0:T(8,128)(2,1)S(1)} %get-tuple-element.33), channel_id=1, source_target_pairs={{0,28},{4,24},{8,20},{12,16},{16,12},{20,8},{24,4},{28,0},{1,29},{... | collective-permute-start | bytes 393224 | tf_op jit(solution)/shard_map/ppermute | solution.py:371
  26.9 6.6 %collective-permute-start.6 = (bf16[256,256]{1,0:T(8,128)(2,1)S(1)}, bf16[256,256]{1,0:T(8,128)(2,1)S(1)}, u32[]{:S(2)}, u32[]{:S(2)}) collective-permute-start(bf16[256,256]{1,0:T(8,128)(2,1)S(1)} %get-tuple-element.34), channel_id=1, source_target_pairs={{0,4},{4,0},{8,12},{12,8},{16,20},{20,16},{24,28},{28,24},{1,5},{5... | collective-permute-start | bytes 393224 | tf_op jit(solution)/shard_map/ppermute | solution.py:371
  30.1 4.8 %collective-permute-start.8 = (bf16[256,256]{1,0:T(8,128)(2,1)S(1)}, bf16[256,256]{1,0:T(8,128)(2,1)S(1)}, u32[]{:S(2)}, u32[]{:S(2)}) collective-permute-start(bf16[256,256]{1,0:T(8,128)(2,1)S(1)} %get-tuple-element.35), channel_id=1, source_target_pairs={{0,12},{4,8},{8,4},{12,0},{16,28},{20,24},{24,20},{28,16},{1,13},{... | collective-permute-start | bytes 393224 | tf_op jit(solution)/shard_map/ppermute | solution.py:371
  31.9 3.8 %collective-permute-start.7 = (bf16[256,256]{1,0:T(8,128)(2,1)S(1)}, bf16[256,256]{1,0:T(8,128)(2,1)S(1)}, u32[]{:S(2)}, u32[]{:S(2)}) collective-permute-start(bf16[256,256]{1,0:T(8,128)(2,1)S(1)} %get-tuple-element.31.after), channel_id=1, source_target_pairs={{0,8},{4,12},{8,0},{12,4},{16,24},{20,28},{24,16},{28,20},{1,9},{5... | collective-permute-start | bytes 393224 | tf_op jit(solution)/shard_map/ppermute | solution.py:371

commit v6 on v5

v6 whole, which is shorter than its diff:
```python
import functools

import jax
import jax.numpy as jnp
from jax import lax
from jax.experimental import pallas as pl
from jax.experimental.pallas import tpu as pltpu
from jax.sharding import PartitionSpec as P

RT = 1024
AT = 512
BAND = 64
BLK = 128
HALF = BLK // 2
WIDE = 2 * BLK
RANGE_TILES = RT // BLK + 2
AZ_TILES = AT // BLK + 1
HEAD = RT // BLK + 1
GROUP = 2 * BLK
LIMIT = 24 * 1024 * 1024
PACK_FLOPS = 2 * 10**9

VMEM = functools.partial(pl.BlockSpec, memory_space=pltpu.VMEM)
HBM = functools.partial(pl.BlockSpec, memory_space=pltpu.HBM)


def call(body, name, out_shape, in_specs, out_specs, scratch_shapes=(), flops=0):
    return pl.pallas_call(
        body,
        out_shape=out_shape,
        in_specs=in_specs,
        out_specs=out_specs,
        scratch_shapes=scratch_shapes,
        compiler_params=pltpu.CompilerParams(vmem_limit_bytes=LIMIT),
        cost_estimate=pl.CostEstimate(flops=flops, bytes_accessed=0, transcendentals=0),
        name=name,
    )


def bf16(*shape):
    return jax.ShapeDtypeStruct(shape, jnp.bfloat16)


def pack_body(echoes, near, down, up):
    odd = lax.axis_index("rng") % 2 == 1

    def fill(first, last):
        for part in range(2):
            lanes = slice(part * BLK, (part + 1) * BLK)
            for block in range(HEAD):
                first[block, :, lanes] = echoes[part, :, block * BLK : (block + 1) * BLK]
            last[0, :, lanes] = echoes[part, :, echoes.shape[2] - BLK :]

    pl.when(odd)(lambda: fill(near, up))
    pl.when(jnp.logical_not(odd))(lambda: fill(down, near))


def pack(echoes):
    pulses = echoes.shape[1]
    return call(
        pack_body,
        "pack",
        (bf16(HEAD, pulses, WIDE),) * 2 + (bf16(1, pulses, WIDE),),
        [VMEM()],
        (VMEM(),) * 3,
        flops=PACK_FLOPS,
    )(echoes)


def toeplitz_tiles(taps, tiles, shift, out):
    width = (tiles + 1) * BLK
    tap_total = taps.shape[1]
    skewed = []
    for part in range(2):
        row = jnp.concatenate(
            [
                jnp.zeros((1, BLK), jnp.float32),
                taps[part : part + 1, :].astype(jnp.float32),
                jnp.zeros((1, width - BLK - tap_total), jnp.float32),
            ],
            axis=1,
        )
        row = jnp.broadcast_to(row, (BLK, width))
        skewed.append(pltpu.roll(row, shift, 1, stride=1, stride_axis=0))
    for tile in range(tiles):
        span = slice((tile + 1) * BLK, (tile + 2) * BLK)
        real = skewed[0][:, span].T
        imag = skewed[1][:, span].T
        out[tile, :BLK, :BLK] = real.astype(jnp.bfloat16)
        out[tile, :BLK, BLK:] = (-imag).astype(jnp.bfloat16)
        out[tile, BLK:, :BLK] = imag.astype(jnp.bfloat16)
        out[tile, BLK:, BLK:] = real.astype(jnp.bfloat16)


def prepare_body(range_ref, range_out):
    toeplitz_tiles(range_ref, RANGE_TILES, HALF, range_out)


def prepare(range_ref):
    return call(
        prepare_body, "prepare", bf16(RANGE_TILES, WIDE, WIDE), [VMEM()], VMEM()
    )(range_ref)


def band(weights, offsets, block):
    span = pl.ds(pl.multiple_of(block * BLK, BLK), BLK)
    placed = jnp.concatenate(
        [weights[:, span].astype(jnp.float32), jnp.zeros((BLK - BAND, BLK), jnp.float32)], axis=0
    )
    shifts = offsets[pl.ds(block, 1), :]
    for bit in range((BAND // 2).bit_length()):
        chosen = jnp.broadcast_to((shifts >> bit) & 1, (BLK, BLK)) == 1
        placed = jnp.where(chosen, pltpu.roll(placed, 1 << bit, 0), placed)
    wide = jnp.concatenate([placed.T, jnp.zeros((BLK, BLK), jnp.float32)], axis=1)
    skewed = pltpu.roll(wide, BAND // 2, 1, stride=1, stride_axis=0)
    outside = (lax.axis_index("rng") == 0) & (block == 0)
    lane = lax.broadcasted_iota(jnp.int32, (BLK, WIDE), 1)
    return jnp.where(outside & (lane < HALF), 0.0, skewed).astype(jnp.bfloat16)


def assemble(echoes, near, down, up, out):
    blocks = echoes.shape[2] // BLK
    for block in range(blocks):
        for part in range(2):
            out[block + 1, :, part * BLK : (part + 1) * BLK] = echoes[
                part, :, block * BLK : (block + 1) * BLK
            ]

    def ends(low, high):
        out[0] = low[0]
        out[blocks + 1 :] = high[...]

    odd = lax.axis_index("rng") % 2 == 1
    pl.when(odd)(lambda: ends(near, down))
    pl.when(jnp.logical_not(odd))(lambda: ends(up, near))


def compress(samples, range_tiles, block):
    window = jnp.concatenate([samples[block + tile] for tile in range(RANGE_TILES)], axis=1)
    total = jnp.dot(
        window,
        range_tiles[...].reshape(RANGE_TILES * WIDE, WIDE),
        preferred_element_type=jnp.float32,
    ).astype(jnp.bfloat16)
    return jnp.concatenate([total[:, :BLK].T, total[:, BLK:].T], axis=1)


def migrate(weights, offsets, turned, first, place):
    reach = pl.multiple_of(place * BLK, BLK)
    return jnp.dot(
        band(weights, offsets, first + place),
        turned[pl.ds(reach, WIDE)],
        preferred_element_type=jnp.float32,
    ).astype(jnp.bfloat16)


def groups_of(first, count, spots, samples, range_tiles, weights, offsets, turned, outs):
    for block in range(count + 1):
        turned[block * BLK : (block + 1) * BLK, :] = compress(samples, range_tiles, first + block)
    rows = [out.at[pl.ds(i, GROUP)] for out in outs for i in range(0, out.shape[0], GROUP)]
    for spot, out in zip(spots, rows):
        for block in range(GROUP // BLK):
            out[block * BLK : (block + 1) * BLK, :] = migrate(
                weights, offsets, turned, first, spot * (GROUP // BLK) + block
            )


def group_sends(steps, samples, range_tiles, weights, offsets, turned, outs):
    me = lax.axis_index("pulse")
    blocks = GROUP // BLK
    if len(steps) == 1:
        first, spots = blocks * (me ^ steps[0]), [0]
    else:
        first, spots = 2 * blocks * (me // 2 ^ steps[0] // 2), [me % 2 ^ k % 2 for k in steps]
    groups_of(first, blocks * len(steps), spots, samples, range_tiles, weights, offsets, turned, outs)


def first_range_body(steps, echoes, near, down, up, range_tiles, weights, offsets, samples, *rest):
    assemble(echoes, near, down, up, samples)
    group_sends(steps, samples, range_tiles, weights, offsets, rest[-1], rest[:-1])


def first_range(steps, echoes, near, down, up, range_tiles, weights, offsets):
    pulses = echoes.shape[1]
    blocks = 1 + echoes.shape[2] // BLK + HEAD
    samples, *made = call(
        functools.partial(first_range_body, steps),
        "first_range",
        (bf16(blocks, pulses, WIDE),) + (bf16(GROUP, 2 * pulses),) * len(steps),
        [VMEM()] * 7,
        (VMEM(),) * (1 + len(steps)),
        [pltpu.VMEM((5 * BLK, 2 * pulses), jnp.bfloat16)],
    )(echoes, near, down, up, range_tiles, weights, offsets)
    return samples, made


def next_range_body(steps, after, samples, range_tiles, weights, offsets, *rest):
    *outs, turned = rest
    done = row = 0
    for some in steps:
        size = len(some) * (GROUP // BLK) + 1
        group_sends(
            some,
            samples,
            range_tiles,
            weights,
            offsets,
            turned.at[pl.ds(row * BLK, size * BLK)],
            outs[done : done + len(some)],
        )
        done, row = done + len(some), row + size


def next_range(steps, after, samples, range_tiles, weights, offsets):
    pulses = samples.shape[1]
    count = sum(map(len, steps))
    size = count * (GROUP // BLK) + len(steps)
    return call(
        functools.partial(next_range_body, steps),
        "next_range",
        (bf16(GROUP, 2 * pulses),) * count,
        [VMEM()] * 5,
        (VMEM(),) * count,
        [pltpu.VMEM((size * BLK, 2 * pulses), jnp.bfloat16)],
    )(after, samples, range_tiles, weights, offsets)


def own_range_body(after, samples, range_tiles, weights, offsets, az_taps, out, az_out, turned):
    group_sends([0], samples, range_tiles, weights, offsets, turned, [out])
    toeplitz_tiles(az_taps, AZ_TILES, 0, az_out)


def own_range(after, samples, range_tiles, weights, offsets, azimuth_ref):
    pulses = samples.shape[1]
    return call(
        own_range_body,
        "own_range",
        (bf16(GROUP, 2 * pulses), bf16(AZ_TILES, WIDE, WIDE)),
        [VMEM()] * 6,
        (VMEM(),) * 2,
        [pltpu.VMEM((3 * BLK, 2 * pulses), jnp.bfloat16)],
    )(after, samples, range_tiles, weights, offsets, azimuth_ref)


def gate_body(*refs):
    pass


def gate(values, after=(), flops=0):
    whole = pl.BlockSpec(memory_space=pl.ANY)
    values = list(values)
    return pl.pallas_call(
        gate_body,
        out_shape=tuple(jax.ShapeDtypeStruct(value.shape, value.dtype) for value in values),
        in_specs=[whole] * (len(values) + len(after)),
        out_specs=(whole,) * len(values),
        input_output_aliases={i: i for i in range(len(values))},
        compiler_params=pltpu.CompilerParams(vmem_limit_bytes=LIMIT),
        cost_estimate=pl.CostEstimate(flops=flops, bytes_accessed=0, transcendentals=0),
        name="gate",
    )(*values, *after)


def whole_body(count, echoes, near, down, up, range_tiles, weights, offsets, az_taps, out, az_out, samples, turned):
    assemble(echoes, near, down, up, samples)
    for block in range(count + 1):
        turned[block * BLK : (block + 1) * BLK, :] = compress(samples, range_tiles, block)
    for block in range(count):
        out[block * BLK : (block + 1) * BLK, :] = migrate(weights, offsets, turned, 0, block)
    toeplitz_tiles(az_taps, AZ_TILES, 0, az_out)


def whole_quarter(echoes, near, down, up, range_tiles, weights, offsets, azimuth_ref):
    pulses = echoes.shape[1]
    count = weights.shape[1] // BLK
    return call(
        functools.partial(whole_body, count),
        "whole_quarter",
        (bf16(count * BLK, 2 * pulses), bf16(AZ_TILES, WIDE, WIDE)),
        [VMEM()] * 8,
        (VMEM(),) * 2,
        [
            pltpu.VMEM((1 + count + HEAD, pulses, WIDE), jnp.bfloat16),
            pltpu.VMEM(((count + 1) * BLK, 2 * pulses), jnp.bfloat16),
        ],
    )(echoes, near, down, up, range_tiles, weights, offsets, azimuth_ref)


def azimuth_rows(bins, steps, parts, rows):
    me = lax.axis_index("pulse")
    for part, step in zip(parts, steps):
        rows[pl.ds(pl.multiple_of((me ^ step) * bins, bins), bins)] = part[...]


def azimuth_blocks(bins, count, rows, az_tiles, image, done=lambda block: None):
    reach = AZ_TILES // 2
    for block in range(count):
        low, high = max(0, reach - block), min(AZ_TILES, count + reach - block)
        window = jnp.concatenate(
            [
                rows[(block + tile - reach) * bins : (block + tile - reach + 1) * bins]
                for tile in range(low, high)
            ],
            axis=1,
        )
        total = jnp.dot(
            window,
            az_tiles[low:high].reshape((high - low) * WIDE, WIDE),
            preferred_element_type=jnp.float32,
        )
        for part in range(2):
            image[part, 0, :, block * BLK : (block + 1) * BLK] = total[
                :, part * BLK : (part + 1) * BLK
            ]
        done(block)


def column(image, out, sems, block):
    span = pl.ds(pl.multiple_of(block * BLK, BLK), BLK)
    return pltpu.make_async_copy(image.at[:, :, :, span], out.at[:, :, :, span], sems.at[block])


def azimuth_body(steps, az_tiles, *rest):
    *parts, out, rows, image, sems = rest
    bins = image.shape[2]
    count = image.shape[3] // BLK
    if steps:
        azimuth_rows(bins, steps, parts, rows)
    else:
        rows[...] = parts[0][...]
    azimuth_blocks(
        bins,
        count,
        rows,
        az_tiles,
        image,
        lambda block: column(image, out, sems, block).start(),
    )
    for block in range(count):
        column(image, out, sems, block).wait()


def azimuth(steps, count, az_tiles, parts):
    bins = sum(part.shape[0] for part in parts) // count
    shape = (2, 1, bins, count * BLK)
    return call(
        functools.partial(azimuth_body, steps),
        "azimuth",
        jax.ShapeDtypeStruct(shape, jnp.float32),
        [VMEM()] * (1 + len(parts)),
        HBM(),
        [
            pltpu.VMEM((count * bins, WIDE), jnp.bfloat16),
            pltpu.VMEM(shape, jnp.float32),
            pltpu.SemaphoreType.DMA((count,)),
        ],
    )(az_tiles, *parts)


def per_device(echoes, range_ref, band_weights, band_offsets, azimuth_ref):
    quarter_len = echoes.shape[2]
    peers = lax.axis_size("pulse")
    quarters = lax.axis_size("rng")
    bins = quarter_len // peers
    near, down, up = pack(echoes)
    cores = [(i, i + 1) for i in range(0, quarters - 1, 2)]
    chips = [(i, i + 1) for i in range(1, quarters - 1, 2)]
    near = lax.ppermute(near, "rng", cores + [(j, i) for i, j in cores])
    down = lax.ppermute(down, "rng", [(j, i) for i, j in chips])
    up = lax.ppermute(up, "rng", chips)
    range_tiles = prepare(range_ref)
    weights, offsets = band_weights, band_offsets.reshape(-1, BLK)

    if bins != GROUP or peers != 8:
        mine, az_tiles = whole_quarter(echoes, near, down, up, range_tiles, weights, offsets, azimuth_ref)
        swapped = lax.all_to_all(
            mine.reshape(peers, bins, WIDE), "pulse", split_axis=0, concat_axis=0, tiled=True
        )
        return azimuth(None, peers, az_tiles, [swapped.reshape(mine.shape)])

    def send(piece, k):
        return lax.ppermute(piece, "pulse", [(i, i ^ k) for i in range(peers)])

    samples, made = first_range([4, 5], echoes, near, down, up, range_tiles, weights, offsets)
    parts = {k: send(piece, k) for k, piece in zip([4, 5], made)}
    for some in [[6, 7]]:
        made = next_range([some], made[0], samples, range_tiles, weights, offsets)
        parts.update({k: send(piece, k) for k, piece in zip(some, made)})
    ready = {}
    for some in [[2, 3], [1]]:
        made = next_range([some], made[0], samples, range_tiles, weights, offsets)
        ready.update(zip(some, made))
    parts[3] = send(ready[3], 3)
    parts[1] = send(gate([ready[1]], (parts[5],))[0], 1)
    parts[2] = send(gate([ready[2]], (parts[4],))[0], 2)
    parts[0], az_tiles = own_range(made[0], samples, range_tiles, weights, offsets, azimuth_ref)
    held = gate((parts[6], parts[7]), (), 1000000000) + (parts[3],)
    parts.update(zip((6, 7, 3), gate(held, (), 2 * 10**8)))
    return azimuth(list(parts), peers, az_tiles, list(parts.values()))


def solution(mesh):
    return jax.shard_map(
        per_device,
        mesh=mesh,
        in_specs=(P(None, "pulse", "rng"), P(), P(None, "rng"), P("rng"), P()),
        out_specs=P(None, "rng", "pulse", None),
        check_vma=False,
    )
```

time: 38.6 us -> 37.3 us (0.966); the launches traced: 38 us -> 37.1 us
  waiting for transfers between devices: 11.4 us -> 7.36 us
  starting transfers between devices: 15.1 us -> 18.5 us
    ppermute x7, waiting for transfers between devices: 4.86 us -> 2.36 us  [send(): return lax.ppermute(piece, 'pulse', [(i, i ^ k) for i in range(peers)])]
    ppermute x7, starting transfers between devices: 10.4 us -> 12.5 us  [send(): return lax.ppermute(piece, 'pulse', [(i, i ^ k) for i in range(peers)])]
    ppermute x2 -> x3, waiting for transfers between devices: 6.52 us -> 5 us  [the longest x1 4.28 us: per_device(): down = lax.ppermute(down, 'rng', [(j, i) for i, j in chips])]
    ppermute x2 -> x3, starting transfers between devices: 4.72 us -> 6.04 us  [the longest x1 4.51 us: per_device(): up = lax.ppermute(up, 'rng', chips)]
    pallas_call x3, Pallas kernels: 3.64 us -> 2.93 us  [the longest x1 2.24 us: azimuth(): call(functools.partial(azimuth_body, steps), 'azimuth', jax.ShapeDtypeStr...]
    pallas_call x2 -> x3, Pallas kernels: 3.87 us -> 4.09 us  [next_range(): call(functools.partial(next_range_body, steps), 'next_range', (bf16(GROUP...]
  transfers between devices with their start and end apart: 9 -> 10, of which waited for: 5 -> 5; matrix products, arithmetic and copies ran while one was open for 0% -> 0% of each run, Pallas kernels for 16% -> 15%
where the time goes in v6:
time: 37.3 us; the launch traced here: 37.1 us
  starting transfers between devices  18.5 us (50%)
  Pallas kernels  9.8 us (26%)
  waiting for transfers between devices  7.36 us (20%)
  local copies, waits for them, and re-layouts  1.29 us (3%)
    ppermute x7, starting transfers between devices, send(): return lax.ppermute(piece, 'pulse', [(i, i ^ k) for i in range(peers)])  12.5 us
    ppermute x1, starting transfers between devices, per_device(): up = lax.ppermute(up, 'rng', chips)  4.51 us
    ppermute x1, waiting for transfers between devices, per_device(): down = lax.ppermute(down, 'rng', [(j, i) for i, j in chips])  4.28 us
    pallas_call x3, Pallas kernels, next_range(): call(functools.partial(next_range_body, steps), 'next_range', (bf16(GROUP...  4.09 us
    ppermute x7, waiting for transfers between devices, send(): return lax.ppermute(piece, 'pulse', [(i, i ^ k) for i in range(peers)])  2.36 us
    pallas_call x1, Pallas kernels, azimuth(): call(functools.partial(azimuth_body, steps), 'azimuth', jax.ShapeDtypeStr...  2.24 us
    pallas_call x1, Pallas kernels, first_range(): call(functools.partial(first_range_body, steps), 'first_range', (bf16(blo...  1.81 us
    ppermute x1, starting transfers between devices, per_device(): down = lax.ppermute(down, 'rng', [(j, i) for i, j in chips])  1.41 us
  transfers between devices with their start and end apart: 10, of which 5 were waited for; matrix products, arithmetic and copies ran while one was open for 0% of the time, Pallas kernels for 15%

profile of v6, /device:TPU:1, one launch (start us, length us, event | category | flops | bytes accessed | tf_op | source)
XLA Modules:
  0.0 37.1 jit_solution(9908420678159885016)
XLA Ops:
  0.0 0.0 copy-start
  0.0 0.0 copy-start.1
  0.0 1.3 %copy-done.1 = bf16[2,128,2048]{2,1,0:T(8,128)(2,1)S(1)} copy-done((bf16[2,128,2048]{2,1,0:T(8,128)(2,1)S(1)}, bf16[2,128,2048]{2,1,0:T(8,128)(2,1)}, u32[]{:S(2)}) %copy-start.1) | copy-done | bytes 1048600
  1.3 0.0 copy-start.4
  1.3 0.0 copy-start.3
  1.3 0.1 pack.1
  1.4 0.0 copy-start.2
  1.4 0.1 collective-permute-start
  1.5 1.4 %collective-permute-start.1 = (bf16[9,128,256]{2,1,0:T(8,128)(2,1)S(1)}, bf16[9,128,256]{2,1,0:T(8,128)(2,1)S(1)}, u32[]{:S(2)}, u32[]{:S(2)}) collective-permute-start(bf16[9,128,256]{2,1,0:T(8,128)(2,1)S(1)} %get-tuple-element.23), channel_id=1, source_target_pairs={{2,1},{6,5},{10,9},{14,13},{18,17},{22,21},{26,25},{30,29}} | collective-permute-start | bytes 1769480 | tf_op jit(solution)/shard_map/ppermute | solution.py:369
  2.9 4.5 %collective-permute-start.2 = (bf16[1,128,256]{2,1,0:T(8,128)(2,1)S(1)}, bf16[1,128,256]{2,1,0:T(8,128)(2,1)S(1)}, u32[]{:S(2)}, u32[]{:S(2)}) collective-permute-start(bf16[1,128,256]{2,1,0:T(8,128)(2,1)S(1)} %get-tuple-element.24), channel_id=1, source_target_pairs={{1,2},{5,6},{9,10},{13,14},{17,18},{21,22},{25,26},{29,30}} | collective-permute-start | bytes 196616 | tf_op jit(solution)/shard_map/ppermute | solution.py:370
  7.5 0.0 copy-done.4
  7.5 0.6 %prepare.1.range_tiles = bf16[10,256,256]{2,1,0:T(8,128)(2,1)S(1)} custom-call(bf16[2,1024]{1,0:T(2,128)(2,1)S(1)} %copy-done.4), custom_call_target="tpu_custom_call" | custom-call | tf_op jit(solution)/shard_map/prepare/pallas_call | solution.py:100
  8.1 0.7 %collective-permute-done.2.up = bf16[1,128,256]{2,1,0:T(8,128)(2,1)S(1)} collective-permute-done((bf16[1,128,256]{2,1,0:T(8,128)(2,1)S(1)}, bf16[1,128,256]{2,1,0:T(8,128)(2,1)S(1)}, u32[]{:S(2)}, u32[]{:S(2)}) %collective-permute-start.2) | collective-permute-done | bytes 65568 | tf_op jit(solution)/shard_map/ppermute | solution.py:370
  8.8 0.0 collective-permute-done.near
  8.8 4.3 %collective-permute-done.1.down = bf16[9,128,256]{2,1,0:T(8,128)(2,1)S(1)} collective-permute-done((bf16[9,128,256]{2,1,0:T(8,128)(2,1)S(1)}, bf16[9,128,256]{2,1,0:T(8,128)(2,1)S(1)}, u32[]{:S(2)}, u32[]{:S(2)}) %collective-permute-start.1) | collective-permute-done | bytes 589856 | tf_op jit(solution)/shard_map/ppermute | solution.py:369
  13.1 0.0 copy-done
  13.1 0.0 copy-done.3
  13.1 0.0 copy-done.2
  13.1 1.8 %first_range.1 = (bf16[26,128,256]{2,1,0:T(8,128)(2,1)S(1)}, bf16[256,256]{1,0:T(8,128)(2,1)S(1)}, bf16[256,256]{1,0:T(8,128)(2,1)S(1)}) custom-call(bf16[2,128,2048]{2,1,0:T(8,128)(2,1)S(1)} %copy-done.2, bf16[9,128,256]{2,1,0:T(8,128)(2,1)S(1)} %collective-permute-done.near, bf16[9,128,256]{2,1,0:T(8,128)(2,1)S(1)} %collective-permute-done.1.down, ...), custom_call_target="tpu_custom_call" | custom-call | tf_op jit(solution)/shard_map/first_range/pallas_call | solution.py:186
  14.9 3.8 %collective-permute-start.3 = (bf16[256,256]{1,0:T(8,128)(2,1)S(1)}, bf16[256,256]{1,0:T(8,128)(2,1)S(1)}, u32[]{:S(2)}, u32[]{:S(2)}) collective-permute-start(bf16[256,256]{1,0:T(8,128)(2,1)S(1)} %get-tuple-element.25.after), channel_id=1, source_target_pairs={{0,16},{4,20},{8,24},{12,28},{16,0},{20,4},{24,8},{28,12},{1,17},{... | collective-permute-start | bytes 393224 | tf_op jit(solution)/shard_map/ppermute | solution.py:382
  18.7 0.7 %collective-permute-start.4 = (bf16[256,256]{1,0:T(8,128)(2,1)S(1)}, bf16[256,256]{1,0:T(8,128)(2,1)S(1)}, u32[]{:S(2)}, u32[]{:S(2)}) collective-permute-start(bf16[256,256]{1,0:T(8,128)(2,1)S(1)} %get-tuple-element.30), channel_id=1, source_target_pairs={{0,20},{4,16},{8,28},{12,24},{16,4},{20,0},{24,12},{28,8},{1,21},{... | collective-permute-start | bytes 393224 | tf_op jit(solution)/shard_map/ppermute | solution.py:382
  19.4 1.6 %next_range.3 = (bf16[256,256]{1,0:T(8,128)(2,1)S(1)}, bf16[256,256]{1,0:T(8,128)(2,1)S(1)}) custom-call(bf16[256,256]{1,0:T(8,128)(2,1)S(1)} %get-tuple-element.25.after, bf16[26,128,256]{2,1,0:T(8,128)(2,1)S(1)} %get-tuple-element.26.samples, bf16[10,256,256]{2,1,0:T(8,128)(2,1)S(1)} %prepare.1.range_tiles, bf16[64,2048]{1,0:T(8,128)(2,1)S(1)} %copy-done, ...), custom_call_target="tpu_custom_call" | custom-call | tf_op jit(solution)/shard_map/next_range/pallas_call | solution.py:218
  21.0 3.6 %collective-permute-start.6 = (bf16[256,256]{1,0:T(8,128)(2,1)S(1)}, bf16[256,256]{1,0:T(8,128)(2,1)S(1)}, u32[]{:S(2)}, u32[]{:S(2)}) collective-permute-start(bf16[256,256]{1,0:T(8,128)(2,1)S(1)} %get-tuple-element.31), channel_id=1, source_target_pairs={{0,28},{4,24},{8,20},{12,16},{16,12},{20,8},{24,4},{28,0},{1,29},{... | collective-permute-start | bytes 393224 | tf_op jit(solution)/shard_map/ppermute | solution.py:382
  24.6 0.1 collective-permute-start.5
  24.7 1.6 %next_range.4 = (bf16[256,256]{1,0:T(8,128)(2,1)S(1)}, bf16[256,256]{1,0:T(8,128)(2,1)S(1)}) custom-call(bf16[256,256]{1,0:T(8,128)(2,1)S(1)} %get-tuple-element.27.after, bf16[26,128,256]{2,1,0:T(8,128)(2,1)S(1)} %get-tuple-element.26.samples, bf16[10,256,256]{2,1,0:T(8,128)(2,1)S(1)} %prepare.1.range_tiles, bf16[64,2048]{1,0:T(8,128)(2,1)S(1)} %copy-done, ...), custom_call_target="tpu_custom_call" | custom-call | tf_op jit(solution)/shard_map/next_range/pallas_call | solution.py:218
  26.3 0.4 collective-permute-start.7
  26.7 0.0 copy-start.5
  26.7 0.9 %next_range.5.after.refs_0_ = bf16[256,256]{1,0:T(8,128)(2,1)S(1)} custom-call(bf16[256,256]{1,0:T(8,128)(2,1)S(1)} %get-tuple-element.28.after.refs_0_, bf16[26,128,256]{2,1,0:T(8,128)(2,1)S(1)} %get-tuple-element.26.samples, bf16[10,256,256]{2,1,0:T(8,128)(2,1)S(1)} %prepare.1.range_tiles, bf16[64,2048]{1,0:T(8,128)(2,1)S(1)} %copy-done, s32[16,128]{1,0:T(8,128)S(1)} %bitcast.4), custom_call_target="tpu_custom_call" | custom-call | tf_op jit(solution)/shard_map/next_range/pallas_call | solution.py:218
  27.6 0.0 copy-done.5
  27.6 1.0 %own_range.1 = (bf16[256,256]{1,0:T(8,128)(2,1)S(1)}, bf16[5,256,256]{2,1,0:T(8,128)(2,1)S(1)}) custom-call(bf16[256,256]{1,0:T(8,128)(2,1)S(1)} %next_range.5.after.refs_0_, bf16[26,128,256]{2,1,0:T(8,128)(2,1)S(1)} %get-tuple-element.26.samples, bf16[10,256,256]{2,1,0:T(8,128)(2,1)S(1)} %prepare.1.range_tiles, bf16[64,2048]{1,0:T(8,128)(2,1)S(1)} %copy-done, ...), custom_call_target="tpu_custom_call" | custom-call | tf_op jit(solution)/shard_map/own_range/pallas_call | solution.py:235
  28.6 0.0 collective-permute-done.3.refs_1_.rest_0_
  28.6 2.1 %collective-permute-start.9 = (bf16[256,256]{1,0:T(8,128)(2,1)S(1)}, bf16[256,256]{1,0:T(8,128)(2,1)S(1)}, u32[]{:S(2)}, u32[]{:S(2)}) collective-permute-start(bf16[256,256]{1,0:T(8,128)(2,1)S(1)} %gate.7), channel_id=1, source_target_pairs={{0,8},{4,12},{8,0},{12,4},{16,24},{20,28},{24,16},{28,20},{1,9},{5... | collective-permute-start | bytes 393224 | tf_op jit(solution)/shard_map/ppermute | solution.py:382
  30.7 0.0 collective-permute-done.4.refs_1_.rest_1_
  30.7 1.8 %collective-permute-start.8 = (bf16[256,256]{1,0:T(8,128)(2,1)S(1)}, bf16[256,256]{1,0:T(8,128)(2,1)S(1)}, u32[]{:S(2)}, u32[]{:S(2)}) collective-permute-start(bf16[256,256]{1,0:T(8,128)(2,1)S(1)} %gate.6), channel_id=1, source_target_pairs={{0,4},{4,0},{8,12},{12,8},{16,20},{20,16},{24,28},{28,24},{1,5},{5... | collective-permute-start | bytes 393224 | tf_op jit(solution)/shard_map/ppermute | solution.py:382
  32.5 0.0 collective-permute-done.6.refs_1_
  32.5 0.0 collective-permute-done.5.refs_0_
  32.5 0.3 collective-permute-done.7.refs_2_
  32.8 1.2 %collective-permute-done.9.rest_6_ = bf16[256,256]{1,0:T(8,128)(2,1)S(1)} collective-permute-done((bf16[256,256]{1,0:T(8,128)(2,1)S(1)}, bf16[256,256]{1,0:T(8,128)(2,1)S(1)}, u32[]{:S(2)}, u32[]{:S(2)}) %collective-permute-start.9) | collective-permute-done | bytes 131104 | tf_op jit(solution)/shard_map/ppermute | solution.py:382
  34.0 0.8 %collective-permute-done.8.rest_5_ = bf16[256,256]{1,0:T(8,128)(2,1)S(1)} collective-permute-done((bf16[256,256]{1,0:T(8,128)(2,1)S(1)}, bf16[256,256]{1,0:T(8,128)(2,1)S(1)}, u32[]{:S(2)}, u32[]{:S(2)}) %collective-permute-start.8) | collective-permute-done | bytes 131104 | tf_op jit(solution)/shard_map/ppermute | solution.py:382
  34.8 2.2 %azimuth.1 = f32[2,1,256,1024]{3,2,1,0:T(8,128)} custom-call(bf16[5,256,256]{2,1,0:T(8,128)(2,1)S(1)} %get-tuple-element.29.az_tiles, bf16[256,256]{1,0:T(8,128)(2,1)S(1)} %collective-permute-done.3.refs_1_.rest_0_, bf16[256,256]{1,0:T(8,128)(2,1)S(1)} %collective-permute-done.4.refs_1_.rest_1_, bf16[256,256]{1,0:T(8,128)(2,1)S(1)} %get-tuple-element.35.rest_2_, ...), custom_call_target="tpu_custom_call" | custom-call | tf_op jit(solution)/shard_map/azimuth/pallas_call | solution.py:346
  (4 shorter events, 0.0 us)
Async XLA Ops:
  0.0 13.1 %copy-start = (bf16[64,2048]{1,0:T(8,128)(2,1)S(1)}, bf16[64,2048]{1,0:T(8,128)(2,1)}, u32[]{:S(2)}) copy-start(bf16[64,2048]{1,0:T(8,128)(2,1)} %weights.9) | copy-start | bytes 786436
  0.0 1.3 %copy-start.1 = (bf16[2,128,2048]{2,1,0:T(8,128)(2,1)S(1)}, bf16[2,128,2048]{2,1,0:T(8,128)(2,1)}, u32[]{:S(2)}) copy-start(bf16[2,128,2048]{2,1,0:T(8,128)(2,1)} %echoes.3) | copy-start | bytes 3145732
  1.3 6.2 %copy-start.4 = (bf16[2,1024]{1,0:T(2,128)(2,1)S(1)}, bf16[2,1024]{1,0:T(2,128)(2,1)}, u32[]{:S(2)}) copy-start(bf16[2,1024]{1,0:T(2,128)(2,1)} %range_ref.1) | copy-start | bytes 12292
  1.3 11.8 %copy-start.3 = (s32[2048]{0:T(1024)S(1)}, s32[2048]{0:T(1024)}, u32[]{:S(2)}) copy-start(s32[2048]{0:T(1024)} %param.8) | copy-start | bytes 24580
  1.4 11.7 %copy-start.2 = (bf16[2,128,2048]{2,1,0:T(8,128)(2,1)S(1)}, bf16[2,128,2048]{2,1,0:T(8,128)(2,1)}, u32[]{:S(2)}) copy-start(bf16[2,128,2048]{2,1,0:T(8,128)(2,1)} %echoes.3) | copy-start | bytes 3145732
  1.4 7.4 %collective-permute-start = (bf16[9,128,256]{2,1,0:T(8,128)(2,1)S(1)}, bf16[9,128,256]{2,1,0:T(8,128)(2,1)S(1)}, u32[]{:S(2)}, u32[]{:S(2)}) collective-permute-start(bf16[9,128,256]{2,1,0:T(8,128)(2,1)S(1)} %get-tuple-element.22), channel_id=1, source_target_pairs={{0,1},{2,3},{1,0},{3,2},{4,5},{6,7},{5,4},{7,6},{8,9},{10,11},{9,8... | collective-permute-start | bytes 1769480 | tf_op jit(solution)/shard_map/ppermute | solution.py:368
  1.5 11.5 %collective-permute-start.1 = (bf16[9,128,256]{2,1,0:T(8,128)(2,1)S(1)}, bf16[9,128,256]{2,1,0:T(8,128)(2,1)S(1)}, u32[]{:S(2)}, u32[]{:S(2)}) collective-permute-start(bf16[9,128,256]{2,1,0:T(8,128)(2,1)S(1)} %get-tuple-element.23), channel_id=1, source_target_pairs={{2,1},{6,5},{10,9},{14,13},{18,17},{22,21},{26,25},{30,29}} | collective-permute-start | bytes 1769480 | tf_op jit(solution)/shard_map/ppermute | solution.py:369
  2.9 5.8 %collective-permute-start.2 = (bf16[1,128,256]{2,1,0:T(8,128)(2,1)S(1)}, bf16[1,128,256]{2,1,0:T(8,128)(2,1)S(1)}, u32[]{:S(2)}, u32[]{:S(2)}) collective-permute-start(bf16[1,128,256]{2,1,0:T(8,128)(2,1)S(1)} %get-tuple-element.24), channel_id=1, source_target_pairs={{1,2},{5,6},{9,10},{13,14},{17,18},{21,22},{25,26},{29,30}} | collective-permute-start | bytes 196616 | tf_op jit(solution)/shard_map/ppermute | solution.py:370
  14.9 13.7 %collective-permute-start.3 = (bf16[256,256]{1,0:T(8,128)(2,1)S(1)}, bf16[256,256]{1,0:T(8,128)(2,1)S(1)}, u32[]{:S(2)}, u32[]{:S(2)}) collective-permute-start(bf16[256,256]{1,0:T(8,128)(2,1)S(1)} %get-tuple-element.25.after), channel_id=1, source_target_pairs={{0,16},{4,20},{8,24},{12,28},{16,0},{20,4},{24,8},{28,12},{1,17},{... | collective-permute-start | bytes 393224 | tf_op jit(solution)/shard_map/ppermute | solution.py:382
  18.7 12.0 %collective-permute-start.4 = (bf16[256,256]{1,0:T(8,128)(2,1)S(1)}, bf16[256,256]{1,0:T(8,128)(2,1)S(1)}, u32[]{:S(2)}, u32[]{:S(2)}) collective-permute-start(bf16[256,256]{1,0:T(8,128)(2,1)S(1)} %get-tuple-element.30), channel_id=1, source_target_pairs={{0,20},{4,16},{8,28},{12,24},{16,4},{20,0},{24,12},{28,8},{1,21},{... | collective-permute-start | bytes 393224 | tf_op jit(solution)/shard_map/ppermute | solution.py:382
  21.0 11.5 %collective-permute-start.6 = (bf16[256,256]{1,0:T(8,128)(2,1)S(1)}, bf16[256,256]{1,0:T(8,128)(2,1)S(1)}, u32[]{:S(2)}, u32[]{:S(2)}) collective-permute-start(bf16[256,256]{1,0:T(8,128)(2,1)S(1)} %get-tuple-element.31), channel_id=1, source_target_pairs={{0,28},{4,24},{8,20},{12,16},{16,12},{20,8},{24,4},{28,0},{1,29},{... | collective-permute-start | bytes 393224 | tf_op jit(solution)/shard_map/ppermute | solution.py:382
  24.6 7.9 %collective-permute-start.5 = (bf16[256,256]{1,0:T(8,128)(2,1)S(1)}, bf16[256,256]{1,0:T(8,128)(2,1)S(1)}, u32[]{:S(2)}, u32[]{:S(2)}) collective-permute-start(bf16[256,256]{1,0:T(8,128)(2,1)S(1)} %get-tuple-element.27.after), channel_id=1, source_target_pairs={{0,24},{4,28},{8,16},{12,20},{16,8},{20,12},{24,0},{28,4},{1,25},{... | collective-permute-start | bytes 393224 | tf_op jit(solution)/shard_map/ppermute | solution.py:382
  26.3 6.5 %collective-permute-start.7 = (bf16[256,256]{1,0:T(8,128)(2,1)S(1)}, bf16[256,256]{1,0:T(8,128)(2,1)S(1)}, u32[]{:S(2)}, u32[]{:S(2)}) collective-permute-start(bf16[256,256]{1,0:T(8,128)(2,1)S(1)} %get-tuple-element.34), channel_id=1, source_target_pairs={{0,12},{4,8},{8,4},{12,0},{16,28},{20,24},{24,20},{28,16},{1,13},{... | collective-permute-start | bytes 393224 | tf_op jit(solution)/shard_map/ppermute | solution.py:382
  26.7 1.0 %copy-start.5 = (bf16[2,512]{1,0:T(2,128)(2,1)S(1)}, bf16[2,512]{1,0:T(2,128)(2,1)}, u32[]{:S(2)}) copy-start(bf16[2,512]{1,0:T(2,128)(2,1)} %az_taps.1) | copy-start | bytes 6148
  28.6 5.4 %collective-permute-start.9 = (bf16[256,256]{1,0:T(8,128)(2,1)S(1)}, bf16[256,256]{1,0:T(8,128)(2,1)S(1)}, u32[]{:S(2)}, u32[]{:S(2)}) collective-permute-start(bf16[256,256]{1,0:T(8,128)(2,1)S(1)} %gate.7), channel_id=1, source_target_pairs={{0,8},{4,12},{8,0},{12,4},{16,24},{20,28},{24,16},{28,20},{1,9},{5... | collective-permute-start | bytes 393224 | tf_op jit(solution)/shard_map/ppermute | solution.py:382
  30.7 4.2 %collective-permute-start.8 = (bf16[256,256]{1,0:T(8,128)(2,1)S(1)}, bf16[256,256]{1,0:T(8,128)(2,1)S(1)}, u32[]{:S(2)}, u32[]{:S(2)}) collective-permute-start(bf16[256,256]{1,0:T(8,128)(2,1)S(1)} %gate.6), channel_id=1, source_target_pairs={{0,4},{4,0},{8,12},{12,8},{16,20},{20,16},{24,28},{28,24},{1,5},{5... | collective-permute-start | bytes 393224 | tf_op jit(solution)/shard_map/ppermute | solution.py:382

commit v7 on v6

--- a/solution.py
+++ b/solution.py
@@ -90,16 +90,6 @@
         out[tile, :BLK, BLK:] = (-imag).astype(jnp.bfloat16)
         out[tile, BLK:, :BLK] = imag.astype(jnp.bfloat16)
         out[tile, BLK:, BLK:] = real.astype(jnp.bfloat16)
-
-
-def prepare_body(range_ref, range_out):
-    toeplitz_tiles(range_ref, RANGE_TILES, HALF, range_out)
-
-
-def prepare(range_ref):
-    return call(
-        prepare_body, "prepare", bf16(RANGE_TILES, WIDE, WIDE), [VMEM()], VMEM()
-    )(range_ref)
 
 
 def band(weights, offsets, block):
@@ -118,17 +108,32 @@
     return jnp.where(outside & (lane < HALF), 0.0, skewed).astype(jnp.bfloat16)
 
 
-def assemble(echoes, near, down, up, out):
-    blocks = echoes.shape[2] // BLK
-    for block in range(blocks):
+def prepare_body(echoes, range_ref, samples, range_out):
+    toeplitz_tiles(range_ref, RANGE_TILES, HALF, range_out)
+    for block in range(echoes.shape[2] // BLK):
         for part in range(2):
-            out[block + 1, :, part * BLK : (part + 1) * BLK] = echoes[
+            samples[block + 1, :, part * BLK : (part + 1) * BLK] = echoes[
                 part, :, block * BLK : (block + 1) * BLK
             ]
 
+
+def prepare(echoes, range_ref):
+    blocks = 1 + echoes.shape[2] // BLK + HEAD
+    return call(
+        prepare_body,
+        "prepare",
+        (bf16(blocks, echoes.shape[1], WIDE), bf16(RANGE_TILES, WIDE, WIDE)),
+        [VMEM()] * 2,
+        (VMEM(),) * 2,
+    )(echoes, range_ref)
+
+
+def add_ends(near, down, up, out):
+    count = near.shape[0]
+
     def ends(low, high):
         out[0] = low[0]
-        out[blocks + 1 :] = high[...]
+        out[out.shape[0] - count :] = high[...]
 
     odd = lax.axis_index("rng") % 2 == 1
     pl.when(odd)(lambda: ends(near, down))
@@ -154,17 +159,6 @@
     ).astype(jnp.bfloat16)
 
 
-def groups_of(first, count, spots, samples, range_tiles, weights, offsets, turned, outs):
-    for block in range(count + 1):
-        turned[block * BLK : (block + 1) * BLK, :] = compress(samples, range_tiles, first + block)
-    rows = [out.at[pl.ds(i, GROUP)] for out in outs for i in range(0, out.shape[0], GROUP)]
-    for spot, out in zip(spots, rows):
-        for block in range(GROUP // BLK):
-            out[block * BLK : (block + 1) * BLK, :] = migrate(
-                weights, offsets, turned, first, spot * (GROUP // BLK) + block
-            )
-
-
 def group_sends(steps, samples, range_tiles, weights, offsets, turned, outs):
     me = lax.axis_index("pulse")
     blocks = GROUP // BLK
@@ -172,25 +166,36 @@
         first, spots = blocks * (me ^ steps[0]), [0]
     else:
         first, spots = 2 * blocks * (me // 2 ^ steps[0] // 2), [me % 2 ^ k % 2 for k in steps]
-    groups_of(first, blocks * len(steps), spots, samples, range_tiles, weights, offsets, turned, outs)
-
-
-def first_range_body(steps, echoes, near, down, up, range_tiles, weights, offsets, samples, *rest):
-    assemble(echoes, near, down, up, samples)
+    for block in range(blocks * len(steps) + 1):
+        turned[block * BLK : (block + 1) * BLK, :] = compress(samples, range_tiles, first + block)
+    for spot, out in zip(spots, outs):
+        for block in range(blocks):
+            out[block * BLK : (block + 1) * BLK, :] = migrate(
+                weights, offsets, turned, first, spot * blocks + block
+            )
+
+
+def first_range_body(
+    steps, start, near, down, up, range_tiles, weights, offsets, samples, *rest
+):
+    add_ends(near, down, up, samples)
     group_sends(steps, samples, range_tiles, weights, offsets, rest[-1], rest[:-1])
 
 
-def first_range(steps, echoes, near, down, up, range_tiles, weights, offsets):
-    pulses = echoes.shape[1]
-    blocks = 1 + echoes.shape[2] // BLK + HEAD
-    samples, *made = call(
+def first_range(steps, samples, near, down, up, range_tiles, weights, offsets):
+    pulses = samples.shape[1]
+    samples, *made = pl.pallas_call(
         functools.partial(first_range_body, steps),
-        "first_range",
-        (bf16(blocks, pulses, WIDE),) + (bf16(GROUP, 2 * pulses),) * len(steps),
-        [VMEM()] * 7,
-        (VMEM(),) * (1 + len(steps)),
-        [pltpu.VMEM((5 * BLK, 2 * pulses), jnp.bfloat16)],
-    )(echoes, near, down, up, range_tiles, weights, offsets)
+        out_shape=(jax.ShapeDtypeStruct(samples.shape, samples.dtype),)
+        + (bf16(GROUP, 2 * pulses),) * len(steps),
+        in_specs=[VMEM()] * 7,
+        out_specs=(VMEM(),) * (1 + len(steps)),
+        scratch_shapes=[pltpu.VMEM((5 * BLK, 2 * pulses), jnp.bfloat16)],
+        input_output_aliases={0: 0},
+        compiler_params=pltpu.CompilerParams(vmem_limit_bytes=LIMIT),
+        cost_estimate=pl.CostEstimate(flops=0, bytes_accessed=0, transcendentals=0),
+        name="first_range",
+    )(samples, near, down, up, range_tiles, weights, offsets)
     return samples, made
 
 
@@ -261,8 +266,10 @@
     )(*values, *after)
 
 
-def whole_body(count, echoes, near, down, up, range_tiles, weights, offsets, az_taps, out, az_out, samples, turned):
-    assemble(echoes, near, down, up, samples)
+def whole_body(count, start, near, down, up, range_tiles, weights, offsets, az_taps, *rest):
+    out, az_out, samples, turned = rest
+    samples[...] = start[...]
+    add_ends(near, down, up, samples)
     for block in range(count + 1):
         turned[block * BLK : (block + 1) * BLK, :] = compress(samples, range_tiles, block)
     for block in range(count):
@@ -270,8 +277,8 @@
     toeplitz_tiles(az_taps, AZ_TILES, 0, az_out)
 
 
-def whole_quarter(echoes, near, down, up, range_tiles, weights, offsets, azimuth_ref):
-    pulses = echoes.shape[1]
+def whole_quarter(samples, near, down, up, range_tiles, weights, offsets, azimuth_ref):
+    pulses = samples.shape[1]
     count = weights.shape[1] // BLK
     return call(
         functools.partial(whole_body, count),
@@ -280,10 +287,10 @@
         [VMEM()] * 8,
         (VMEM(),) * 2,
         [
-            pltpu.VMEM((1 + count + HEAD, pulses, WIDE), jnp.bfloat16),
+            pltpu.VMEM(samples.shape, jnp.bfloat16),
             pltpu.VMEM(((count + 1) * BLK, 2 * pulses), jnp.bfloat16),
         ],
-    )(echoes, near, down, up, range_tiles, weights, offsets, azimuth_ref)
+    )(samples, near, down, up, range_tiles, weights, offsets, azimuth_ref)
 
 
 def azimuth_rows(bins, steps, parts, rows):
@@ -357,6 +364,71 @@
     )(az_tiles, *parts)
 
 
+def azimuth_most_body(steps, absent, az_tiles, *rest):
+    *parts, image, rows = rest
+    bins = image.shape[2]
+    azimuth_rows(bins, [absent], [jnp.zeros((bins, WIDE), jnp.bfloat16)], rows)
+    azimuth_rows(bins, steps, parts, rows)
+    azimuth_blocks(bins, image.shape[3] // BLK, rows, az_tiles, image)
+
+
+def azimuth_most(steps, absent, az_tiles, parts):
+    bins = parts[0].shape[0]
+    count = len(steps) + 1
+    return call(
+        functools.partial(azimuth_most_body, steps, absent),
+        "azimuth_most",
+        jax.ShapeDtypeStruct((2, 1, bins, count * BLK), jnp.float32),
+        [VMEM()] * (1 + len(parts)),
+        VMEM(),
+        [pltpu.VMEM((count * bins, WIDE), jnp.bfloat16)],
+    )(az_tiles, *parts)
+
+
+def azimuth_last_body(step, az_tiles, most, part, out, image, sems):
+    count = most.shape[3] // BLK
+    low = (lax.axis_index("pulse") ^ step) - AZ_TILES // 2
+
+    def move(source, place, block):
+        span = pl.ds(pl.multiple_of(block * BLK, BLK), BLK)
+        return pltpu.make_async_copy(
+            source.at[:, :, :, pl.ds(pl.multiple_of(place * BLK, BLK), BLK)],
+            out.at[:, :, :, span],
+            sems.at[block],
+        )
+
+    for block in range(count):
+        pl.when((block < low) | (block >= low + AZ_TILES))(move(most, block, block).start)
+    for i in range(AZ_TILES):
+        total = jnp.dot(
+            part[...], az_tiles[AZ_TILES - 1 - i], preferred_element_type=jnp.float32
+        )
+        block = low + i
+        held = pl.ds(pl.multiple_of(jnp.clip(block, 0, count - 1) * BLK, BLK), BLK)
+        for side in range(2):
+            image[side, 0, :, i * BLK : (i + 1) * BLK] = (
+                most[side, 0, :, held] + total[:, side * BLK : (side + 1) * BLK]
+            )
+        inside = (block >= 0) & (block < count)
+        pl.when(inside)(lambda i=i, block=block: move(image, i, block).start())
+    for block in range(count):
+        move(most, block, block).wait()
+
+
+def azimuth_last(step, az_tiles, most, part):
+    return call(
+        functools.partial(azimuth_last_body, step),
+        "azimuth_last",
+        jax.ShapeDtypeStruct(most.shape, most.dtype),
+        [VMEM()] * 3,
+        HBM(),
+        [
+            pltpu.VMEM(most.shape[:3] + (AZ_TILES * BLK,), jnp.float32),
+            pltpu.SemaphoreType.DMA((most.shape[3] // BLK,)),
+        ],
+    )(az_tiles, most, part)
+
+
 def per_device(echoes, range_ref, band_weights, band_offsets, azimuth_ref):
     quarter_len = echoes.shape[2]
     peers = lax.axis_size("pulse")
@@ -368,11 +440,13 @@
     near = lax.ppermute(near, "rng", cores + [(j, i) for i, j in cores])
     down = lax.ppermute(down, "rng", [(j, i) for i, j in chips])
     up = lax.ppermute(up, "rng", chips)
-    range_tiles = prepare(range_ref)
     weights, offsets = band_weights, band_offsets.reshape(-1, BLK)
+    samples, range_tiles = prepare(echoes, range_ref)
 
     if bins != GROUP or peers != 8:
-        mine, az_tiles = whole_quarter(echoes, near, down, up, range_tiles, weights, offsets, azimuth_ref)
+        mine, az_tiles = whole_quarter(
+            samples, near, down, up, range_tiles, weights, offsets, azimuth_ref
+        )
         swapped = lax.all_to_all(
             mine.reshape(peers, bins, WIDE), "pulse", split_axis=0, concat_axis=0, tiled=True
         )
@@ -381,11 +455,12 @@
     def send(piece, k):
         return lax.ppermute(piece, "pulse", [(i, i ^ k) for i in range(peers)])
 
-    samples, made = first_range([4, 5], echoes, near, down, up, range_tiles, weights, offsets)
-    parts = {k: send(piece, k) for k, piece in zip([4, 5], made)}
-    for some in [[6, 7]]:
-        made = next_range([some], made[0], samples, range_tiles, weights, offsets)
-        parts.update({k: send(piece, k) for k, piece in zip(some, made)})
+    samples, made = first_range(
+        [4, 5], samples, near, down, up, range_tiles, weights, offsets
+    )
+    parts = {k: send(piece, k) for k, piece in zip((4, 5), made)}
+    made = next_range([[6, 7]], made[0], samples, range_tiles, weights, offsets)
+    parts.update({k: send(piece, k) for k, piece in zip((6, 7), made)})
     ready = {}
     for some in [[2, 3], [1]]:
         made = next_range([some], made[0], samples, range_tiles, weights, offsets)
@@ -393,10 +468,12 @@
     parts[3] = send(ready[3], 3)
     parts[1] = send(gate([ready[1]], (parts[5],))[0], 1)
     parts[2] = send(gate([ready[2]], (parts[4],))[0], 2)
-    parts[0], az_tiles = own_range(made[0], samples, range_tiles, weights, offsets, azimuth_ref)
+    parts[0], az_tiles = own_range(parts[5], samples, range_tiles, weights, offsets, azimuth_ref)
     held = gate((parts[6], parts[7]), (), 1000000000) + (parts[3],)
     parts.update(zip((6, 7, 3), gate(held, (), 2 * 10**8)))
-    return azimuth(list(parts), peers, az_tiles, list(parts.values()))
+    last = parts.pop(2)
+    most = azimuth_most(list(parts), 2, az_tiles, list(parts.values()))
+    return azimuth_last(2, az_tiles, most, last)
 
 
 def solution(mesh):

time: 37.3 us -> 36.8 us (0.987)
  starting transfers between devices: 18.5 us -> 17.1 us
  Pallas kernels: 9.8 us -> 10.4 us
  waiting for transfers between devices: 7.36 us -> 7.78 us
    ppermute x7, starting transfers between devices: 12.5 us -> 11.2 us  [send(): return lax.ppermute(piece, 'pulse', [(i, i ^ k) for i in range(peers)])]
    pallas_call x3 -> x4, Pallas kernels: 4.62 us -> 5.2 us  [the longest x1 1.62 us: first_range(): pl.pallas_call(functools.partial(first_range_body, steps), out_shape=(jax...]
    unnamed x12 -> x10, local copies, waits for them, and re-layouts: 1.29 us -> 1.28 us
  transfers between devices with their start and end apart: 10 -> 10, of which waited for: 5 -> 5; matrix products, arithmetic and copies ran while one was open for 0% -> 0% of each run, Pallas kernels for 15% -> 19%
where the time goes in v7:
time: 36.8 us; the launch traced here: 36.7 us
  starting transfers between devices  17.1 us (46%)
  Pallas kernels  10.4 us (28%)
  waiting for transfers between devices  7.78 us (21%)
  local copies, waits for them, and re-layouts  1.28 us (3%)
    ppermute x7, starting transfers between devices, send(): return lax.ppermute(piece, 'pulse', [(i, i ^ k) for i in range(peers)])  11.2 us
    ppermute x1, waiting for transfers between devices, per_device(): down = lax.ppermute(down, 'rng', [(j, i) for i, j in chips])  4.57 us
    ppermute x1, starting transfers between devices, per_device(): up = lax.ppermute(up, 'rng', chips)  4.51 us
    pallas_call x3, Pallas kernels, next_range(): call(functools.partial(next_range_body, steps), 'next_range', (bf16(GROUP...  4.09 us
    ppermute x7, waiting for transfers between devices, send(): return lax.ppermute(piece, 'pulse', [(i, i ^ k) for i in range(peers)])  2.62 us
    pallas_call x1, Pallas kernels, first_range(): pl.pallas_call(functools.partial(first_range_body, steps), out_shape=(jax...  1.62 us
    pallas_call x1, Pallas kernels, azimuth_last(): call(functools.partial(azimuth_last_body, step), 'azimuth_last', jax.Shap...  1.51 us
    pallas_call x1, Pallas kernels, azimuth_most(): call(functools.partial(azimuth_most_body, steps, absent), 'azimuth_most',...  1.36 us
  transfers between devices with their start and end apart: 10, of which 5 were waited for; matrix products, arithmetic and copies ran while one was open for 0% of the time, Pallas kernels for 19%

profile of v7, /device:TPU:1, one launch (start us, length us, event | category | flops | bytes accessed | tf_op | source)
XLA Modules:
  0.0 36.7 jit_solution(1909172074476579848)
XLA Ops:
  0.0 0.0 copy-start
  0.0 0.0 copy-start.1
  0.0 1.3 %copy-done.1 = bf16[2,128,2048]{2,1,0:T(8,128)(2,1)S(1)} copy-done((bf16[2,128,2048]{2,1,0:T(8,128)(2,1)S(1)}, bf16[2,128,2048]{2,1,0:T(8,128)(2,1)}, u32[]{:S(2)}) %copy-start.1) | copy-done | bytes 1048600
  1.3 0.0 copy-start.3
  1.3 0.0 copy-start.2
  1.3 0.1 pack.1
  1.4 0.1 collective-permute-start
  1.5 1.3 %collective-permute-start.1 = (bf16[9,128,256]{2,1,0:T(8,128)(2,1)S(1)}, bf16[9,128,256]{2,1,0:T(8,128)(2,1)S(1)}, u32[]{:S(2)}, u32[]{:S(2)}) collective-permute-start(bf16[9,128,256]{2,1,0:T(8,128)(2,1)S(1)} %get-tuple-element.26), channel_id=1, source_target_pairs={{2,1},{6,5},{10,9},{14,13},{18,17},{22,21},{26,25},{30,29}} | collective-permute-start | bytes 1769480 | tf_op jit(solution)/shard_map/ppermute | solution.py:441
  2.8 4.5 %collective-permute-start.2 = (bf16[1,128,256]{2,1,0:T(8,128)(2,1)S(1)}, bf16[1,128,256]{2,1,0:T(8,128)(2,1)S(1)}, u32[]{:S(2)}, u32[]{:S(2)}) collective-permute-start(bf16[1,128,256]{2,1,0:T(8,128)(2,1)S(1)} %get-tuple-element.27), channel_id=1, source_target_pairs={{1,2},{5,6},{9,10},{13,14},{17,18},{21,22},{25,26},{29,30}} | collective-permute-start | bytes 196616 | tf_op jit(solution)/shard_map/ppermute | solution.py:442
  7.3 0.0 copy-done.3
  7.3 0.7 %prepare.1 = (bf16[26,128,256]{2,1,0:T(8,128)(2,1)S(1)}, bf16[10,256,256]{2,1,0:T(8,128)(2,1)S(1)}) custom-call(bf16[2,128,2048]{2,1,0:T(8,128)(2,1)S(1)} %copy-done.1, bf16[2,1024]{1,0:T(2,128)(2,1)S(1)} %copy-done.3), custom_call_target="tpu_custom_call" | custom-call | tf_op jit(solution)/shard_map/prepare/pallas_call | solution.py:122
  8.1 0.6 %collective-permute-done.2.up = bf16[1,128,256]{2,1,0:T(8,128)(2,1)S(1)} collective-permute-done((bf16[1,128,256]{2,1,0:T(8,128)(2,1)S(1)}, bf16[1,128,256]{2,1,0:T(8,128)(2,1)S(1)}, u32[]{:S(2)}, u32[]{:S(2)}) %collective-permute-start.2) | collective-permute-done | bytes 65568 | tf_op jit(solution)/shard_map/ppermute | solution.py:442
  8.6 0.0 collective-permute-done.near
  8.6 4.6 %collective-permute-done.1.down = bf16[9,128,256]{2,1,0:T(8,128)(2,1)S(1)} collective-permute-done((bf16[9,128,256]{2,1,0:T(8,128)(2,1)S(1)}, bf16[9,128,256]{2,1,0:T(8,128)(2,1)S(1)}, u32[]{:S(2)}, u32[]{:S(2)}) %collective-permute-start.1) | collective-permute-done | bytes 589856 | tf_op jit(solution)/shard_map/ppermute | solution.py:441
  13.2 0.0 copy-done
  13.2 0.0 copy-done.2
  13.2 1.6 %first_range.1 = (bf16[26,128,256]{2,1,0:T(8,128)(2,1)S(1)}, bf16[256,256]{1,0:T(8,128)(2,1)S(1)}, bf16[256,256]{1,0:T(8,128)(2,1)S(1)}) custom-call(bf16[26,128,256]{2,1,0:T(8,128)(2,1)S(1)} %get-tuple-element.24.start, bf16[9,128,256]{2,1,0:T(8,128)(2,1)S(1)} %collective-permute-done.near, ...), custom_call_target="tpu_custom_call", output_to_operand_aliasing={{0}: (0, {})} | custom-call | tf_op jit(solution)/shard_map/first_range/pallas_call | solution.py:187
  14.8 4.3 %collective-permute-start.3 = (bf16[256,256]{1,0:T(8,128)(2,1)S(1)}, bf16[256,256]{1,0:T(8,128)(2,1)S(1)}, u32[]{:S(2)}, u32[]{:S(2)}) collective-permute-start(bf16[256,256]{1,0:T(8,128)(2,1)S(1)} %get-tuple-element.29), channel_id=1, source_target_pairs={{0,20},{4,16},{8,28},{12,24},{16,4},{20,0},{24,12},{28,8},{1,21},{... | collective-permute-start | bytes 393224 | tf_op jit(solution)/shard_map/ppermute | solution.py:456
  19.1 0.4 collective-permute-start.4
  19.5 1.6 %next_range.3 = (bf16[256,256]{1,0:T(8,128)(2,1)S(1)}, bf16[256,256]{1,0:T(8,128)(2,1)S(1)}) custom-call(bf16[256,256]{1,0:T(8,128)(2,1)S(1)} %get-tuple-element.32.after, bf16[26,128,256]{2,1,0:T(8,128)(2,1)S(1)} %get-tuple-element.30.samples, bf16[10,256,256]{2,1,0:T(8,128)(2,1)S(1)} %get-tuple-element.28.range_tiles, bf16[64,2048]{1,0:T(8,128)(2,1)S(1)} %copy-done, ...), custom_call_target="tpu_custom_call" | custom-call | tf_op jit(solution)/shard_map/next_range/pallas_call | solution.py:223
  21.0 3.3 %collective-permute-start.6 = (bf16[256,256]{1,0:T(8,128)(2,1)S(1)}, bf16[256,256]{1,0:T(8,128)(2,1)S(1)}, u32[]{:S(2)}, u32[]{:S(2)}) collective-permute-start(bf16[256,256]{1,0:T(8,128)(2,1)S(1)} %get-tuple-element.34), channel_id=1, source_target_pairs={{0,28},{4,24},{8,20},{12,16},{16,12},{20,8},{24,4},{28,0},{1,29},{... | collective-permute-start | bytes 393224 | tf_op jit(solution)/shard_map/ppermute | solution.py:456
  24.4 0.1 collective-permute-start.5
  24.5 1.6 %next_range.4 = (bf16[256,256]{1,0:T(8,128)(2,1)S(1)}, bf16[256,256]{1,0:T(8,128)(2,1)S(1)}) custom-call(bf16[256,256]{1,0:T(8,128)(2,1)S(1)} %get-tuple-element.33.after, bf16[26,128,256]{2,1,0:T(8,128)(2,1)S(1)} %get-tuple-element.30.samples, bf16[10,256,256]{2,1,0:T(8,128)(2,1)S(1)} %get-tuple-element.28.range_tiles, bf16[64,2048]{1,0:T(8,128)(2,1)S(1)} %copy-done, ...), custom_call_target="tpu_custom_call" | custom-call | tf_op jit(solution)/shard_map/next_range/pallas_call | solution.py:223
  26.1 0.3 collective-permute-start.7
  26.4 0.0 copy-start.4
  26.4 0.9 %next_range.5.refs_0_ = bf16[256,256]{1,0:T(8,128)(2,1)S(1)} custom-call(bf16[256,256]{1,0:T(8,128)(2,1)S(1)} %get-tuple-element.41.after.refs_0_, bf16[26,128,256]{2,1,0:T(8,128)(2,1)S(1)} %get-tuple-element.30.samples, bf16[10,256,256]{2,1,0:T(8,128)(2,1)S(1)} %get-tuple-element.28.range_tiles, bf16[64,2048]{1,0:T(8,128)(2,1)S(1)} %copy-done, ...), custom_call_target="tpu_custom_call" | custom-call | tf_op jit(solution)/shard_map/next_range/pallas_call | solution.py:223
  27.4 0.0 collective-permute-done.3.after.refs_1_.rest_1_
  27.4 2.2 %collective-permute-start.8 = (bf16[256,256]{1,0:T(8,128)(2,1)S(1)}, bf16[256,256]{1,0:T(8,128)(2,1)S(1)}, u32[]{:S(2)}, u32[]{:S(2)}) collective-permute-start(bf16[256,256]{1,0:T(8,128)(2,1)S(1)} %gate.6), channel_id=1, source_target_pairs={{0,4},{4,0},{8,12},{12,8},{16,20},{20,16},{24,28},{28,24},{1,5},{5... | collective-permute-start | bytes 393224 | tf_op jit(solution)/shard_map/ppermute | solution.py:456
  29.6 1.8 %collective-permute-done.4.rest_0_.refs_1_ = bf16[256,256]{1,0:T(8,128)(2,1)S(1)} collective-permute-done((bf16[256,256]{1,0:T(8,128)(2,1)S(1)}, bf16[256,256]{1,0:T(8,128)(2,1)S(1)}, u32[]{:S(2)}, u32[]{:S(2)}) %collective-permute-start.4) | collective-permute-done | bytes 131104 | tf_op jit(solution)/shard_map/ppermute | solution.py:456
  31.3 0.6 %collective-permute-start.9 = (bf16[256,256]{1,0:T(8,128)(2,1)S(1)}, bf16[256,256]{1,0:T(8,128)(2,1)S(1)}, u32[]{:S(2)}, u32[]{:S(2)}) collective-permute-start(bf16[256,256]{1,0:T(8,128)(2,1)S(1)} %gate.7), channel_id=1, source_target_pairs={{0,8},{4,12},{8,0},{12,4},{16,24},{20,28},{24,16},{28,20},{1,9},{5... | collective-permute-start | bytes 393224 | tf_op jit(solution)/shard_map/ppermute | solution.py:456
  31.9 0.0 copy-done.4
  31.9 1.0 %own_range.1 = (bf16[256,256]{1,0:T(8,128)(2,1)S(1)}, bf16[5,256,256]{2,1,0:T(8,128)(2,1)S(1)}) custom-call(bf16[256,256]{1,0:T(8,128)(2,1)S(1)} %collective-permute-done.3.after.refs_1_.rest_1_, bf16[26,128,256]{2,1,0:T(8,128)(2,1)S(1)} %get-tuple-element.30.samples, bf16[10,256,256]{2,1,0:T(8,128)(2,1)S(1)} %get-tuple-element.28.range_tiles, ...), custom_call_target="tpu_custom_call" | custom-call | tf_op jit(solution)/shard_map/own_range/pallas_call | solution.py:240
  32.9 0.0 collective-permute-done.6.refs_1_
  32.9 0.0 collective-permute-done.5.refs_0_
  32.9 0.0 collective-permute-done.7.refs_2_
  33.0 0.2 collective-permute-done.8.rest_5_
  33.2 1.4 %azimuth_most.1.most = f32[2,1,256,1024]{3,2,1,0:T(8,128)S(1)} custom-call(bf16[5,256,256]{2,1,0:T(8,128)(2,1)S(1)} %get-tuple-element.31.az_tiles, bf16[256,256]{1,0:T(8,128)(2,1)S(1)} %collective-permute-done.4.rest_0_.refs_1_, bf16[256,256]{1,0:T(8,128)(2,1)S(1)} %collective-permute-done.3.after.refs_1_.rest_1_, ...), custom_call_target="tpu_custom_call" | custom-call | tf_op jit(solution)/shard_map/azimuth_most/pallas_call | solution.py:378
  34.5 0.6 %collective-permute-done.9.part = bf16[256,256]{1,0:T(8,128)(2,1)S(1)} collective-permute-done((bf16[256,256]{1,0:T(8,128)(2,1)S(1)}, bf16[256,256]{1,0:T(8,128)(2,1)S(1)}, u32[]{:S(2)}, u32[]{:S(2)}) %collective-permute-start.9) | collective-permute-done | bytes 131104 | tf_op jit(solution)/shard_map/ppermute | solution.py:456
  35.2 1.5 %azimuth_last.1 = f32[2,1,256,1024]{3,2,1,0:T(8,128)} custom-call(bf16[5,256,256]{2,1,0:T(8,128)(2,1)S(1)} %get-tuple-element.31.az_tiles, f32[2,1,256,1024]{3,2,1,0:T(8,128)S(1)} %azimuth_most.1.most, bf16[256,256]{1,0:T(8,128)(2,1)S(1)} %collective-permute-done.9.part), custom_call_target="tpu_custom_call" | custom-call | tf_op jit(solution)/shard_map/azimuth_last/pallas_call | solution.py:419
  (4 shorter events, 0.0 us)
Async XLA Ops:
  0.0 13.2 %copy-start = (bf16[64,2048]{1,0:T(8,128)(2,1)S(1)}, bf16[64,2048]{1,0:T(8,128)(2,1)}, u32[]{:S(2)}) copy-start(bf16[64,2048]{1,0:T(8,128)(2,1)} %weights.9) | copy-start | bytes 786436
  0.0 1.3 %copy-start.1 = (bf16[2,128,2048]{2,1,0:T(8,128)(2,1)S(1)}, bf16[2,128,2048]{2,1,0:T(8,128)(2,1)}, u32[]{:S(2)}) copy-start(bf16[2,128,2048]{2,1,0:T(8,128)(2,1)} %echoes.3) | copy-start | bytes 3145732
  1.3 6.1 %copy-start.3 = (bf16[2,1024]{1,0:T(2,128)(2,1)S(1)}, bf16[2,1024]{1,0:T(2,128)(2,1)}, u32[]{:S(2)}) copy-start(bf16[2,1024]{1,0:T(2,128)(2,1)} %range_ref.1) | copy-start | bytes 12292
  1.3 11.9 %copy-start.2 = (s32[2048]{0:T(1024)S(1)}, s32[2048]{0:T(1024)}, u32[]{:S(2)}) copy-start(s32[2048]{0:T(1024)} %param.8) | copy-start | bytes 24580
  1.4 7.2 %collective-permute-start = (bf16[9,128,256]{2,1,0:T(8,128)(2,1)S(1)}, bf16[9,128,256]{2,1,0:T(8,128)(2,1)S(1)}, u32[]{:S(2)}, u32[]{:S(2)}) collective-permute-start(bf16[9,128,256]{2,1,0:T(8,128)(2,1)S(1)} %get-tuple-element.25), channel_id=1, source_target_pairs={{0,1},{2,3},{1,0},{3,2},{4,5},{6,7},{5,4},{7,6},{8,9},{10,11},{9,8... | collective-permute-start | bytes 1769480 | tf_op jit(solution)/shard_map/ppermute | solution.py:440
  1.5 11.7 %collective-permute-start.1 = (bf16[9,128,256]{2,1,0:T(8,128)(2,1)S(1)}, bf16[9,128,256]{2,1,0:T(8,128)(2,1)S(1)}, u32[]{:S(2)}, u32[]{:S(2)}) collective-permute-start(bf16[9,128,256]{2,1,0:T(8,128)(2,1)S(1)} %get-tuple-element.26), channel_id=1, source_target_pairs={{2,1},{6,5},{10,9},{14,13},{18,17},{22,21},{26,25},{30,29}} | collective-permute-start | bytes 1769480 | tf_op jit(solution)/shard_map/ppermute | solution.py:441
  2.8 5.8 %collective-permute-start.2 = (bf16[1,128,256]{2,1,0:T(8,128)(2,1)S(1)}, bf16[1,128,256]{2,1,0:T(8,128)(2,1)S(1)}, u32[]{:S(2)}, u32[]{:S(2)}) collective-permute-start(bf16[1,128,256]{2,1,0:T(8,128)(2,1)S(1)} %get-tuple-element.27), channel_id=1, source_target_pairs={{1,2},{5,6},{9,10},{13,14},{17,18},{21,22},{25,26},{29,30}} | collective-permute-start | bytes 196616 | tf_op jit(solution)/shard_map/ppermute | solution.py:442
  14.8 12.5 %collective-permute-start.3 = (bf16[256,256]{1,0:T(8,128)(2,1)S(1)}, bf16[256,256]{1,0:T(8,128)(2,1)S(1)}, u32[]{:S(2)}, u32[]{:S(2)}) collective-permute-start(bf16[256,256]{1,0:T(8,128)(2,1)S(1)} %get-tuple-element.29), channel_id=1, source_target_pairs={{0,20},{4,16},{8,28},{12,24},{16,4},{20,0},{24,12},{28,8},{1,21},{... | collective-permute-start | bytes 393224 | tf_op jit(solution)/shard_map/ppermute | solution.py:456
  19.1 12.2 %collective-permute-start.4 = (bf16[256,256]{1,0:T(8,128)(2,1)S(1)}, bf16[256,256]{1,0:T(8,128)(2,1)S(1)}, u32[]{:S(2)}, u32[]{:S(2)}) collective-permute-start(bf16[256,256]{1,0:T(8,128)(2,1)S(1)} %get-tuple-element.32.after), channel_id=1, source_target_pairs={{0,16},{4,20},{8,24},{12,28},{16,0},{20,4},{24,8},{28,12},{1,17},{... | collective-permute-start | bytes 393224 | tf_op jit(solution)/shard_map/ppermute | solution.py:456
  21.0 11.9 %collective-permute-start.6 = (bf16[256,256]{1,0:T(8,128)(2,1)S(1)}, bf16[256,256]{1,0:T(8,128)(2,1)S(1)}, u32[]{:S(2)}, u32[]{:S(2)}) collective-permute-start(bf16[256,256]{1,0:T(8,128)(2,1)S(1)} %get-tuple-element.34), channel_id=1, source_target_pairs={{0,28},{4,24},{8,20},{12,16},{16,12},{20,8},{24,4},{28,0},{1,29},{... | collective-permute-start | bytes 393224 | tf_op jit(solution)/shard_map/ppermute | solution.py:456
  24.4 8.5 %collective-permute-start.5 = (bf16[256,256]{1,0:T(8,128)(2,1)S(1)}, bf16[256,256]{1,0:T(8,128)(2,1)S(1)}, u32[]{:S(2)}, u32[]{:S(2)}) collective-permute-start(bf16[256,256]{1,0:T(8,128)(2,1)S(1)} %get-tuple-element.33.after), channel_id=1, source_target_pairs={{0,24},{4,28},{8,16},{12,20},{16,8},{20,12},{24,0},{28,4},{1,25},{... | collective-permute-start | bytes 393224 | tf_op jit(solution)/shard_map/ppermute | solution.py:456
  26.1 6.8 %collective-permute-start.7 = (bf16[256,256]{1,0:T(8,128)(2,1)S(1)}, bf16[256,256]{1,0:T(8,128)(2,1)S(1)}, u32[]{:S(2)}, u32[]{:S(2)}) collective-permute-start(bf16[256,256]{1,0:T(8,128)(2,1)S(1)} %get-tuple-element.37), channel_id=1, source_target_pairs={{0,12},{4,8},{8,4},{12,0},{16,28},{20,24},{24,20},{28,16},{1,13},{... | collective-permute-start | bytes 393224 | tf_op jit(solution)/shard_map/ppermute | solution.py:456
  26.4 5.5 %copy-start.4 = (bf16[2,512]{1,0:T(2,128)(2,1)S(1)}, bf16[2,512]{1,0:T(2,128)(2,1)}, u32[]{:S(2)}) copy-start(bf16[2,512]{1,0:T(2,128)(2,1)} %az_taps.1) | copy-start | bytes 6148
  27.4 5.8 %collective-permute-start.8 = (bf16[256,256]{1,0:T(8,128)(2,1)S(1)}, bf16[256,256]{1,0:T(8,128)(2,1)S(1)}, u32[]{:S(2)}, u32[]{:S(2)}) collective-permute-start(bf16[256,256]{1,0:T(8,128)(2,1)S(1)} %gate.6), channel_id=1, source_target_pairs={{0,4},{4,0},{8,12},{12,8},{16,20},{20,16},{24,28},{28,24},{1,5},{5... | collective-permute-start | bytes 393224 | tf_op jit(solution)/shard_map/ppermute | solution.py:456
  31.3 3.8 %collective-permute-start.9 = (bf16[256,256]{1,0:T(8,128)(2,1)S(1)}, bf16[256,256]{1,0:T(8,128)(2,1)S(1)}, u32[]{:S(2)}, u32[]{:S(2)}) collective-permute-start(bf16[256,256]{1,0:T(8,128)(2,1)S(1)} %gate.7), channel_id=1, source_target_pairs={{0,8},{4,12},{8,0},{12,4},{16,24},{20,28},{24,16},{28,20},{1,9},{5... | collective-permute-start | bytes 393224 | tf_op jit(solution)/shard_map/ppermute | solution.py:456

commit v8 on v7

--- a/solution.py
+++ b/solution.py
@@ -44,15 +44,30 @@
 def pack_body(echoes, near, down, up):
     odd = lax.axis_index("rng") % 2 == 1
 
-    def fill(first, last):
+    def block(part, place):
+        return echoes[part, :, place * BLK : (place + 1) * BLK]
+
+    def put_last(out):
         for part in range(2):
-            lanes = slice(part * BLK, (part + 1) * BLK)
-            for block in range(HEAD):
-                first[block, :, lanes] = echoes[part, :, block * BLK : (block + 1) * BLK]
-            last[0, :, lanes] = echoes[part, :, echoes.shape[2] - BLK :]
-
-    pl.when(odd)(lambda: fill(near, up))
-    pl.when(jnp.logical_not(odd))(lambda: fill(down, near))
+            out[0, :, part * BLK : (part + 1) * BLK] = block(part, echoes.shape[2] // BLK - 1)
+
+    @pl.when(odd)
+    def to_even():
+        for part in range(2):
+            for place in range(HEAD):
+                near[place, :, part * BLK : (part + 1) * BLK] = block(part, place)
+        put_last(up)
+
+    @pl.when(jnp.logical_not(odd))
+    def to_odd():
+        for part in range(2):
+            for place in range(HEAD - 1):
+                down[2 * place + part] = block(part, place)
+        lane = lax.broadcasted_iota(jnp.int32, near.shape[1:2] + (BLK,), 1)
+        real, imag = (block(part, HEAD - 1).astype(jnp.float32) for part in range(2))
+        joined = jnp.where(lane < HALF, real, pltpu.roll(imag, HALF, 1))
+        down[2 * HEAD - 2] = joined.astype(jnp.bfloat16)
+        put_last(near)
 
 
 def pack(echoes):
@@ -60,7 +75,11 @@
     return call(
         pack_body,
         "pack",
-        (bf16(HEAD, pulses, WIDE),) * 2 + (bf16(1, pulses, WIDE),),
+        (
+            bf16(HEAD, pulses, WIDE),
+            bf16(2 * HEAD - 1, pulses, BLK),
+            bf16(1, pulses, WIDE),
+        ),
         [VMEM()],
         (VMEM(),) * 3,
         flops=PACK_FLOPS,
@@ -129,15 +148,26 @@
 
 
 def add_ends(near, down, up, out):
-    count = near.shape[0]
-
-    def ends(low, high):
-        out[0] = low[0]
-        out[out.shape[0] - count :] = high[...]
-
+    start = out.shape[0] - HEAD
     odd = lax.axis_index("rng") % 2 == 1
-    pl.when(odd)(lambda: ends(near, down))
-    pl.when(jnp.logical_not(odd))(lambda: ends(up, near))
+
+    @pl.when(odd)
+    def from_even():
+        out[0] = near[0]
+        for place in range(HEAD - 1):
+            for part in range(2):
+                out[start + place, :, part * BLK : (part + 1) * BLK] = down[2 * place + part]
+        lane = lax.broadcasted_iota(jnp.int32, down.shape[1:], 1)
+        joined = down[2 * HEAD - 2].astype(jnp.float32)
+        for part, value in enumerate((joined, pltpu.roll(joined, HALF, 1))):
+            out[start + HEAD - 1, :, part * BLK : (part + 1) * BLK] = jnp.where(
+                lane < HALF, value, 0.0
+            ).astype(jnp.bfloat16)
+
+    @pl.when(jnp.logical_not(odd))
+    def from_odd():
+        out[0] = up[0]
+        out[start:] = near[...]
 
 
 def compress(samples, range_tiles, block):
@@ -458,19 +488,22 @@
     samples, made = first_range(
         [4, 5], samples, near, down, up, range_tiles, weights, offsets
     )
-    parts = {k: send(piece, k) for k, piece in zip((4, 5), made)}
-    made = next_range([[6, 7]], made[0], samples, range_tiles, weights, offsets)
-    parts.update({k: send(piece, k) for k, piece in zip((6, 7), made)})
-    ready = {}
-    for some in [[2, 3], [1]]:
+    ready = dict(zip([4, 5], made))
+    for some in [[6, 7], [2, 3], [1]]:
         made = next_range([some], made[0], samples, range_tiles, weights, offsets)
         ready.update(zip(some, made))
+    parts = {}
+    parts[4] = send(ready[4], 4)
+    parts[5] = send(ready[5], 5)
+    parts[6] = send(ready[6], 6)
+    parts[7] = send(ready[7], 7)
     parts[3] = send(ready[3], 3)
     parts[1] = send(gate([ready[1]], (parts[5],))[0], 1)
     parts[2] = send(gate([ready[2]], (parts[4],))[0], 2)
-    parts[0], az_tiles = own_range(parts[5], samples, range_tiles, weights, offsets, azimuth_ref)
-    held = gate((parts[6], parts[7]), (), 1000000000) + (parts[3],)
-    parts.update(zip((6, 7, 3), gate(held, (), 2 * 10**8)))
+    after = parts[5]
+    parts[0], az_tiles = own_range(after, samples, range_tiles, weights, offsets, azimuth_ref)
+    parts.update(zip([6, 7], gate((parts[6], parts[7],), (), 1000000000)))
+    parts.update(zip([6, 7, 3], gate((parts[6], parts[7], parts[3],), (), 200000000)))
     last = parts.pop(2)
     most = azimuth_most(list(parts), 2, az_tiles, list(parts.values()))
     return azimuth_last(2, az_tiles, most, last)

time: 36.8 us -> 36.8 us (level)
  starting transfers between devices: 17.1 us -> 16.5 us
  waiting for transfers between devices: 7.78 us -> 8.27 us
    ppermute x7, waiting for transfers between devices: 2.62 us -> 3.46 us  [send(): return lax.ppermute(piece, 'pulse', [(i, i ^ k) for i in range(peers)])]
    ppermute x7, starting transfers between devices: 11.2 us -> 10.6 us  [send(): return lax.ppermute(piece, 'pulse', [(i, i ^ k) for i in range(peers)])]
  transfers between devices with their start and end apart: 10 -> 10, of which waited for: 5 -> 6; matrix products, arithmetic and copies ran while one was open for 0% -> 0% of each run, Pallas kernels for 19% -> 19%
where the time goes in v8:
time: 36.8 us; the launch traced here: 36.7 us
  starting transfers between devices  16.5 us (45%)
  Pallas kernels  10.5 us (29%)
  waiting for transfers between devices  8.27 us (22%)
  local copies, waits for them, and re-layouts  1.28 us (3%)
    ppermute x7, starting transfers between devices, send(): return lax.ppermute(piece, 'pulse', [(i, i ^ k) for i in range(peers)])  10.6 us
    ppermute x1, starting transfers between devices, per_device(): up = lax.ppermute(up, 'rng', chips)  4.51 us
    ppermute x1, waiting for transfers between devices, per_device(): down = lax.ppermute(down, 'rng', [(j, i) for i, j in chips])  4.23 us
    pallas_call x3, Pallas kernels, next_range(): call(functools.partial(next_range_body, steps), 'next_range', (bf16(GROUP...  4.09 us
    ppermute x7, waiting for transfers between devices, send(): return lax.ppermute(piece, 'pulse', [(i, i ^ k) for i in range(peers)])  3.46 us
    pallas_call x1, Pallas kernels, first_range(): pl.pallas_call(functools.partial(first_range_body, steps), out_shape=(jax...  1.69 us
    pallas_call x1, Pallas kernels, azimuth_last(): call(functools.partial(azimuth_last_body, step), 'azimuth_last', jax.Shap...  1.51 us
    pallas_call x1, Pallas kernels, azimuth_most(): call(functools.partial(azimuth_most_body, steps, absent), 'azimuth_most',...  1.36 us
  transfers between devices with their start and end apart: 10, of which 6 were waited for; matrix products, arithmetic and copies ran while one was open for 0% of the time, Pallas kernels for 19%

profile of v8, /device:TPU:1, one launch (start us, length us, event | category | flops | bytes accessed | tf_op | source)
XLA Modules:
  0.0 36.7 jit_solution(6390771454935946596)
XLA Ops:
  0.0 0.0 copy-start
  0.0 0.0 copy-start.1
  0.0 1.3 %copy-done.1 = bf16[2,128,2048]{2,1,0:T(8,128)(2,1)S(1)} copy-done((bf16[2,128,2048]{2,1,0:T(8,128)(2,1)S(1)}, bf16[2,128,2048]{2,1,0:T(8,128)(2,1)}, u32[]{:S(2)}) %copy-start.1) | copy-done | bytes 1048600
  1.3 0.0 copy-start.3
  1.3 0.0 copy-start.2
  1.3 0.1 pack.1
  1.4 0.1 collective-permute-start
  1.5 1.3 %collective-permute-start.1 = (bf16[17,128,128]{2,1,0:T(8,128)(2,1)S(1)}, bf16[17,128,128]{2,1,0:T(8,128)(2,1)S(1)}, u32[]{:S(2)}, u32[]{:S(2)}) collective-permute-start(bf16[17,128,128]{2,1,0:T(8,128)(2,1)S(1)} %get-tuple-element.26), channel_id=1, source_target_pairs={{2,1},{6,5},{10,9},{14,13},{18,17},{22,21},{26,25},{30,29}} | collective-permute-start | bytes 1671176 | tf_op jit(solution)/shard_map/ppermute | solution.py:471
  2.8 4.5 %collective-permute-start.2 = (bf16[1,128,256]{2,1,0:T(8,128)(2,1)S(1)}, bf16[1,128,256]{2,1,0:T(8,128)(2,1)S(1)}, u32[]{:S(2)}, u32[]{:S(2)}) collective-permute-start(bf16[1,128,256]{2,1,0:T(8,128)(2,1)S(1)} %get-tuple-element.27), channel_id=1, source_target_pairs={{1,2},{5,6},{9,10},{13,14},{17,18},{21,22},{25,26},{29,30}} | collective-permute-start | bytes 196616 | tf_op jit(solution)/shard_map/ppermute | solution.py:472
  7.3 0.0 copy-done.3
  7.3 0.7 %prepare.1 = (bf16[26,128,256]{2,1,0:T(8,128)(2,1)S(1)}, bf16[10,256,256]{2,1,0:T(8,128)(2,1)S(1)}) custom-call(bf16[2,128,2048]{2,1,0:T(8,128)(2,1)S(1)} %copy-done.1, bf16[2,1024]{1,0:T(2,128)(2,1)S(1)} %copy-done.3), custom_call_target="tpu_custom_call" | custom-call | tf_op jit(solution)/shard_map/prepare/pallas_call | solution.py:141
  8.0 0.6 %collective-permute-done.2.up = bf16[1,128,256]{2,1,0:T(8,128)(2,1)S(1)} collective-permute-done((bf16[1,128,256]{2,1,0:T(8,128)(2,1)S(1)}, bf16[1,128,256]{2,1,0:T(8,128)(2,1)S(1)}, u32[]{:S(2)}, u32[]{:S(2)}) %collective-permute-start.2) | collective-permute-done | bytes 65568 | tf_op jit(solution)/shard_map/ppermute | solution.py:472
  8.6 4.2 %collective-permute-done.1.down = bf16[17,128,128]{2,1,0:T(8,128)(2,1)S(1)} collective-permute-done((bf16[17,128,128]{2,1,0:T(8,128)(2,1)S(1)}, bf16[17,128,128]{2,1,0:T(8,128)(2,1)S(1)}, u32[]{:S(2)}, u32[]{:S(2)}) %collective-permute-start.1) | collective-permute-done | bytes 557088 | tf_op jit(solution)/shard_map/ppermute | solution.py:471
  12.9 0.0 collective-permute-done.near
  12.9 0.0 copy-done
  12.9 0.0 copy-done.2
  12.9 1.7 %first_range.1 = (bf16[26,128,256]{2,1,0:T(8,128)(2,1)S(1)}, bf16[256,256]{1,0:T(8,128)(2,1)S(1)}, bf16[256,256]{1,0:T(8,128)(2,1)S(1)}) custom-call(bf16[26,128,256]{2,1,0:T(8,128)(2,1)S(1)} %get-tuple-element.24.start, bf16[9,128,256]{2,1,0:T(8,128)(2,1)S(1)} %collective-permute-done.near, ...), custom_call_target="tpu_custom_call", output_to_operand_aliasing={{0}: (0, {})} | custom-call | tf_op jit(solution)/shard_map/first_range/pallas_call | solution.py:217
  14.6 4.3 %collective-permute-start.3 = (bf16[256,256]{1,0:T(8,128)(2,1)S(1)}, bf16[256,256]{1,0:T(8,128)(2,1)S(1)}, u32[]{:S(2)}, u32[]{:S(2)}) collective-permute-start(bf16[256,256]{1,0:T(8,128)(2,1)S(1)} %get-tuple-element.29), channel_id=1, source_target_pairs={{0,20},{4,16},{8,28},{12,24},{16,4},{20,0},{24,12},{28,8},{1,21},{... | collective-permute-start | bytes 393224 | tf_op jit(solution)/shard_map/ppermute | solution.py:486
  18.8 0.4 collective-permute-start.4
  19.2 1.6 %next_range.3 = (bf16[256,256]{1,0:T(8,128)(2,1)S(1)}, bf16[256,256]{1,0:T(8,128)(2,1)S(1)}) custom-call(bf16[256,256]{1,0:T(8,128)(2,1)S(1)} %get-tuple-element.32.after, bf16[26,128,256]{2,1,0:T(8,128)(2,1)S(1)} %get-tuple-element.30.samples, bf16[10,256,256]{2,1,0:T(8,128)(2,1)S(1)} %get-tuple-element.28.range_tiles, bf16[64,2048]{1,0:T(8,128)(2,1)S(1)} %copy-done, ...), custom_call_target="tpu_custom_call" | custom-call | tf_op jit(solution)/shard_map/next_range/pallas_call | solution.py:253
  20.8 3.3 %collective-permute-start.6 = (bf16[256,256]{1,0:T(8,128)(2,1)S(1)}, bf16[256,256]{1,0:T(8,128)(2,1)S(1)}, u32[]{:S(2)}, u32[]{:S(2)}) collective-permute-start(bf16[256,256]{1,0:T(8,128)(2,1)S(1)} %get-tuple-element.34), channel_id=1, source_target_pairs={{0,28},{4,24},{8,20},{12,16},{16,12},{20,8},{24,4},{28,0},{1,29},{... | collective-permute-start | bytes 393224 | tf_op jit(solution)/shard_map/ppermute | solution.py:486
  24.1 0.1 collective-permute-start.5
  24.2 1.6 %next_range.4 = (bf16[256,256]{1,0:T(8,128)(2,1)S(1)}, bf16[256,256]{1,0:T(8,128)(2,1)S(1)}) custom-call(bf16[256,256]{1,0:T(8,128)(2,1)S(1)} %get-tuple-element.33.after, bf16[26,128,256]{2,1,0:T(8,128)(2,1)S(1)} %get-tuple-element.30.samples, bf16[10,256,256]{2,1,0:T(8,128)(2,1)S(1)} %get-tuple-element.28.range_tiles, bf16[64,2048]{1,0:T(8,128)(2,1)S(1)} %copy-done, ...), custom_call_target="tpu_custom_call" | custom-call | tf_op jit(solution)/shard_map/next_range/pallas_call | solution.py:253
  25.8 0.3 collective-permute-start.7
  26.2 0.0 copy-start.4
  26.2 0.9 %next_range.5.refs_0_ = bf16[256,256]{1,0:T(8,128)(2,1)S(1)} custom-call(bf16[256,256]{1,0:T(8,128)(2,1)S(1)} %get-tuple-element.41.after.refs_0_, bf16[26,128,256]{2,1,0:T(8,128)(2,1)S(1)} %get-tuple-element.30.samples, bf16[10,256,256]{2,1,0:T(8,128)(2,1)S(1)} %get-tuple-element.28.range_tiles, bf16[64,2048]{1,0:T(8,128)(2,1)S(1)} %copy-done, ...), custom_call_target="tpu_custom_call" | custom-call | tf_op jit(solution)/shard_map/next_range/pallas_call | solution.py:253
  27.1 0.9 %collective-permute-done.3.after.refs_1_.rest_1_ = bf16[256,256]{1,0:T(8,128)(2,1)S(1)} collective-permute-done((bf16[256,256]{1,0:T(8,128)(2,1)S(1)}, bf16[256,256]{1,0:T(8,128)(2,1)S(1)}, u32[]{:S(2)}, u32[]{:S(2)}) %collective-permute-start.3) | collective-permute-done | bytes 131104 | tf_op jit(solution)/shard_map/ppermute | solution.py:486
  28.0 1.5 %collective-permute-start.8 = (bf16[256,256]{1,0:T(8,128)(2,1)S(1)}, bf16[256,256]{1,0:T(8,128)(2,1)S(1)}, u32[]{:S(2)}, u32[]{:S(2)}) collective-permute-start(bf16[256,256]{1,0:T(8,128)(2,1)S(1)} %gate.6), channel_id=1, source_target_pairs={{0,4},{4,0},{8,12},{12,8},{16,20},{20,16},{24,28},{28,24},{1,5},{5... | collective-permute-start | bytes 393224 | tf_op jit(solution)/shard_map/ppermute | solution.py:486
  29.6 1.8 %collective-permute-done.4.rest_0_.refs_1_ = bf16[256,256]{1,0:T(8,128)(2,1)S(1)} collective-permute-done((bf16[256,256]{1,0:T(8,128)(2,1)S(1)}, bf16[256,256]{1,0:T(8,128)(2,1)S(1)}, u32[]{:S(2)}, u32[]{:S(2)}) %collective-permute-start.4) | collective-permute-done | bytes 131104 | tf_op jit(solution)/shard_map/ppermute | solution.py:486
  31.3 0.7 %collective-permute-start.9 = (bf16[256,256]{1,0:T(8,128)(2,1)S(1)}, bf16[256,256]{1,0:T(8,128)(2,1)S(1)}, u32[]{:S(2)}, u32[]{:S(2)}) collective-permute-start(bf16[256,256]{1,0:T(8,128)(2,1)S(1)} %gate.7), channel_id=1, source_target_pairs={{0,8},{4,12},{8,0},{12,4},{16,24},{20,28},{24,16},{28,20},{1,9},{5... | collective-permute-start | bytes 393224 | tf_op jit(solution)/shard_map/ppermute | solution.py:486
  32.0 0.0 copy-done.4
  32.0 1.0 %own_range.1 = (bf16[256,256]{1,0:T(8,128)(2,1)S(1)}, bf16[5,256,256]{2,1,0:T(8,128)(2,1)S(1)}) custom-call(bf16[256,256]{1,0:T(8,128)(2,1)S(1)} %collective-permute-done.3.after.refs_1_.rest_1_, bf16[26,128,256]{2,1,0:T(8,128)(2,1)S(1)} %get-tuple-element.30.samples, bf16[10,256,256]{2,1,0:T(8,128)(2,1)S(1)} %get-tuple-element.28.range_tiles, ...), custom_call_target="tpu_custom_call" | custom-call | tf_op jit(solution)/shard_map/own_range/pallas_call | solution.py:270
  33.0 0.0 collective-permute-done.6.refs_1_
  33.0 0.0 collective-permute-done.5.refs_0_
  33.0 0.0 collective-permute-done.7.refs_2_
  33.0 0.3 collective-permute-done.8.rest_5_
  33.3 1.4 %azimuth_most.1.most = f32[2,1,256,1024]{3,2,1,0:T(8,128)S(1)} custom-call(bf16[5,256,256]{2,1,0:T(8,128)(2,1)S(1)} %get-tuple-element.31.az_tiles, bf16[256,256]{1,0:T(8,128)(2,1)S(1)} %collective-permute-done.4.rest_0_.refs_1_, bf16[256,256]{1,0:T(8,128)(2,1)S(1)} %collective-permute-done.3.after.refs_1_.rest_1_, ...), custom_call_target="tpu_custom_call" | custom-call | tf_op jit(solution)/shard_map/azimuth_most/pallas_call | solution.py:408
  34.7 0.5 %collective-permute-done.9.part = bf16[256,256]{1,0:T(8,128)(2,1)S(1)} collective-permute-done((bf16[256,256]{1,0:T(8,128)(2,1)S(1)}, bf16[256,256]{1,0:T(8,128)(2,1)S(1)}, u32[]{:S(2)}, u32[]{:S(2)}) %collective-permute-start.9) | collective-permute-done | bytes 131104 | tf_op jit(solution)/shard_map/ppermute | solution.py:486
  35.2 1.5 %azimuth_last.1 = f32[2,1,256,1024]{3,2,1,0:T(8,128)} custom-call(bf16[5,256,256]{2,1,0:T(8,128)(2,1)S(1)} %get-tuple-element.31.az_tiles, f32[2,1,256,1024]{3,2,1,0:T(8,128)S(1)} %azimuth_most.1.most, bf16[256,256]{1,0:T(8,128)(2,1)S(1)} %collective-permute-done.9.part), custom_call_target="tpu_custom_call" | custom-call | tf_op jit(solution)/shard_map/azimuth_last/pallas_call | solution.py:449
  (4 shorter events, 0.0 us)
Async XLA Ops:
  0.0 12.9 %copy-start = (bf16[64,2048]{1,0:T(8,128)(2,1)S(1)}, bf16[64,2048]{1,0:T(8,128)(2,1)}, u32[]{:S(2)}) copy-start(bf16[64,2048]{1,0:T(8,128)(2,1)} %weights.9) | copy-start | bytes 786436
  0.0 1.3 %copy-start.1 = (bf16[2,128,2048]{2,1,0:T(8,128)(2,1)S(1)}, bf16[2,128,2048]{2,1,0:T(8,128)(2,1)}, u32[]{:S(2)}) copy-start(bf16[2,128,2048]{2,1,0:T(8,128)(2,1)} %echoes.3) | copy-start | bytes 3145732
  1.3 6.1 %copy-start.3 = (bf16[2,1024]{1,0:T(2,128)(2,1)S(1)}, bf16[2,1024]{1,0:T(2,128)(2,1)}, u32[]{:S(2)}) copy-start(bf16[2,1024]{1,0:T(2,128)(2,1)} %range_ref.1) | copy-start | bytes 12292
  1.3 11.6 %copy-start.2 = (s32[2048]{0:T(1024)S(1)}, s32[2048]{0:T(1024)}, u32[]{:S(2)}) copy-start(s32[2048]{0:T(1024)} %param.8) | copy-start | bytes 24580
  1.4 11.5 %collective-permute-start = (bf16[9,128,256]{2,1,0:T(8,128)(2,1)S(1)}, bf16[9,128,256]{2,1,0:T(8,128)(2,1)S(1)}, u32[]{:S(2)}, u32[]{:S(2)}) collective-permute-start(bf16[9,128,256]{2,1,0:T(8,128)(2,1)S(1)} %get-tuple-element.25), channel_id=1, source_target_pairs={{0,1},{2,3},{1,0},{3,2},{4,5},{6,7},{5,4},{7,6},{8,9},{10,11},{9,8... | collective-permute-start | bytes 1769480 | tf_op jit(solution)/shard_map/ppermute | solution.py:470
  1.5 11.3 %collective-permute-start.1 = (bf16[17,128,128]{2,1,0:T(8,128)(2,1)S(1)}, bf16[17,128,128]{2,1,0:T(8,128)(2,1)S(1)}, u32[]{:S(2)}, u32[]{:S(2)}) collective-permute-start(bf16[17,128,128]{2,1,0:T(8,128)(2,1)S(1)} %get-tuple-element.26), channel_id=1, source_target_pairs={{2,1},{6,5},{10,9},{14,13},{18,17},{22,21},{26,25},{30,29}} | collective-permute-start | bytes 1671176 | tf_op jit(solution)/shard_map/ppermute | solution.py:471
  2.8 5.8 %collective-permute-start.2 = (bf16[1,128,256]{2,1,0:T(8,128)(2,1)S(1)}, bf16[1,128,256]{2,1,0:T(8,128)(2,1)S(1)}, u32[]{:S(2)}, u32[]{:S(2)}) collective-permute-start(bf16[1,128,256]{2,1,0:T(8,128)(2,1)S(1)} %get-tuple-element.27), channel_id=1, source_target_pairs={{1,2},{5,6},{9,10},{13,14},{17,18},{21,22},{25,26},{29,30}} | collective-permute-start | bytes 196616 | tf_op jit(solution)/shard_map/ppermute | solution.py:472
  14.6 13.4 %collective-permute-start.3 = (bf16[256,256]{1,0:T(8,128)(2,1)S(1)}, bf16[256,256]{1,0:T(8,128)(2,1)S(1)}, u32[]{:S(2)}, u32[]{:S(2)}) collective-permute-start(bf16[256,256]{1,0:T(8,128)(2,1)S(1)} %get-tuple-element.29), channel_id=1, source_target_pairs={{0,20},{4,16},{8,28},{12,24},{16,4},{20,0},{24,12},{28,8},{1,21},{... | collective-permute-start | bytes 393224 | tf_op jit(solution)/shard_map/ppermute | solution.py:486
  18.8 12.5 %collective-permute-start.4 = (bf16[256,256]{1,0:T(8,128)(2,1)S(1)}, bf16[256,256]{1,0:T(8,128)(2,1)S(1)}, u32[]{:S(2)}, u32[]{:S(2)}) collective-permute-start(bf16[256,256]{1,0:T(8,128)(2,1)S(1)} %get-tuple-element.32.after), channel_id=1, source_target_pairs={{0,16},{4,20},{8,24},{12,28},{16,0},{20,4},{24,8},{28,12},{1,17},{... | collective-permute-start | bytes 393224 | tf_op jit(solution)/shard_map/ppermute | solution.py:486
  20.8 12.2 %collective-permute-start.6 = (bf16[256,256]{1,0:T(8,128)(2,1)S(1)}, bf16[256,256]{1,0:T(8,128)(2,1)S(1)}, u32[]{:S(2)}, u32[]{:S(2)}) collective-permute-start(bf16[256,256]{1,0:T(8,128)(2,1)S(1)} %get-tuple-element.34), channel_id=1, source_target_pairs={{0,28},{4,24},{8,20},{12,16},{16,12},{20,8},{24,4},{28,0},{1,29},{... | collective-permute-start | bytes 393224 | tf_op jit(solution)/shard_map/ppermute | solution.py:486
  24.1 8.9 %collective-permute-start.5 = (bf16[256,256]{1,0:T(8,128)(2,1)S(1)}, bf16[256,256]{1,0:T(8,128)(2,1)S(1)}, u32[]{:S(2)}, u32[]{:S(2)}) collective-permute-start(bf16[256,256]{1,0:T(8,128)(2,1)S(1)} %get-tuple-element.33.after), channel_id=1, source_target_pairs={{0,24},{4,28},{8,16},{12,20},{16,8},{20,12},{24,0},{28,4},{1,25},{... | collective-permute-start | bytes 393224 | tf_op jit(solution)/shard_map/ppermute | solution.py:486
  25.8 7.2 %collective-permute-start.7 = (bf16[256,256]{1,0:T(8,128)(2,1)S(1)}, bf16[256,256]{1,0:T(8,128)(2,1)S(1)}, u32[]{:S(2)}, u32[]{:S(2)}) collective-permute-start(bf16[256,256]{1,0:T(8,128)(2,1)S(1)} %get-tuple-element.37), channel_id=1, source_target_pairs={{0,12},{4,8},{8,4},{12,0},{16,28},{20,24},{24,20},{28,16},{1,13},{... | collective-permute-start | bytes 393224 | tf_op jit(solution)/shard_map/ppermute | solution.py:486
  26.2 5.8 %copy-start.4 = (bf16[2,512]{1,0:T(2,128)(2,1)S(1)}, bf16[2,512]{1,0:T(2,128)(2,1)}, u32[]{:S(2)}) copy-start(bf16[2,512]{1,0:T(2,128)(2,1)} %az_taps.1) | copy-start | bytes 6148
  28.0 5.3 %collective-permute-start.8 = (bf16[256,256]{1,0:T(8,128)(2,1)S(1)}, bf16[256,256]{1,0:T(8,128)(2,1)S(1)}, u32[]{:S(2)}, u32[]{:S(2)}) collective-permute-start(bf16[256,256]{1,0:T(8,128)(2,1)S(1)} %gate.6), channel_id=1, source_target_pairs={{0,4},{4,0},{8,12},{12,8},{16,20},{20,16},{24,28},{28,24},{1,5},{5... | collective-permute-start | bytes 393224 | tf_op jit(solution)/shard_map/ppermute | solution.py:486
  31.3 3.8 %collective-permute-start.9 = (bf16[256,256]{1,0:T(8,128)(2,1)S(1)}, bf16[256,256]{1,0:T(8,128)(2,1)S(1)}, u32[]{:S(2)}, u32[]{:S(2)}) collective-permute-start(bf16[256,256]{1,0:T(8,128)(2,1)S(1)} %gate.7), channel_id=1, source_target_pairs={{0,8},{4,12},{8,0},{12,4},{16,24},{20,28},{24,16},{28,20},{1,9},{5... | collective-permute-start | bytes 393224 | tf_op jit(solution)/shard_map/ppermute | solution.py:486

commit v9 on v8

--- a/solution.py
+++ b/solution.py
@@ -19,6 +19,7 @@
 GROUP = 2 * BLK
 LIMIT = 24 * 1024 * 1024
 PACK_FLOPS = 2 * 10**9
+TILE_FLOPS = 2 * 10**9
 
 VMEM = functools.partial(pl.BlockSpec, memory_space=pltpu.VMEM)
 HBM = functools.partial(pl.BlockSpec, memory_space=pltpu.HBM)
@@ -41,7 +42,7 @@
     return jax.ShapeDtypeStruct(shape, jnp.bfloat16)
 
 
-def pack_body(echoes, near, down, up):
+def pack_body(echoes, after, near, down, up):
     odd = lax.axis_index("rng") % 2 == 1
 
     def block(part, place):
@@ -70,7 +71,7 @@
         put_last(near)
 
 
-def pack(echoes):
+def pack(echoes, after):
     pulses = echoes.shape[1]
     return call(
         pack_body,
@@ -80,10 +81,10 @@
             bf16(2 * HEAD - 1, pulses, BLK),
             bf16(1, pulses, WIDE),
         ),
-        [VMEM()],
+        [VMEM()] * 2,
         (VMEM(),) * 3,
         flops=PACK_FLOPS,
-    )(echoes)
+    )(echoes, after)
 
 
 def toeplitz_tiles(taps, tiles, shift, out):
@@ -127,8 +128,22 @@
     return jnp.where(outside & (lane < HALF), 0.0, skewed).astype(jnp.bfloat16)
 
 
-def prepare_body(echoes, range_ref, samples, range_out):
+def range_tiles_body(range_ref, range_out):
     toeplitz_tiles(range_ref, RANGE_TILES, HALF, range_out)
+
+
+def make_range_tiles(range_ref):
+    return call(
+        range_tiles_body,
+        "range_tiles",
+        bf16(RANGE_TILES, WIDE, WIDE),
+        [VMEM()],
+        VMEM(),
+        flops=TILE_FLOPS,
+    )(range_ref)
+
+
+def lay_out_body(echoes, samples):
     for block in range(echoes.shape[2] // BLK):
         for part in range(2):
             samples[block + 1, :, part * BLK : (part + 1) * BLK] = echoes[
@@ -136,15 +151,11 @@
             ]
 
 
-def prepare(echoes, range_ref):
+def lay_out(echoes):
     blocks = 1 + echoes.shape[2] // BLK + HEAD
     return call(
-        prepare_body,
-        "prepare",
-        (bf16(blocks, echoes.shape[1], WIDE), bf16(RANGE_TILES, WIDE, WIDE)),
-        [VMEM()] * 2,
-        (VMEM(),) * 2,
-    )(echoes, range_ref)
+        lay_out_body, "lay_out", bf16(blocks, echoes.shape[1], WIDE), [VMEM()], VMEM()
+    )(echoes)
 
 
 def add_ends(near, down, up, out):
@@ -464,14 +475,15 @@
     peers = lax.axis_size("pulse")
     quarters = lax.axis_size("rng")
     bins = quarter_len // peers
-    near, down, up = pack(echoes)
+    range_tiles = make_range_tiles(range_ref)
+    near, down, up = pack(echoes, range_tiles)
     cores = [(i, i + 1) for i in range(0, quarters - 1, 2)]
     chips = [(i, i + 1) for i in range(1, quarters - 1, 2)]
     near = lax.ppermute(near, "rng", cores + [(j, i) for i, j in cores])
     down = lax.ppermute(down, "rng", [(j, i) for i, j in chips])
     up = lax.ppermute(up, "rng", chips)
     weights, offsets = band_weights, band_offsets.reshape(-1, BLK)
-    samples, range_tiles = prepare(echoes, range_ref)
+    samples = lay_out(echoes)
 
     if bins != GROUP or peers != 8:
         mine, az_tiles = whole_quarter(
@@ -489,7 +501,7 @@
         [4, 5], samples, near, down, up, range_tiles, weights, offsets
     )
     ready = dict(zip([4, 5], made))
-    for some in [[6, 7], [2, 3], [1]]:
+    for some in [[6, 7], [1], [2, 3]]:
         made = next_range([some], made[0], samples, range_tiles, weights, offsets)
         ready.update(zip(some, made))
     parts = {}
@@ -497,13 +509,13 @@
     parts[5] = send(ready[5], 5)
     parts[6] = send(ready[6], 6)
     parts[7] = send(ready[7], 7)
-    parts[3] = send(ready[3], 3)
-    parts[1] = send(gate([ready[1]], (parts[5],))[0], 1)
+    parts[1] = send(ready[1], 1)
+    parts[3] = send(gate([ready[3]], (parts[5],))[0], 3)
     parts[2] = send(gate([ready[2]], (parts[4],))[0], 2)
     after = parts[5]
     parts[0], az_tiles = own_range(after, samples, range_tiles, weights, offsets, azimuth_ref)
     parts.update(zip([6, 7], gate((parts[6], parts[7],), (), 1000000000)))
-    parts.update(zip([6, 7, 3], gate((parts[6], parts[7], parts[3],), (), 200000000)))
+    parts.update(zip([6, 7, 1], gate((parts[6], parts[7], parts[1],), (), 200000000)))
     last = parts.pop(2)
     most = azimuth_most(list(parts), 2, az_tiles, list(parts.values()))
     return azimuth_last(2, az_tiles, most, last)

time: 36.8 us -> 36.8 us (level)
  waiting for transfers between devices: 8.27 us -> 9.11 us
  starting transfers between devices: 16.5 us -> 16 us
  local copies, waits for them, and re-layouts: 1.28 us -> 0.8 us
    ppermute x7, starting transfers between devices: 10.6 us -> 10.1 us  [send(): return lax.ppermute(piece, 'pulse', [(i, i ^ k) for i in range(peers)])]
    ppermute x1, waiting for transfers between devices: 0.58 us -> 1.12 us  [per_device(): up = lax.ppermute(up, 'rng', chips)]
    unnamed x10, local copies, waits for them, and re-layouts: 1.28 us -> 0.8 us
    pallas_call x1 -> x2, Pallas kernels: 0.71 us -> 0.76 us  [the longest x1 0.57 us: make_range_tiles(): call(range_tiles_body, 'range_tiles', bf16(RANGE_TILES, WIDE, WIDE), [VME...]
  transfers between devices with their start and end apart: 10 -> 10, of which waited for: 6 -> 5; matrix products, arithmetic and copies ran while one was open for 0% -> 0% of each run, Pallas kernels for 19% -> 18%
where the time goes in v9:
time: 36.8 us; the launch traced here: 36.6 us
  starting transfers between devices  16 us (43%)
  Pallas kernels  10.5 us (29%)
  waiting for transfers between devices  9.11 us (25%)
  local copies, waits for them, and re-layouts  0.8 us (2%)
    ppermute x7, starting transfers between devices, send(): return lax.ppermute(piece, 'pulse', [(i, i ^ k) for i in range(peers)])  10.1 us
    ppermute x1, starting transfers between devices, per_device(): up = lax.ppermute(up, 'rng', chips)  4.51 us
    ppermute x1, waiting for transfers between devices, per_device(): down = lax.ppermute(down, 'rng', [(j, i) for i, j in chips])  4.23 us
    pallas_call x3, Pallas kernels, next_range(): call(functools.partial(next_range_body, steps), 'next_range', (bf16(GROUP...  4.09 us
    ppermute x7, waiting for transfers between devices, send(): return lax.ppermute(piece, 'pulse', [(i, i ^ k) for i in range(peers)])  3.76 us
    pallas_call x1, Pallas kernels, first_range(): pl.pallas_call(functools.partial(first_range_body, steps), out_shape=(jax...  1.7 us
    pallas_call x1, Pallas kernels, azimuth_last(): call(functools.partial(azimuth_last_body, step), 'azimuth_last', jax.Shap...  1.51 us
    pallas_call x1, Pallas kernels, azimuth_most(): call(functools.partial(azimuth_most_body, steps, absent), 'azimuth_most',...  1.36 us
  transfers between devices with their start and end apart: 10, of which 5 were waited for; matrix products, arithmetic and copies ran while one was open for 0% of the time, Pallas kernels for 18%

profile of v9, /device:TPU:1, one launch (start us, length us, event | category | flops | bytes accessed | tf_op | source)
XLA Modules:
  0.0 36.6 jit_solution(10102370878819261137)
XLA Ops:
  0.0 0.0 copy-start.1
  0.0 0.0 copy-start.4
  0.0 0.8 %copy-done.4 = bf16[2,1024]{1,0:T(2,128)(2,1)S(1)} copy-done((bf16[2,1024]{1,0:T(2,128)(2,1)S(1)}, bf16[2,1024]{1,0:T(2,128)(2,1)}, u32[]{:S(2)}) %copy-start.4) | copy-done | bytes 4120
  0.8 0.6 %range_tiles.1.after = bf16[10,256,256]{2,1,0:T(8,128)(2,1)S(1)} custom-call(bf16[2,1024]{1,0:T(2,128)(2,1)S(1)} %copy-done.4), custom_call_target="tpu_custom_call" | custom-call | flops 2000000000 | tf_op jit(solution)/shard_map/range_tiles/pallas_call | solution.py:136
  1.4 0.0 copy-done.1
  1.4 0.1 pack.1
  1.5 0.0 copy-start
  1.5 0.0 copy-start.2
  1.5 0.1 collective-permute-start
  1.7 1.3 %collective-permute-start.1 = (bf16[17,128,128]{2,1,0:T(8,128)(2,1)S(1)}, bf16[17,128,128]{2,1,0:T(8,128)(2,1)S(1)}, u32[]{:S(2)}, u32[]{:S(2)}) collective-permute-start(bf16[17,128,128]{2,1,0:T(8,128)(2,1)S(1)} %get-tuple-element.23), channel_id=1, source_target_pairs={{2,1},{6,5},{10,9},{14,13},{18,17},{22,21},{26,25},{30,29}} | collective-permute-start | bytes 1671176 | tf_op jit(solution)/shard_map/ppermute | solution.py:483
  2.9 4.5 %collective-permute-start.2 = (bf16[1,128,256]{2,1,0:T(8,128)(2,1)S(1)}, bf16[1,128,256]{2,1,0:T(8,128)(2,1)S(1)}, u32[]{:S(2)}, u32[]{:S(2)}) collective-permute-start(bf16[1,128,256]{2,1,0:T(8,128)(2,1)S(1)} %get-tuple-element.24), channel_id=1, source_target_pairs={{1,2},{5,6},{9,10},{13,14},{17,18},{21,22},{25,26},{29,30}} | collective-permute-start | bytes 196616 | tf_op jit(solution)/shard_map/ppermute | solution.py:484
  7.5 0.2 lay_out.1.start
  7.6 1.1 %collective-permute-done.2.up = bf16[1,128,256]{2,1,0:T(8,128)(2,1)S(1)} collective-permute-done((bf16[1,128,256]{2,1,0:T(8,128)(2,1)S(1)}, bf16[1,128,256]{2,1,0:T(8,128)(2,1)S(1)}, u32[]{:S(2)}, u32[]{:S(2)}) %collective-permute-start.2) | collective-permute-done | bytes 65568 | tf_op jit(solution)/shard_map/ppermute | solution.py:484
  8.8 4.2 %collective-permute-done.1.down = bf16[17,128,128]{2,1,0:T(8,128)(2,1)S(1)} collective-permute-done((bf16[17,128,128]{2,1,0:T(8,128)(2,1)S(1)}, bf16[17,128,128]{2,1,0:T(8,128)(2,1)S(1)}, u32[]{:S(2)}, u32[]{:S(2)}) %collective-permute-start.1) | collective-permute-done | bytes 557088 | tf_op jit(solution)/shard_map/ppermute | solution.py:483
  13.0 0.0 collective-permute-done.near
  13.0 0.0 copy-done
  13.0 0.0 copy-done.2
  13.0 1.7 %first_range.1 = (bf16[26,128,256]{2,1,0:T(8,128)(2,1)S(1)}, bf16[256,256]{1,0:T(8,128)(2,1)S(1)}, bf16[256,256]{1,0:T(8,128)(2,1)S(1)}) custom-call(bf16[26,128,256]{2,1,0:T(8,128)(2,1)S(1)} %lay_out.1.start, bf16[9,128,256]{2,1,0:T(8,128)(2,1)S(1)} %collective-permute-done.near, ...), custom_call_target="tpu_custom_call", output_to_operand_aliasing={{0}: (0, {})} | custom-call | tf_op jit(solution)/shard_map/first_range/pallas_call | solution.py:228
  14.7 4.3 %collective-permute-start.3 = (bf16[256,256]{1,0:T(8,128)(2,1)S(1)}, bf16[256,256]{1,0:T(8,128)(2,1)S(1)}, u32[]{:S(2)}, u32[]{:S(2)}) collective-permute-start(bf16[256,256]{1,0:T(8,128)(2,1)S(1)} %get-tuple-element.25), channel_id=1, source_target_pairs={{0,20},{4,16},{8,28},{12,24},{16,4},{20,0},{24,12},{28,8},{1,21},{... | collective-permute-start | bytes 393224 | tf_op jit(solution)/shard_map/ppermute | solution.py:498
  19.0 0.4 collective-permute-start.4
  19.3 1.6 %next_range.3 = (bf16[256,256]{1,0:T(8,128)(2,1)S(1)}, bf16[256,256]{1,0:T(8,128)(2,1)S(1)}) custom-call(bf16[256,256]{1,0:T(8,128)(2,1)S(1)} %get-tuple-element.28.after, bf16[26,128,256]{2,1,0:T(8,128)(2,1)S(1)} %get-tuple-element.26.samples, bf16[10,256,256]{2,1,0:T(8,128)(2,1)S(1)} %range_tiles.1.after, bf16[64,2048]{1,0:T(8,128)(2,1)S(1)} %copy-done, ...), custom_call_target="tpu_custom_call" | custom-call | tf_op jit(solution)/shard_map/next_range/pallas_call | solution.py:264
  20.9 3.3 %collective-permute-start.6 = (bf16[256,256]{1,0:T(8,128)(2,1)S(1)}, bf16[256,256]{1,0:T(8,128)(2,1)S(1)}, u32[]{:S(2)}, u32[]{:S(2)}) collective-permute-start(bf16[256,256]{1,0:T(8,128)(2,1)S(1)} %get-tuple-element.30), channel_id=1, source_target_pairs={{0,28},{4,24},{8,20},{12,16},{16,12},{20,8},{24,4},{28,0},{1,29},{... | collective-permute-start | bytes 393224 | tf_op jit(solution)/shard_map/ppermute | solution.py:498
  24.2 0.1 collective-permute-start.5
  24.4 0.9 %next_range.4.after = bf16[256,256]{1,0:T(8,128)(2,1)S(1)} custom-call(bf16[256,256]{1,0:T(8,128)(2,1)S(1)} %get-tuple-element.29.after, bf16[26,128,256]{2,1,0:T(8,128)(2,1)S(1)} %get-tuple-element.26.samples, bf16[10,256,256]{2,1,0:T(8,128)(2,1)S(1)} %range_tiles.1.after, bf16[64,2048]{1,0:T(8,128)(2,1)S(1)} %copy-done, s32[16,128]{1,0:T(8,128)S(1)} %bitcast.3), custom_call_target="tpu_custom_call" | custom-call | tf_op jit(solution)/shard_map/next_range/pallas_call | solution.py:264
  25.3 0.0 copy-start.3
  25.3 1.2 %collective-permute-start.7 = (bf16[256,256]{1,0:T(8,128)(2,1)S(1)}, bf16[256,256]{1,0:T(8,128)(2,1)S(1)}, u32[]{:S(2)}, u32[]{:S(2)}) collective-permute-start(bf16[256,256]{1,0:T(8,128)(2,1)S(1)} %next_range.4.after), channel_id=1, source_target_pairs={{0,4},{4,0},{8,12},{12,8},{16,20},{20,16},{24,28},{28,24},{1,5},{5... | collective-permute-start | bytes 393224 | tf_op jit(solution)/shard_map/ppermute | solution.py:498
  26.5 1.6 %next_range.5 = (bf16[256,256]{1,0:T(8,128)(2,1)S(1)}, bf16[256,256]{1,0:T(8,128)(2,1)S(1)}) custom-call(bf16[256,256]{1,0:T(8,128)(2,1)S(1)} %next_range.4.after, bf16[26,128,256]{2,1,0:T(8,128)(2,1)S(1)} %get-tuple-element.26.samples, bf16[10,256,256]{2,1,0:T(8,128)(2,1)S(1)} %range_tiles.1.after, bf16[64,2048]{1,0:T(8,128)(2,1)S(1)} %copy-done, ...), custom_call_target="tpu_custom_call" | custom-call | tf_op jit(solution)/shard_map/next_range/pallas_call | solution.py:264
  28.1 0.0 collective-permute-done.3.after.refs_1_.rest_1_
  28.1 0.1 collective-permute-start.8
  28.2 3.1 %collective-permute-done.4.rest_0_.refs_1_ = bf16[256,256]{1,0:T(8,128)(2,1)S(1)} collective-permute-done((bf16[256,256]{1,0:T(8,128)(2,1)S(1)}, bf16[256,256]{1,0:T(8,128)(2,1)S(1)}, u32[]{:S(2)}, u32[]{:S(2)}) %collective-permute-start.4) | collective-permute-done | bytes 131104 | tf_op jit(solution)/shard_map/ppermute | solution.py:498
  31.3 0.7 %collective-permute-start.9 = (bf16[256,256]{1,0:T(8,128)(2,1)S(1)}, bf16[256,256]{1,0:T(8,128)(2,1)S(1)}, u32[]{:S(2)}, u32[]{:S(2)}) collective-permute-start(bf16[256,256]{1,0:T(8,128)(2,1)S(1)} %gate.7), channel_id=1, source_target_pairs={{0,8},{4,12},{8,0},{12,4},{16,24},{20,28},{24,16},{28,20},{1,9},{5... | collective-permute-start | bytes 393224 | tf_op jit(solution)/shard_map/ppermute | solution.py:498
  32.0 0.0 copy-done.3
  32.0 1.0 %own_range.1 = (bf16[256,256]{1,0:T(8,128)(2,1)S(1)}, bf16[5,256,256]{2,1,0:T(8,128)(2,1)S(1)}) custom-call(bf16[256,256]{1,0:T(8,128)(2,1)S(1)} %collective-permute-done.3.after.refs_1_.rest_1_, bf16[26,128,256]{2,1,0:T(8,128)(2,1)S(1)} %get-tuple-element.26.samples, bf16[10,256,256]{2,1,0:T(8,128)(2,1)S(1)} %range_tiles.1.after, ...), custom_call_target="tpu_custom_call" | custom-call | tf_op jit(solution)/shard_map/own_range/pallas_call | solution.py:281
  32.9 0.0 collective-permute-done.6.refs_1_
  33.0 0.0 collective-permute-done.5.refs_0_
  33.0 0.0 collective-permute-done.7.refs_2_
  33.0 0.4 %collective-permute-done.8.rest_5_ = bf16[256,256]{1,0:T(8,128)(2,1)S(1)} collective-permute-done((bf16[256,256]{1,0:T(8,128)(2,1)S(1)}, bf16[256,256]{1,0:T(8,128)(2,1)S(1)}, u32[]{:S(2)}, u32[]{:S(2)}) %collective-permute-start.8) | collective-permute-done | bytes 131104 | tf_op jit(solution)/shard_map/ppermute | solution.py:498
  33.4 1.4 %azimuth_most.1.most = f32[2,1,256,1024]{3,2,1,0:T(8,128)S(1)} custom-call(bf16[5,256,256]{2,1,0:T(8,128)(2,1)S(1)} %get-tuple-element.27.az_tiles, bf16[256,256]{1,0:T(8,128)(2,1)S(1)} %collective-permute-done.4.rest_0_.refs_1_, bf16[256,256]{1,0:T(8,128)(2,1)S(1)} %collective-permute-done.3.after.refs_1_.rest_1_, ...), custom_call_target="tpu_custom_call" | custom-call | tf_op jit(solution)/shard_map/azimuth_most/pallas_call | solution.py:419
  34.8 0.3 collective-permute-done.9.part
  35.1 1.5 %azimuth_last.1 = f32[2,1,256,1024]{3,2,1,0:T(8,128)} custom-call(bf16[5,256,256]{2,1,0:T(8,128)(2,1)S(1)} %get-tuple-element.27.az_tiles, f32[2,1,256,1024]{3,2,1,0:T(8,128)S(1)} %azimuth_most.1.most, bf16[256,256]{1,0:T(8,128)(2,1)S(1)} %collective-permute-done.9.part), custom_call_target="tpu_custom_call" | custom-call | tf_op jit(solution)/shard_map/azimuth_last/pallas_call | solution.py:460
  (4 shorter events, 0.0 us)
Async XLA Ops:
  0.0 1.4 %copy-start.1 = (bf16[2,128,2048]{2,1,0:T(8,128)(2,1)S(1)}, bf16[2,128,2048]{2,1,0:T(8,128)(2,1)}, u32[]{:S(2)}) copy-start(bf16[2,128,2048]{2,1,0:T(8,128)(2,1)} %echoes.3) | copy-start | bytes 3145732
  0.0 0.8 %copy-start.4 = (bf16[2,1024]{1,0:T(2,128)(2,1)S(1)}, bf16[2,1024]{1,0:T(2,128)(2,1)}, u32[]{:S(2)}) copy-start(bf16[2,1024]{1,0:T(2,128)(2,1)} %range_ref.1) | copy-start | bytes 12292
  1.5 11.5 %copy-start = (bf16[64,2048]{1,0:T(8,128)(2,1)S(1)}, bf16[64,2048]{1,0:T(8,128)(2,1)}, u32[]{:S(2)}) copy-start(bf16[64,2048]{1,0:T(8,128)(2,1)} %weights.9) | copy-start | bytes 786436
  1.5 11.5 %copy-start.2 = (s32[2048]{0:T(1024)S(1)}, s32[2048]{0:T(1024)}, u32[]{:S(2)}) copy-start(s32[2048]{0:T(1024)} %param.8) | copy-start | bytes 24580
  1.5 11.5 %collective-permute-start = (bf16[9,128,256]{2,1,0:T(8,128)(2,1)S(1)}, bf16[9,128,256]{2,1,0:T(8,128)(2,1)S(1)}, u32[]{:S(2)}, u32[]{:S(2)}) collective-permute-start(bf16[9,128,256]{2,1,0:T(8,128)(2,1)S(1)} %get-tuple-element.22), channel_id=1, source_target_pairs={{0,1},{2,3},{1,0},{3,2},{4,5},{6,7},{5,4},{7,6},{8,9},{10,11},{9,8... | collective-permute-start | bytes 1769480 | tf_op jit(solution)/shard_map/ppermute | solution.py:482
  1.7 11.3 %collective-permute-start.1 = (bf16[17,128,128]{2,1,0:T(8,128)(2,1)S(1)}, bf16[17,128,128]{2,1,0:T(8,128)(2,1)S(1)}, u32[]{:S(2)}, u32[]{:S(2)}) collective-permute-start(bf16[17,128,128]{2,1,0:T(8,128)(2,1)S(1)} %get-tuple-element.23), channel_id=1, source_target_pairs={{2,1},{6,5},{10,9},{14,13},{18,17},{22,21},{26,25},{30,29}} | collective-permute-start | bytes 1671176 | tf_op jit(solution)/shard_map/ppermute | solution.py:483
  2.9 5.8 %collective-permute-start.2 = (bf16[1,128,256]{2,1,0:T(8,128)(2,1)S(1)}, bf16[1,128,256]{2,1,0:T(8,128)(2,1)S(1)}, u32[]{:S(2)}, u32[]{:S(2)}) collective-permute-start(bf16[1,128,256]{2,1,0:T(8,128)(2,1)S(1)} %get-tuple-element.24), channel_id=1, source_target_pairs={{1,2},{5,6},{9,10},{13,14},{17,18},{21,22},{25,26},{29,30}} | collective-permute-start | bytes 196616 | tf_op jit(solution)/shard_map/ppermute | solution.py:484
  14.7 13.4 %collective-permute-start.3 = (bf16[256,256]{1,0:T(8,128)(2,1)S(1)}, bf16[256,256]{1,0:T(8,128)(2,1)S(1)}, u32[]{:S(2)}, u32[]{:S(2)}) collective-permute-start(bf16[256,256]{1,0:T(8,128)(2,1)S(1)} %get-tuple-element.25), channel_id=1, source_target_pairs={{0,20},{4,16},{8,28},{12,24},{16,4},{20,0},{24,12},{28,8},{1,21},{... | collective-permute-start | bytes 393224 | tf_op jit(solution)/shard_map/ppermute | solution.py:498
  19.0 12.3 %collective-permute-start.4 = (bf16[256,256]{1,0:T(8,128)(2,1)S(1)}, bf16[256,256]{1,0:T(8,128)(2,1)S(1)}, u32[]{:S(2)}, u32[]{:S(2)}) collective-permute-start(bf16[256,256]{1,0:T(8,128)(2,1)S(1)} %get-tuple-element.28.after), channel_id=1, source_target_pairs={{0,16},{4,20},{8,24},{12,28},{16,0},{20,4},{24,8},{28,12},{1,17},{... | collective-permute-start | bytes 393224 | tf_op jit(solution)/shard_map/ppermute | solution.py:498
  20.9 12.0 %collective-permute-start.6 = (bf16[256,256]{1,0:T(8,128)(2,1)S(1)}, bf16[256,256]{1,0:T(8,128)(2,1)S(1)}, u32[]{:S(2)}, u32[]{:S(2)}) collective-permute-start(bf16[256,256]{1,0:T(8,128)(2,1)S(1)} %get-tuple-element.30), channel_id=1, source_target_pairs={{0,28},{4,24},{8,20},{12,16},{16,12},{20,8},{24,4},{28,0},{1,29},{... | collective-permute-start | bytes 393224 | tf_op jit(solution)/shard_map/ppermute | solution.py:498
  24.2 8.7 %collective-permute-start.5 = (bf16[256,256]{1,0:T(8,128)(2,1)S(1)}, bf16[256,256]{1,0:T(8,128)(2,1)S(1)}, u32[]{:S(2)}, u32[]{:S(2)}) collective-permute-start(bf16[256,256]{1,0:T(8,128)(2,1)S(1)} %get-tuple-element.29.after), channel_id=1, source_target_pairs={{0,24},{4,28},{8,16},{12,20},{16,8},{20,12},{24,0},{28,4},{1,25},{... | collective-permute-start | bytes 393224 | tf_op jit(solution)/shard_map/ppermute | solution.py:498
  25.3 6.6 %copy-start.3 = (bf16[2,512]{1,0:T(2,128)(2,1)S(1)}, bf16[2,512]{1,0:T(2,128)(2,1)}, u32[]{:S(2)}) copy-start(bf16[2,512]{1,0:T(2,128)(2,1)} %az_taps.1) | copy-start | bytes 6148
  25.3 7.6 %collective-permute-start.7 = (bf16[256,256]{1,0:T(8,128)(2,1)S(1)}, bf16[256,256]{1,0:T(8,128)(2,1)S(1)}, u32[]{:S(2)}, u32[]{:S(2)}) collective-permute-start(bf16[256,256]{1,0:T(8,128)(2,1)S(1)} %next_range.4.after), channel_id=1, source_target_pairs={{0,4},{4,0},{8,12},{12,8},{16,20},{20,16},{24,28},{28,24},{1,5},{5... | collective-permute-start | bytes 393224 | tf_op jit(solution)/shard_map/ppermute | solution.py:498
  28.1 5.3 %collective-permute-start.8 = (bf16[256,256]{1,0:T(8,128)(2,1)S(1)}, bf16[256,256]{1,0:T(8,128)(2,1)S(1)}, u32[]{:S(2)}, u32[]{:S(2)}) collective-permute-start(bf16[256,256]{1,0:T(8,128)(2,1)S(1)} %gate.6), channel_id=1, source_target_pairs={{0,12},{4,8},{8,4},{12,0},{16,28},{20,24},{24,20},{28,16},{1,13},{... | collective-permute-start | bytes 393224 | tf_op jit(solution)/shard_map/ppermute | solution.py:498
  31.3 3.8 %collective-permute-start.9 = (bf16[256,256]{1,0:T(8,128)(2,1)S(1)}, bf16[256,256]{1,0:T(8,128)(2,1)S(1)}, u32[]{:S(2)}, u32[]{:S(2)}) collective-permute-start(bf16[256,256]{1,0:T(8,128)(2,1)S(1)} %gate.7), channel_id=1, source_target_pairs={{0,8},{4,12},{8,0},{12,4},{16,24},{20,28},{24,16},{28,20},{1,9},{5... | collective-permute-start | bytes 393224 | tf_op jit(solution)/shard_map/ppermute | solution.py:498

commit v10 on v9

--- a/solution.py
+++ b/solution.py
@@ -512,7 +512,7 @@
     parts[1] = send(ready[1], 1)
     parts[3] = send(gate([ready[3]], (parts[5],))[0], 3)
     parts[2] = send(gate([ready[2]], (parts[4],))[0], 2)
-    after = parts[5]
+    after = parts[6]
     parts[0], az_tiles = own_range(after, samples, range_tiles, weights, offsets, azimuth_ref)
     parts.update(zip([6, 7], gate((parts[6], parts[7],), (), 1000000000)))
     parts.update(zip([6, 7, 1], gate((parts[6], parts[7], parts[1],), (), 200000000)))

time: 36.8 us -> 36.8 us (level)
  no operation moved by 1% of the time
where the time goes in v10:
time: 36.8 us; the launch traced here: 36.6 us
  starting transfers between devices  16 us (43%)
  Pallas kernels  10.5 us (29%)
  waiting for transfers between devices  9.07 us (25%)
  local copies, waits for them, and re-layouts  0.8 us (2%)
    ppermute x7, starting transfers between devices, send(): return lax.ppermute(piece, 'pulse', [(i, i ^ k) for i in range(peers)])  10.1 us
    ppermute x1, starting transfers between devices, per_device(): up = lax.ppermute(up, 'rng', chips)  4.51 us
    ppermute x1, waiting for transfers between devices, per_device(): down = lax.ppermute(down, 'rng', [(j, i) for i, j in chips])  4.23 us
    pallas_call x3, Pallas kernels, next_range(): call(functools.partial(next_range_body, steps), 'next_range', (bf16(GROUP...  4.09 us
    ppermute x7, waiting for transfers between devices, send(): return lax.ppermute(piece, 'pulse', [(i, i ^ k) for i in range(peers)])  3.73 us
    pallas_call x1, Pallas kernels, first_range(): pl.pallas_call(functools.partial(first_range_body, steps), out_shape=(jax...  1.7 us
    pallas_call x1, Pallas kernels, azimuth_last(): call(functools.partial(azimuth_last_body, step), 'azimuth_last', jax.Shap...  1.51 us
    pallas_call x1, Pallas kernels, azimuth_most(): call(functools.partial(azimuth_most_body, steps, absent), 'azimuth_most',...  1.36 us
  transfers between devices with their start and end apart: 10, of which 5 were waited for; matrix products, arithmetic and copies ran while one was open for 0% of the time, Pallas kernels for 18%

profile of v10, /device:TPU:1, one launch (start us, length us, event | category | flops | bytes accessed | tf_op | source)
XLA Modules:
  0.0 36.6 jit_solution(8437955026787410930)
XLA Ops:
  0.0 0.0 copy-start.1
  0.0 0.0 copy-start.4
  0.0 0.8 %copy-done.4 = bf16[2,1024]{1,0:T(2,128)(2,1)S(1)} copy-done((bf16[2,1024]{1,0:T(2,128)(2,1)S(1)}, bf16[2,1024]{1,0:T(2,128)(2,1)}, u32[]{:S(2)}) %copy-start.4) | copy-done | bytes 4120
  0.8 0.6 %range_tiles.1.after = bf16[10,256,256]{2,1,0:T(8,128)(2,1)S(1)} custom-call(bf16[2,1024]{1,0:T(2,128)(2,1)S(1)} %copy-done.4), custom_call_target="tpu_custom_call" | custom-call | flops 2000000000 | tf_op jit(solution)/shard_map/range_tiles/pallas_call | solution.py:136
  1.4 0.0 copy-done.1
  1.4 0.1 pack.1
  1.5 0.0 copy-start
  1.5 0.0 copy-start.2
  1.5 0.1 collective-permute-start
  1.7 1.3 %collective-permute-start.1 = (bf16[17,128,128]{2,1,0:T(8,128)(2,1)S(1)}, bf16[17,128,128]{2,1,0:T(8,128)(2,1)S(1)}, u32[]{:S(2)}, u32[]{:S(2)}) collective-permute-start(bf16[17,128,128]{2,1,0:T(8,128)(2,1)S(1)} %get-tuple-element.23), channel_id=1, source_target_pairs={{2,1},{6,5},{10,9},{14,13},{18,17},{22,21},{26,25},{30,29}} | collective-permute-start | bytes 1671176 | tf_op jit(solution)/shard_map/ppermute | solution.py:483
  2.9 4.5 %collective-permute-start.2 = (bf16[1,128,256]{2,1,0:T(8,128)(2,1)S(1)}, bf16[1,128,256]{2,1,0:T(8,128)(2,1)S(1)}, u32[]{:S(2)}, u32[]{:S(2)}) collective-permute-start(bf16[1,128,256]{2,1,0:T(8,128)(2,1)S(1)} %get-tuple-element.24), channel_id=1, source_target_pairs={{1,2},{5,6},{9,10},{13,14},{17,18},{21,22},{25,26},{29,30}} | collective-permute-start | bytes 196616 | tf_op jit(solution)/shard_map/ppermute | solution.py:484
  7.5 0.2 lay_out.1.start
  7.6 1.1 %collective-permute-done.2.up = bf16[1,128,256]{2,1,0:T(8,128)(2,1)S(1)} collective-permute-done((bf16[1,128,256]{2,1,0:T(8,128)(2,1)S(1)}, bf16[1,128,256]{2,1,0:T(8,128)(2,1)S(1)}, u32[]{:S(2)}, u32[]{:S(2)}) %collective-permute-start.2) | collective-permute-done | bytes 65568 | tf_op jit(solution)/shard_map/ppermute | solution.py:484
  8.8 4.2 %collective-permute-done.1.down = bf16[17,128,128]{2,1,0:T(8,128)(2,1)S(1)} collective-permute-done((bf16[17,128,128]{2,1,0:T(8,128)(2,1)S(1)}, bf16[17,128,128]{2,1,0:T(8,128)(2,1)S(1)}, u32[]{:S(2)}, u32[]{:S(2)}) %collective-permute-start.1) | collective-permute-done | bytes 557088 | tf_op jit(solution)/shard_map/ppermute | solution.py:483
  13.0 0.0 collective-permute-done.near
  13.0 0.0 copy-done
  13.0 0.0 copy-done.2
  13.0 1.7 %first_range.1 = (bf16[26,128,256]{2,1,0:T(8,128)(2,1)S(1)}, bf16[256,256]{1,0:T(8,128)(2,1)S(1)}, bf16[256,256]{1,0:T(8,128)(2,1)S(1)}) custom-call(bf16[26,128,256]{2,1,0:T(8,128)(2,1)S(1)} %lay_out.1.start, bf16[9,128,256]{2,1,0:T(8,128)(2,1)S(1)} %collective-permute-done.near, ...), custom_call_target="tpu_custom_call", output_to_operand_aliasing={{0}: (0, {})} | custom-call | tf_op jit(solution)/shard_map/first_range/pallas_call | solution.py:228
  14.7 4.3 %collective-permute-start.5 = (bf16[256,256]{1,0:T(8,128)(2,1)S(1)}, bf16[256,256]{1,0:T(8,128)(2,1)S(1)}, u32[]{:S(2)}, u32[]{:S(2)}) collective-permute-start(bf16[256,256]{1,0:T(8,128)(2,1)S(1)} %get-tuple-element.29), channel_id=1, source_target_pairs={{0,20},{4,16},{8,28},{12,24},{16,4},{20,0},{24,12},{28,8},{1,21},{... | collective-permute-start | bytes 393224 | tf_op jit(solution)/shard_map/ppermute | solution.py:498
  19.0 0.4 collective-permute-start.4
  19.3 1.6 %next_range.3 = (bf16[256,256]{1,0:T(8,128)(2,1)S(1)}, bf16[256,256]{1,0:T(8,128)(2,1)S(1)}) custom-call(bf16[256,256]{1,0:T(8,128)(2,1)S(1)} %get-tuple-element.25.after, bf16[26,128,256]{2,1,0:T(8,128)(2,1)S(1)} %get-tuple-element.26.samples, bf16[10,256,256]{2,1,0:T(8,128)(2,1)S(1)} %range_tiles.1.after, bf16[64,2048]{1,0:T(8,128)(2,1)S(1)} %copy-done, ...), custom_call_target="tpu_custom_call" | custom-call | tf_op jit(solution)/shard_map/next_range/pallas_call | solution.py:264
  20.9 3.4 %collective-permute-start.3 = (bf16[256,256]{1,0:T(8,128)(2,1)S(1)}, bf16[256,256]{1,0:T(8,128)(2,1)S(1)}, u32[]{:S(2)}, u32[]{:S(2)}) collective-permute-start(bf16[256,256]{1,0:T(8,128)(2,1)S(1)} %get-tuple-element.27.after), channel_id=1, source_target_pairs={{0,24},{4,28},{8,16},{12,20},{16,8},{20,12},{24,0},{28,4},{1,25},{... | collective-permute-start | bytes 393224 | tf_op jit(solution)/shard_map/ppermute | solution.py:498
  24.3 0.0 collective-permute-start.6
  24.3 0.9 %next_range.4.after = bf16[256,256]{1,0:T(8,128)(2,1)S(1)} custom-call(bf16[256,256]{1,0:T(8,128)(2,1)S(1)} %get-tuple-element.27.after, bf16[26,128,256]{2,1,0:T(8,128)(2,1)S(1)} %get-tuple-element.26.samples, bf16[10,256,256]{2,1,0:T(8,128)(2,1)S(1)} %range_tiles.1.after, bf16[64,2048]{1,0:T(8,128)(2,1)S(1)} %copy-done, s32[16,128]{1,0:T(8,128)S(1)} %bitcast.3), custom_call_target="tpu_custom_call" | custom-call | tf_op jit(solution)/shard_map/next_range/pallas_call | solution.py:264
  25.3 0.0 copy-start.3
  25.3 1.3 %collective-permute-start.7 = (bf16[256,256]{1,0:T(8,128)(2,1)S(1)}, bf16[256,256]{1,0:T(8,128)(2,1)S(1)}, u32[]{:S(2)}, u32[]{:S(2)}) collective-permute-start(bf16[256,256]{1,0:T(8,128)(2,1)S(1)} %next_range.4.after), channel_id=1, source_target_pairs={{0,4},{4,0},{8,12},{12,8},{16,20},{20,16},{24,28},{28,24},{1,5},{5... | collective-permute-start | bytes 393224 | tf_op jit(solution)/shard_map/ppermute | solution.py:498
  26.6 1.6 %next_range.5 = (bf16[256,256]{1,0:T(8,128)(2,1)S(1)}, bf16[256,256]{1,0:T(8,128)(2,1)S(1)}) custom-call(bf16[256,256]{1,0:T(8,128)(2,1)S(1)} %next_range.4.after, bf16[26,128,256]{2,1,0:T(8,128)(2,1)S(1)} %get-tuple-element.26.samples, bf16[10,256,256]{2,1,0:T(8,128)(2,1)S(1)} %range_tiles.1.after, bf16[64,2048]{1,0:T(8,128)(2,1)S(1)} %copy-done, ...), custom_call_target="tpu_custom_call" | custom-call | tf_op jit(solution)/shard_map/next_range/pallas_call | solution.py:264
  28.2 0.0 collective-permute-done.5.refs_1_.rest_1_
  28.2 0.1 collective-permute-start.8
  28.3 3.0 %collective-permute-done.4.rest_0_.refs_1_ = bf16[256,256]{1,0:T(8,128)(2,1)S(1)} collective-permute-done((bf16[256,256]{1,0:T(8,128)(2,1)S(1)}, bf16[256,256]{1,0:T(8,128)(2,1)S(1)}, u32[]{:S(2)}, u32[]{:S(2)}) %collective-permute-start.4) | collective-permute-done | bytes 131104 | tf_op jit(solution)/shard_map/ppermute | solution.py:498
  31.3 0.7 %collective-permute-start.9 = (bf16[256,256]{1,0:T(8,128)(2,1)S(1)}, bf16[256,256]{1,0:T(8,128)(2,1)S(1)}, u32[]{:S(2)}, u32[]{:S(2)}) collective-permute-start(bf16[256,256]{1,0:T(8,128)(2,1)S(1)} %gate.7), channel_id=1, source_target_pairs={{0,8},{4,12},{8,0},{12,4},{16,24},{20,28},{24,16},{28,20},{1,9},{5... | collective-permute-start | bytes 393224 | tf_op jit(solution)/shard_map/ppermute | solution.py:498
  31.9 0.0 collective-permute-done.3.after.refs_0_
  31.9 0.0 copy-done.3
  32.0 1.0 %own_range.1 = (bf16[256,256]{1,0:T(8,128)(2,1)S(1)}, bf16[5,256,256]{2,1,0:T(8,128)(2,1)S(1)}) custom-call(bf16[256,256]{1,0:T(8,128)(2,1)S(1)} %collective-permute-done.3.after.refs_0_, bf16[26,128,256]{2,1,0:T(8,128)(2,1)S(1)} %get-tuple-element.26.samples, bf16[10,256,256]{2,1,0:T(8,128)(2,1)S(1)} %range_tiles.1.after, bf16[64,2048]{1,0:T(8,128)(2,1)S(1)} %copy-done, ...), custom_call_target="tpu_custom_call" | custom-call | tf_op jit(solution)/shard_map/own_range/pallas_call | solution.py:281
  32.9 0.0 collective-permute-done.6.refs_1_
  32.9 0.0 collective-permute-done.7.refs_2_
  33.0 0.4 %collective-permute-done.8.rest_5_ = bf16[256,256]{1,0:T(8,128)(2,1)S(1)} collective-permute-done((bf16[256,256]{1,0:T(8,128)(2,1)S(1)}, bf16[256,256]{1,0:T(8,128)(2,1)S(1)}, u32[]{:S(2)}, u32[]{:S(2)}) %collective-permute-start.8) | collective-permute-done | bytes 131104 | tf_op jit(solution)/shard_map/ppermute | solution.py:498
  33.4 1.4 %azimuth_most.1.most = f32[2,1,256,1024]{3,2,1,0:T(8,128)S(1)} custom-call(bf16[5,256,256]{2,1,0:T(8,128)(2,1)S(1)} %get-tuple-element.28.az_tiles, bf16[256,256]{1,0:T(8,128)(2,1)S(1)} %collective-permute-done.4.rest_0_.refs_1_, bf16[256,256]{1,0:T(8,128)(2,1)S(1)} %collective-permute-done.5.refs_1_.rest_1_, ...), custom_call_target="tpu_custom_call" | custom-call | tf_op jit(solution)/shard_map/azimuth_most/pallas_call | solution.py:419
  34.8 0.3 collective-permute-done.9.part
  35.1 1.5 %azimuth_last.1 = f32[2,1,256,1024]{3,2,1,0:T(8,128)} custom-call(bf16[5,256,256]{2,1,0:T(8,128)(2,1)S(1)} %get-tuple-element.28.az_tiles, f32[2,1,256,1024]{3,2,1,0:T(8,128)S(1)} %azimuth_most.1.most, bf16[256,256]{1,0:T(8,128)(2,1)S(1)} %collective-permute-done.9.part), custom_call_target="tpu_custom_call" | custom-call | tf_op jit(solution)/shard_map/azimuth_last/pallas_call | solution.py:460
  (4 shorter events, 0.0 us)
Async XLA Ops:
  0.0 1.4 %copy-start.1 = (bf16[2,128,2048]{2,1,0:T(8,128)(2,1)S(1)}, bf16[2,128,2048]{2,1,0:T(8,128)(2,1)}, u32[]{:S(2)}) copy-start(bf16[2,128,2048]{2,1,0:T(8,128)(2,1)} %echoes.3) | copy-start | bytes 3145732
  0.0 0.8 %copy-start.4 = (bf16[2,1024]{1,0:T(2,128)(2,1)S(1)}, bf16[2,1024]{1,0:T(2,128)(2,1)}, u32[]{:S(2)}) copy-start(bf16[2,1024]{1,0:T(2,128)(2,1)} %range_ref.1) | copy-start | bytes 12292
  1.5 11.5 %copy-start = (bf16[64,2048]{1,0:T(8,128)(2,1)S(1)}, bf16[64,2048]{1,0:T(8,128)(2,1)}, u32[]{:S(2)}) copy-start(bf16[64,2048]{1,0:T(8,128)(2,1)} %weights.9) | copy-start | bytes 786436
  1.5 11.5 %copy-start.2 = (s32[2048]{0:T(1024)S(1)}, s32[2048]{0:T(1024)}, u32[]{:S(2)}) copy-start(s32[2048]{0:T(1024)} %param.8) | copy-start | bytes 24580
  1.5 11.5 %collective-permute-start = (bf16[9,128,256]{2,1,0:T(8,128)(2,1)S(1)}, bf16[9,128,256]{2,1,0:T(8,128)(2,1)S(1)}, u32[]{:S(2)}, u32[]{:S(2)}) collective-permute-start(bf16[9,128,256]{2,1,0:T(8,128)(2,1)S(1)} %get-tuple-element.22), channel_id=1, source_target_pairs={{0,1},{2,3},{1,0},{3,2},{4,5},{6,7},{5,4},{7,6},{8,9},{10,11},{9,8... | collective-permute-start | bytes 1769480 | tf_op jit(solution)/shard_map/ppermute | solution.py:482
  1.7 11.3 %collective-permute-start.1 = (bf16[17,128,128]{2,1,0:T(8,128)(2,1)S(1)}, bf16[17,128,128]{2,1,0:T(8,128)(2,1)S(1)}, u32[]{:S(2)}, u32[]{:S(2)}) collective-permute-start(bf16[17,128,128]{2,1,0:T(8,128)(2,1)S(1)} %get-tuple-element.23), channel_id=1, source_target_pairs={{2,1},{6,5},{10,9},{14,13},{18,17},{22,21},{26,25},{30,29}} | collective-permute-start | bytes 1671176 | tf_op jit(solution)/shard_map/ppermute | solution.py:483
  2.9 5.8 %collective-permute-start.2 = (bf16[1,128,256]{2,1,0:T(8,128)(2,1)S(1)}, bf16[1,128,256]{2,1,0:T(8,128)(2,1)S(1)}, u32[]{:S(2)}, u32[]{:S(2)}) collective-permute-start(bf16[1,128,256]{2,1,0:T(8,128)(2,1)S(1)} %get-tuple-element.24), channel_id=1, source_target_pairs={{1,2},{5,6},{9,10},{13,14},{17,18},{21,22},{25,26},{29,30}} | collective-permute-start | bytes 196616 | tf_op jit(solution)/shard_map/ppermute | solution.py:484
  14.7 13.5 %collective-permute-start.5 = (bf16[256,256]{1,0:T(8,128)(2,1)S(1)}, bf16[256,256]{1,0:T(8,128)(2,1)S(1)}, u32[]{:S(2)}, u32[]{:S(2)}) collective-permute-start(bf16[256,256]{1,0:T(8,128)(2,1)S(1)} %get-tuple-element.29), channel_id=1, source_target_pairs={{0,20},{4,16},{8,28},{12,24},{16,4},{20,0},{24,12},{28,8},{1,21},{... | collective-permute-start | bytes 393224 | tf_op jit(solution)/shard_map/ppermute | solution.py:498
  19.0 12.3 %collective-permute-start.4 = (bf16[256,256]{1,0:T(8,128)(2,1)S(1)}, bf16[256,256]{1,0:T(8,128)(2,1)S(1)}, u32[]{:S(2)}, u32[]{:S(2)}) collective-permute-start(bf16[256,256]{1,0:T(8,128)(2,1)S(1)} %get-tuple-element.25.after), channel_id=1, source_target_pairs={{0,16},{4,20},{8,24},{12,28},{16,0},{20,4},{24,8},{28,12},{1,17},{... | collective-permute-start | bytes 393224 | tf_op jit(solution)/shard_map/ppermute | solution.py:498
  20.9 11.0 %collective-permute-start.3 = (bf16[256,256]{1,0:T(8,128)(2,1)S(1)}, bf16[256,256]{1,0:T(8,128)(2,1)S(1)}, u32[]{:S(2)}, u32[]{:S(2)}) collective-permute-start(bf16[256,256]{1,0:T(8,128)(2,1)S(1)} %get-tuple-element.27.after), channel_id=1, source_target_pairs={{0,24},{4,28},{8,16},{12,20},{16,8},{20,12},{24,0},{28,4},{1,25},{... | collective-permute-start | bytes 393224 | tf_op jit(solution)/shard_map/ppermute | solution.py:498
  24.3 8.6 %collective-permute-start.6 = (bf16[256,256]{1,0:T(8,128)(2,1)S(1)}, bf16[256,256]{1,0:T(8,128)(2,1)S(1)}, u32[]{:S(2)}, u32[]{:S(2)}) collective-permute-start(bf16[256,256]{1,0:T(8,128)(2,1)S(1)} %get-tuple-element.30), channel_id=1, source_target_pairs={{0,28},{4,24},{8,20},{12,16},{16,12},{20,8},{24,4},{28,0},{1,29},{... | collective-permute-start | bytes 393224 | tf_op jit(solution)/shard_map/ppermute | solution.py:498
  25.3 6.7 %copy-start.3 = (bf16[2,512]{1,0:T(2,128)(2,1)S(1)}, bf16[2,512]{1,0:T(2,128)(2,1)}, u32[]{:S(2)}) copy-start(bf16[2,512]{1,0:T(2,128)(2,1)} %az_taps.1) | copy-start | bytes 6148
  25.3 7.7 %collective-permute-start.7 = (bf16[256,256]{1,0:T(8,128)(2,1)S(1)}, bf16[256,256]{1,0:T(8,128)(2,1)S(1)}, u32[]{:S(2)}, u32[]{:S(2)}) collective-permute-start(bf16[256,256]{1,0:T(8,128)(2,1)S(1)} %next_range.4.after), channel_id=1, source_target_pairs={{0,4},{4,0},{8,12},{12,8},{16,20},{20,16},{24,28},{28,24},{1,5},{5... | collective-permute-start | bytes 393224 | tf_op jit(solution)/shard_map/ppermute | solution.py:498
  28.2 5.2 %collective-permute-start.8 = (bf16[256,256]{1,0:T(8,128)(2,1)S(1)}, bf16[256,256]{1,0:T(8,128)(2,1)S(1)}, u32[]{:S(2)}, u32[]{:S(2)}) collective-permute-start(bf16[256,256]{1,0:T(8,128)(2,1)S(1)} %gate.6), channel_id=1, source_target_pairs={{0,12},{4,8},{8,4},{12,0},{16,28},{20,24},{24,20},{28,16},{1,13},{... | collective-permute-start | bytes 393224 | tf_op jit(solution)/shard_map/ppermute | solution.py:498
  31.3 3.8 %collective-permute-start.9 = (bf16[256,256]{1,0:T(8,128)(2,1)S(1)}, bf16[256,256]{1,0:T(8,128)(2,1)S(1)}, u32[]{:S(2)}, u32[]{:S(2)}) collective-permute-start(bf16[256,256]{1,0:T(8,128)(2,1)S(1)} %gate.7), channel_id=1, source_target_pairs={{0,8},{4,12},{8,0},{12,4},{16,24},{20,28},{24,16},{28,20},{1,9},{5... | collective-permute-start | bytes 393224 | tf_op jit(solution)/shard_map/ppermute | solution.py:498

commit v11 on v10

--- a/solution.py
+++ b/solution.py
@@ -498,21 +498,21 @@
         return lax.ppermute(piece, "pulse", [(i, i ^ k) for i in range(peers)])
 
     samples, made = first_range(
-        [4, 5], samples, near, down, up, range_tiles, weights, offsets
+        [5, 4], samples, near, down, up, range_tiles, weights, offsets
     )
-    ready = dict(zip([4, 5], made))
+    ready = dict(zip([5, 4], made))
     for some in [[6, 7], [1], [2, 3]]:
         made = next_range([some], made[0], samples, range_tiles, weights, offsets)
         ready.update(zip(some, made))
     parts = {}
+    parts[5] = send(ready[5], 5)
     parts[4] = send(ready[4], 4)
-    parts[5] = send(ready[5], 5)
     parts[6] = send(ready[6], 6)
     parts[7] = send(ready[7], 7)
     parts[1] = send(ready[1], 1)
-    parts[3] = send(gate([ready[3]], (parts[5],))[0], 3)
-    parts[2] = send(gate([ready[2]], (parts[4],))[0], 2)
-    after = parts[6]
+    parts[3] = send(gate([ready[3]], (parts[4],))[0], 3)
+    parts[2] = send(gate([ready[2]], (parts[5],))[0], 2)
+    after = parts[4]
     parts[0], az_tiles = own_range(after, samples, range_tiles, weights, offsets, azimuth_ref)
     parts.update(zip([6, 7], gate((parts[6], parts[7],), (), 1000000000)))
     parts.update(zip([6, 7, 1], gate((parts[6], parts[7], parts[1],), (), 200000000)))

time: 36.8 us -> 36.9 us (level)
  starting transfers between devices: 16 us -> 15.5 us
  waiting for transfers between devices: 9.07 us -> 9.57 us
    ppermute x7, waiting for transfers between devices: 3.73 us -> 4.52 us  [send(): return lax.ppermute(piece, 'pulse', [(i, i ^ k) for i in range(peers)])]
    ppermute x7, starting transfers between devices: 10.1 us -> 9.63 us  [send(): return lax.ppermute(piece, 'pulse', [(i, i ^ k) for i in range(peers)])]
where the time goes in v11:
time: 36.9 us; the launch traced here: 36.7 us
  starting transfers between devices  15.5 us (42%)
  Pallas kernels  10.6 us (29%)
  waiting for transfers between devices  9.57 us (26%)
  local copies, waits for them, and re-layouts  0.8 us (2%)
    ppermute x7, starting transfers between devices, send(): return lax.ppermute(piece, 'pulse', [(i, i ^ k) for i in range(peers)])  9.63 us
    ppermute x7, waiting for transfers between devices, send(): return lax.ppermute(piece, 'pulse', [(i, i ^ k) for i in range(peers)])  4.52 us
    ppermute x1, starting transfers between devices, per_device(): up = lax.ppermute(up, 'rng', chips)  4.51 us
    pallas_call x3, Pallas kernels, next_range(): call(functools.partial(next_range_body, steps), 'next_range', (bf16(GROUP...  4.09 us
    ppermute x1, waiting for transfers between devices, per_device(): down = lax.ppermute(down, 'rng', [(j, i) for i, j in chips])  3.93 us
    pallas_call x1, Pallas kernels, first_range(): pl.pallas_call(functools.partial(first_range_body, steps), out_shape=(jax...  1.78 us
    pallas_call x1, Pallas kernels, azimuth_last(): call(functools.partial(azimuth_last_body, step), 'azimuth_last', jax.Shap...  1.51 us
    pallas_call x1, Pallas kernels, azimuth_most(): call(functools.partial(azimuth_most_body, steps, absent), 'azimuth_most',...  1.36 us
  transfers between devices with their start and end apart: 10, of which 5 were waited for; matrix products, arithmetic and copies ran while one was open for 0% of the time, Pallas kernels for 18%

profile of v11, /device:TPU:1, one launch (start us, length us, event | category | flops | bytes accessed | tf_op | source)
XLA Modules:
  0.0 36.7 jit_solution(8744190529879389416)
XLA Ops:
  0.0 0.0 copy-start.1
  0.0 0.0 copy-start.4
  0.0 0.8 %copy-done.4 = bf16[2,1024]{1,0:T(2,128)(2,1)S(1)} copy-done((bf16[2,1024]{1,0:T(2,128)(2,1)S(1)}, bf16[2,1024]{1,0:T(2,128)(2,1)}, u32[]{:S(2)}) %copy-start.4) | copy-done | bytes 4120
  0.8 0.6 %range_tiles.1.after = bf16[10,256,256]{2,1,0:T(8,128)(2,1)S(1)} custom-call(bf16[2,1024]{1,0:T(2,128)(2,1)S(1)} %copy-done.4), custom_call_target="tpu_custom_call" | custom-call | flops 2000000000 | tf_op jit(solution)/shard_map/range_tiles/pallas_call | solution.py:136
  1.4 0.0 copy-done.1
  1.4 0.1 pack.1
  1.5 0.0 copy-start
  1.5 0.0 copy-start.2
  1.5 0.1 collective-permute-start
  1.7 1.3 %collective-permute-start.1 = (bf16[17,128,128]{2,1,0:T(8,128)(2,1)S(1)}, bf16[17,128,128]{2,1,0:T(8,128)(2,1)S(1)}, u32[]{:S(2)}, u32[]{:S(2)}) collective-permute-start(bf16[17,128,128]{2,1,0:T(8,128)(2,1)S(1)} %get-tuple-element.23), channel_id=1, source_target_pairs={{2,1},{6,5},{10,9},{14,13},{18,17},{22,21},{26,25},{30,29}} | collective-permute-start | bytes 1671176 | tf_op jit(solution)/shard_map/ppermute | solution.py:483
  2.9 4.5 %collective-permute-start.2 = (bf16[1,128,256]{2,1,0:T(8,128)(2,1)S(1)}, bf16[1,128,256]{2,1,0:T(8,128)(2,1)S(1)}, u32[]{:S(2)}, u32[]{:S(2)}) collective-permute-start(bf16[1,128,256]{2,1,0:T(8,128)(2,1)S(1)} %get-tuple-element.24), channel_id=1, source_target_pairs={{1,2},{5,6},{9,10},{13,14},{17,18},{21,22},{25,26},{29,30}} | collective-permute-start | bytes 196616 | tf_op jit(solution)/shard_map/ppermute | solution.py:484
  7.5 0.2 lay_out.1.start
  7.6 1.1 %collective-permute-done.2.up = bf16[1,128,256]{2,1,0:T(8,128)(2,1)S(1)} collective-permute-done((bf16[1,128,256]{2,1,0:T(8,128)(2,1)S(1)}, bf16[1,128,256]{2,1,0:T(8,128)(2,1)S(1)}, u32[]{:S(2)}, u32[]{:S(2)}) %collective-permute-start.2) | collective-permute-done | bytes 65568 | tf_op jit(solution)/shard_map/ppermute | solution.py:484
  8.8 3.9 %collective-permute-done.1.down = bf16[17,128,128]{2,1,0:T(8,128)(2,1)S(1)} collective-permute-done((bf16[17,128,128]{2,1,0:T(8,128)(2,1)S(1)}, bf16[17,128,128]{2,1,0:T(8,128)(2,1)S(1)}, u32[]{:S(2)}, u32[]{:S(2)}) %collective-permute-start.1) | collective-permute-done | bytes 557088 | tf_op jit(solution)/shard_map/ppermute | solution.py:483
  12.7 0.0 collective-permute-done.near
  12.7 0.0 copy-done
  12.7 0.0 copy-done.2
  12.7 1.8 %first_range.1 = (bf16[26,128,256]{2,1,0:T(8,128)(2,1)S(1)}, bf16[256,256]{1,0:T(8,128)(2,1)S(1)}, bf16[256,256]{1,0:T(8,128)(2,1)S(1)}) custom-call(bf16[26,128,256]{2,1,0:T(8,128)(2,1)S(1)} %lay_out.1.start, bf16[9,128,256]{2,1,0:T(8,128)(2,1)S(1)} %collective-permute-done.near, ...), custom_call_target="tpu_custom_call", output_to_operand_aliasing={{0}: (0, {})} | custom-call | tf_op jit(solution)/shard_map/first_range/pallas_call | solution.py:228
  14.5 3.9 %collective-permute-start.3 = (bf16[256,256]{1,0:T(8,128)(2,1)S(1)}, bf16[256,256]{1,0:T(8,128)(2,1)S(1)}, u32[]{:S(2)}, u32[]{:S(2)}) collective-permute-start(bf16[256,256]{1,0:T(8,128)(2,1)S(1)} %get-tuple-element.25), channel_id=1, source_target_pairs={{0,16},{4,20},{8,24},{12,28},{16,0},{20,4},{24,8},{28,12},{1,17},{... | collective-permute-start | bytes 393224 | tf_op jit(solution)/shard_map/ppermute | solution.py:498
  18.4 0.7 %collective-permute-start.4 = (bf16[256,256]{1,0:T(8,128)(2,1)S(1)}, bf16[256,256]{1,0:T(8,128)(2,1)S(1)}, u32[]{:S(2)}, u32[]{:S(2)}) collective-permute-start(bf16[256,256]{1,0:T(8,128)(2,1)S(1)} %get-tuple-element.28.after), channel_id=1, source_target_pairs={{0,20},{4,16},{8,28},{12,24},{16,4},{20,0},{24,12},{28,8},{1,21},{... | collective-permute-start | bytes 393224 | tf_op jit(solution)/shard_map/ppermute | solution.py:498
  19.1 1.6 %next_range.3 = (bf16[256,256]{1,0:T(8,128)(2,1)S(1)}, bf16[256,256]{1,0:T(8,128)(2,1)S(1)}) custom-call(bf16[256,256]{1,0:T(8,128)(2,1)S(1)} %get-tuple-element.28.after, bf16[26,128,256]{2,1,0:T(8,128)(2,1)S(1)} %get-tuple-element.26.samples, bf16[10,256,256]{2,1,0:T(8,128)(2,1)S(1)} %range_tiles.1.after, bf16[64,2048]{1,0:T(8,128)(2,1)S(1)} %copy-done, ...), custom_call_target="tpu_custom_call" | custom-call | tf_op jit(solution)/shard_map/next_range/pallas_call | solution.py:264
  20.7 3.6 %collective-permute-start.6 = (bf16[256,256]{1,0:T(8,128)(2,1)S(1)}, bf16[256,256]{1,0:T(8,128)(2,1)S(1)}, u32[]{:S(2)}, u32[]{:S(2)}) collective-permute-start(bf16[256,256]{1,0:T(8,128)(2,1)S(1)} %get-tuple-element.30), channel_id=1, source_target_pairs={{0,28},{4,24},{8,20},{12,16},{16,12},{20,8},{24,4},{28,0},{1,29},{... | collective-permute-start | bytes 393224 | tf_op jit(solution)/shard_map/ppermute | solution.py:498
  24.3 0.1 collective-permute-start.5
  24.5 0.9 %next_range.4.after = bf16[256,256]{1,0:T(8,128)(2,1)S(1)} custom-call(bf16[256,256]{1,0:T(8,128)(2,1)S(1)} %get-tuple-element.29.after, bf16[26,128,256]{2,1,0:T(8,128)(2,1)S(1)} %get-tuple-element.26.samples, bf16[10,256,256]{2,1,0:T(8,128)(2,1)S(1)} %range_tiles.1.after, bf16[64,2048]{1,0:T(8,128)(2,1)S(1)} %copy-done, s32[16,128]{1,0:T(8,128)S(1)} %bitcast.3), custom_call_target="tpu_custom_call" | custom-call | tf_op jit(solution)/shard_map/next_range/pallas_call | solution.py:264
  25.4 0.0 copy-start.3
  25.4 1.2 %collective-permute-start.7 = (bf16[256,256]{1,0:T(8,128)(2,1)S(1)}, bf16[256,256]{1,0:T(8,128)(2,1)S(1)}, u32[]{:S(2)}, u32[]{:S(2)}) collective-permute-start(bf16[256,256]{1,0:T(8,128)(2,1)S(1)} %next_range.4.after), channel_id=1, source_target_pairs={{0,4},{4,0},{8,12},{12,8},{16,20},{20,16},{24,28},{28,24},{1,5},{5... | collective-permute-start | bytes 393224 | tf_op jit(solution)/shard_map/ppermute | solution.py:498
  26.6 1.6 %next_range.5 = (bf16[256,256]{1,0:T(8,128)(2,1)S(1)}, bf16[256,256]{1,0:T(8,128)(2,1)S(1)}) custom-call(bf16[256,256]{1,0:T(8,128)(2,1)S(1)} %next_range.4.after, bf16[26,128,256]{2,1,0:T(8,128)(2,1)S(1)} %get-tuple-element.26.samples, bf16[10,256,256]{2,1,0:T(8,128)(2,1)S(1)} %range_tiles.1.after, bf16[64,2048]{1,0:T(8,128)(2,1)S(1)} %copy-done, ...), custom_call_target="tpu_custom_call" | custom-call | tf_op jit(solution)/shard_map/next_range/pallas_call | solution.py:264
  28.2 0.0 collective-permute-done.3.after.refs_1_.rest_1_
  28.2 0.1 collective-permute-start.8
  28.3 3.1 %collective-permute-done.4.rest_0_.refs_1_ = bf16[256,256]{1,0:T(8,128)(2,1)S(1)} collective-permute-done((bf16[256,256]{1,0:T(8,128)(2,1)S(1)}, bf16[256,256]{1,0:T(8,128)(2,1)S(1)}, u32[]{:S(2)}, u32[]{:S(2)}) %collective-permute-start.4) | collective-permute-done | bytes 131104 | tf_op jit(solution)/shard_map/ppermute | solution.py:498
  31.4 0.0 collective-permute-start.9
  31.4 0.0 copy-done.3
  31.4 1.0 %own_range.1 = (bf16[256,256]{1,0:T(8,128)(2,1)S(1)}, bf16[5,256,256]{2,1,0:T(8,128)(2,1)S(1)}) custom-call(bf16[256,256]{1,0:T(8,128)(2,1)S(1)} %collective-permute-done.3.after.refs_1_.rest_1_, bf16[26,128,256]{2,1,0:T(8,128)(2,1)S(1)} %get-tuple-element.26.samples, bf16[10,256,256]{2,1,0:T(8,128)(2,1)S(1)} %range_tiles.1.after, ...), custom_call_target="tpu_custom_call" | custom-call | tf_op jit(solution)/shard_map/own_range/pallas_call | solution.py:281
  32.3 0.0 collective-permute-done.6.refs_1_
  32.4 0.0 collective-permute-done.5.refs_0_
  32.4 0.0 collective-permute-done.7.refs_2_
  32.4 1.1 %collective-permute-done.8.rest_5_ = bf16[256,256]{1,0:T(8,128)(2,1)S(1)} collective-permute-done((bf16[256,256]{1,0:T(8,128)(2,1)S(1)}, bf16[256,256]{1,0:T(8,128)(2,1)S(1)}, u32[]{:S(2)}, u32[]{:S(2)}) %collective-permute-start.8) | collective-permute-done | bytes 131104 | tf_op jit(solution)/shard_map/ppermute | solution.py:498
  33.5 1.4 %azimuth_most.1.most = f32[2,1,256,1024]{3,2,1,0:T(8,128)S(1)} custom-call(bf16[5,256,256]{2,1,0:T(8,128)(2,1)S(1)} %get-tuple-element.27.az_tiles, bf16[256,256]{1,0:T(8,128)(2,1)S(1)} %collective-permute-done.4.rest_0_.refs_1_, bf16[256,256]{1,0:T(8,128)(2,1)S(1)} %collective-permute-done.3.after.refs_1_.rest_1_, ...), custom_call_target="tpu_custom_call" | custom-call | tf_op jit(solution)/shard_map/azimuth_most/pallas_call | solution.py:419
  34.9 0.3 collective-permute-done.9.part
  35.2 1.5 %azimuth_last.1 = f32[2,1,256,1024]{3,2,1,0:T(8,128)} custom-call(bf16[5,256,256]{2,1,0:T(8,128)(2,1)S(1)} %get-tuple-element.27.az_tiles, f32[2,1,256,1024]{3,2,1,0:T(8,128)S(1)} %azimuth_most.1.most, bf16[256,256]{1,0:T(8,128)(2,1)S(1)} %collective-permute-done.9.part), custom_call_target="tpu_custom_call" | custom-call | tf_op jit(solution)/shard_map/azimuth_last/pallas_call | solution.py:460
  (4 shorter events, 0.0 us)
Async XLA Ops:
  0.0 1.4 %copy-start.1 = (bf16[2,128,2048]{2,1,0:T(8,128)(2,1)S(1)}, bf16[2,128,2048]{2,1,0:T(8,128)(2,1)}, u32[]{:S(2)}) copy-start(bf16[2,128,2048]{2,1,0:T(8,128)(2,1)} %echoes.3) | copy-start | bytes 3145732
  0.0 0.8 %copy-start.4 = (bf16[2,1024]{1,0:T(2,128)(2,1)S(1)}, bf16[2,1024]{1,0:T(2,128)(2,1)}, u32[]{:S(2)}) copy-start(bf16[2,1024]{1,0:T(2,128)(2,1)} %range_ref.1) | copy-start | bytes 12292
  1.5 11.2 %copy-start = (bf16[64,2048]{1,0:T(8,128)(2,1)S(1)}, bf16[64,2048]{1,0:T(8,128)(2,1)}, u32[]{:S(2)}) copy-start(bf16[64,2048]{1,0:T(8,128)(2,1)} %weights.9) | copy-start | bytes 786436
  1.5 11.2 %copy-start.2 = (s32[2048]{0:T(1024)S(1)}, s32[2048]{0:T(1024)}, u32[]{:S(2)}) copy-start(s32[2048]{0:T(1024)} %param.8) | copy-start | bytes 24580
  1.5 11.2 %collective-permute-start = (bf16[9,128,256]{2,1,0:T(8,128)(2,1)S(1)}, bf16[9,128,256]{2,1,0:T(8,128)(2,1)S(1)}, u32[]{:S(2)}, u32[]{:S(2)}) collective-permute-start(bf16[9,128,256]{2,1,0:T(8,128)(2,1)S(1)} %get-tuple-element.22), channel_id=1, source_target_pairs={{0,1},{2,3},{1,0},{3,2},{4,5},{6,7},{5,4},{7,6},{8,9},{10,11},{9,8... | collective-permute-start | bytes 1769480 | tf_op jit(solution)/shard_map/ppermute | solution.py:482
  1.7 11.0 %collective-permute-start.1 = (bf16[17,128,128]{2,1,0:T(8,128)(2,1)S(1)}, bf16[17,128,128]{2,1,0:T(8,128)(2,1)S(1)}, u32[]{:S(2)}, u32[]{:S(2)}) collective-permute-start(bf16[17,128,128]{2,1,0:T(8,128)(2,1)S(1)} %get-tuple-element.23), channel_id=1, source_target_pairs={{2,1},{6,5},{10,9},{14,13},{18,17},{22,21},{26,25},{30,29}} | collective-permute-start | bytes 1671176 | tf_op jit(solution)/shard_map/ppermute | solution.py:483
  2.9 5.8 %collective-permute-start.2 = (bf16[1,128,256]{2,1,0:T(8,128)(2,1)S(1)}, bf16[1,128,256]{2,1,0:T(8,128)(2,1)S(1)}, u32[]{:S(2)}, u32[]{:S(2)}) collective-permute-start(bf16[1,128,256]{2,1,0:T(8,128)(2,1)S(1)} %get-tuple-element.24), channel_id=1, source_target_pairs={{1,2},{5,6},{9,10},{13,14},{17,18},{21,22},{25,26},{29,30}} | collective-permute-start | bytes 196616 | tf_op jit(solution)/shard_map/ppermute | solution.py:484
  14.5 13.7 %collective-permute-start.3 = (bf16[256,256]{1,0:T(8,128)(2,1)S(1)}, bf16[256,256]{1,0:T(8,128)(2,1)S(1)}, u32[]{:S(2)}, u32[]{:S(2)}) collective-permute-start(bf16[256,256]{1,0:T(8,128)(2,1)S(1)} %get-tuple-element.25), channel_id=1, source_target_pairs={{0,16},{4,20},{8,24},{12,28},{16,0},{20,4},{24,8},{28,12},{1,17},{... | collective-permute-start | bytes 393224 | tf_op jit(solution)/shard_map/ppermute | solution.py:498
  18.4 13.0 %collective-permute-start.4 = (bf16[256,256]{1,0:T(8,128)(2,1)S(1)}, bf16[256,256]{1,0:T(8,128)(2,1)S(1)}, u32[]{:S(2)}, u32[]{:S(2)}) collective-permute-start(bf16[256,256]{1,0:T(8,128)(2,1)S(1)} %get-tuple-element.28.after), channel_id=1, source_target_pairs={{0,20},{4,16},{8,28},{12,24},{16,4},{20,0},{24,12},{28,8},{1,21},{... | collective-permute-start | bytes 393224 | tf_op jit(solution)/shard_map/ppermute | solution.py:498
  20.7 11.6 %collective-permute-start.6 = (bf16[256,256]{1,0:T(8,128)(2,1)S(1)}, bf16[256,256]{1,0:T(8,128)(2,1)S(1)}, u32[]{:S(2)}, u32[]{:S(2)}) collective-permute-start(bf16[256,256]{1,0:T(8,128)(2,1)S(1)} %get-tuple-element.30), channel_id=1, source_target_pairs={{0,28},{4,24},{8,20},{12,16},{16,12},{20,8},{24,4},{28,0},{1,29},{... | collective-permute-start | bytes 393224 | tf_op jit(solution)/shard_map/ppermute | solution.py:498
  24.3 8.0 %collective-permute-start.5 = (bf16[256,256]{1,0:T(8,128)(2,1)S(1)}, bf16[256,256]{1,0:T(8,128)(2,1)S(1)}, u32[]{:S(2)}, u32[]{:S(2)}) collective-permute-start(bf16[256,256]{1,0:T(8,128)(2,1)S(1)} %get-tuple-element.29.after), channel_id=1, source_target_pairs={{0,24},{4,28},{8,16},{12,20},{16,8},{20,12},{24,0},{28,4},{1,25},{... | collective-permute-start | bytes 393224 | tf_op jit(solution)/shard_map/ppermute | solution.py:498
  25.4 6.0 %copy-start.3 = (bf16[2,512]{1,0:T(2,128)(2,1)S(1)}, bf16[2,512]{1,0:T(2,128)(2,1)}, u32[]{:S(2)}) copy-start(bf16[2,512]{1,0:T(2,128)(2,1)} %az_taps.1) | copy-start | bytes 6148
  25.4 7.0 %collective-permute-start.7 = (bf16[256,256]{1,0:T(8,128)(2,1)S(1)}, bf16[256,256]{1,0:T(8,128)(2,1)S(1)}, u32[]{:S(2)}, u32[]{:S(2)}) collective-permute-start(bf16[256,256]{1,0:T(8,128)(2,1)S(1)} %next_range.4.after), channel_id=1, source_target_pairs={{0,4},{4,0},{8,12},{12,8},{16,20},{20,16},{24,28},{28,24},{1,5},{5... | collective-permute-start | bytes 393224 | tf_op jit(solution)/shard_map/ppermute | solution.py:498
  28.2 5.3 %collective-permute-start.8 = (bf16[256,256]{1,0:T(8,128)(2,1)S(1)}, bf16[256,256]{1,0:T(8,128)(2,1)S(1)}, u32[]{:S(2)}, u32[]{:S(2)}) collective-permute-start(bf16[256,256]{1,0:T(8,128)(2,1)S(1)} %gate.6), channel_id=1, source_target_pairs={{0,12},{4,8},{8,4},{12,0},{16,28},{20,24},{24,20},{28,16},{1,13},{... | collective-permute-start | bytes 393224 | tf_op jit(solution)/shard_map/ppermute | solution.py:498
  31.4 3.8 %collective-permute-start.9 = (bf16[256,256]{1,0:T(8,128)(2,1)S(1)}, bf16[256,256]{1,0:T(8,128)(2,1)S(1)}, u32[]{:S(2)}, u32[]{:S(2)}) collective-permute-start(bf16[256,256]{1,0:T(8,128)(2,1)S(1)} %gate.7), channel_id=1, source_target_pairs={{0,8},{4,12},{8,0},{12,4},{16,24},{20,28},{24,16},{28,20},{1,9},{5... | collective-permute-start | bytes 393224 | tf_op jit(solution)/shard_map/ppermute | solution.py:498
